TPU v7x, 32 devices: a whole 2x2x4 slice. The times are simulated.
32 devices in a mesh: seq: 8 (over z, y), tp: 4 (over x, core).
Axes of the slice: x: 2, y: 2, z: 4, core: 2. Of those that a mesh axis runs over, the one named last changes fastest.
Arguments:
- features: bfloat16 [1024, 3, 4096], P('seq', None, 'tp'), may hold values from -6 to 6
- short_taps: bfloat16 [3, 3, 4096], P(None, None, 'tp'), may hold values from -3.5 to 3.5
- rates: float32 [4096, 16], P('tp'), may hold values from 9.765625e-05 to 0.2
- residues: float32 [4096, 16], P('tp'), may hold values from -0.25 to 0.25
- skip: float32 [4096], P('tp'), may hold values from -6 to 6
- out_weight: bfloat16 [4096, 4096], P('seq', 'tp'), may hold values from -0.09375 to 0.09375
Outputs:
- layer_out: bfloat16 [1024, 4096], P('seq', 'tp')
All inputs are finite; a program needn't handle non-finite values.
Results may differ from a plain program's by a relative error of at most 0.025.
Values may be sent and summed in bfloat16 or wider, within the bound.
No kernel may reach another device: no remote copies, remote signals or barrier semaphores. Data moves between devices by JAX's collectives and lax.ppermute only.
A program may use at most 128 MiB of HBM per device.

v0:
```python
import jax
import jax.numpy as jnp
from jax import lax
from jax.sharding import PartitionSpec as P

HIGH = lax.Precision.HIGHEST


def from_behind(x, axis, by):
    length = lax.axis_size(axis)
    pairs = [(i, i + by) for i in range(length) if 0 <= i + by < length]
    return lax.ppermute(x, axis, pairs)


def prefix(x, axis, join, neutral):
    place = lax.axis_index(axis)
    gathered = jax.tree.map(
        lambda a, kind: lax.all_gather(a.astype(kind), axis), x, (jnp.bfloat16, jnp.bfloat16)
    )
    state = jax.tree.map(lambda a, e: jnp.zeros_like(a) + jnp.asarray(e, a.dtype), x, neutral)

    def one(lap, state):
        return join(
            state,
            jax.tree.map(
                lambda a, own: lax.dynamic_index_in_dim(a, lap, 0, False).astype(own.dtype),
                gathered,
                x,
            ),
        )

    return lax.fori_loop(0, place, one, state)


def per_device(features, short_taps, rates, residues, skip, out_weight):
    tok_rows = features.shape[0]
    channels = features.shape[2]
    tap_count = short_taps.shape[1]
    last_rows = features[tok_rows - (tap_count - 1) :]
    before = from_behind(last_rows, "seq", 1)
    padded = jnp.concatenate([before, features], axis=0).astype(jnp.float32)
    tap_values = short_taps.astype(jnp.float32)
    mixed = tap_values[:, 0, :] * padded[tap_count - 1 :]
    for shift_rows in range(1, tap_count):
        lower = tap_count - 1 - shift_rows
        mixed = mixed + tap_values[:, shift_rows, :] * padded[lower : lower + tok_rows]
    signal = mixed[:, 1, :] * mixed[:, 2, :]
    piece_len = min(32, tok_rows)
    piece_count = tok_rows // piece_len
    rate_rows = rates.T
    residue_rows = residues.T
    offsets = jnp.arange(piece_len).astype(jnp.float32)
    short_filter = jnp.sum(
        residue_rows[None] * jnp.exp(-rate_rows[None] * offsets[:, None, None]), axis=1
    )
    positions = jnp.arange(piece_len)
    onehot = (
        positions[:, None, None] == positions[None, :, None] - positions[None, None, :]
    ).astype(jnp.float32)
    toeplitz = jnp.einsum("lc,lts->tsc", short_filter, onehot, precision=HIGH)
    blocks = signal.reshape(piece_count, piece_len, channels)
    near_part = jnp.einsum("tsc,msc->mtc", toeplitz, blocks, precision=HIGH)
    end_weight = jnp.exp(-rate_rows[None] * (piece_len - 1 - offsets)[:, None, None])
    block_ends = jnp.einsum("src,msc->mrc", end_weight, blocks, precision=HIGH)
    piece_index = jnp.arange(piece_count).astype(jnp.float32)
    piece_decay = jnp.exp(-rate_rows * piece_len)

    def enter_step(state, block_end):
        return (piece_decay * state + block_end, state)

    local_end, local_enter = lax.scan(enter_step, jnp.zeros_like(piece_decay), block_ends)

    def combine(earlier, following):
        return (
            earlier[0] + following[0],
            jnp.exp(-rate_rows * following[0]) * earlier[1] + following[1],
        )

    span_rows = jnp.full((1, 1), float(tok_rows), jnp.float32)
    identity = (jnp.zeros((1, 1), jnp.float32), jnp.zeros_like(local_end))
    _, entering = prefix((span_rows, local_end), "seq", combine, identity)
    incoming = (
        local_enter
        + jnp.exp(-rate_rows[None] * piece_len * piece_index[:, None, None]) * entering[None]
    )
    gain_weight = residue_rows[None] * jnp.exp(-rate_rows[None] * (offsets + 1.0)[:, None, None])
    far_part = jnp.einsum("trc,mrc->mtc", gain_weight, incoming, precision=HIGH)
    conv = (near_part + far_part).reshape(tok_rows, channels) + skip[None] * signal
    gated = (mixed[:, 0, :] * conv).astype(jnp.bfloat16)
    partial_value = lax.dot_general(
        gated,
        lax.all_gather(out_weight, "seq", axis=0, tiled=True),
        (((1,), (1,)), ((), ())),
        preferred_element_type=jnp.float32,
    )
    result = lax.psum_scatter(
        partial_value.astype(jnp.bfloat16), "tp", scatter_dimension=1, tiled=True
    )
    return result


def solution(mesh):
    in_specs = (
        P("seq", None, "tp"),
        P(None, None, "tp"),
        P("tp", None),
        P("tp", None),
        P("tp"),
        P("seq", "tp"),
    )
    out_specs = P("seq", "tp")
    return jax.shard_map(
        per_device, mesh=mesh, in_specs=in_specs, out_specs=out_specs, check_vma=False
    )
```

profile of v0, /device:TPU:1, one launch (start us, length us, event | category | flops | bytes accessed | tf_op | source)
XLA Modules:
  0.0 209.6 jit_solution(7870142993232809009)
XLA Ops:
  6.5 0.0 copy-start.9
  6.5 0.0 copy-start.5
  6.5 0.0 all-gather.3.cloned.1.call-start
  6.5 0.7 all-gather.3.cloned.1.call-update
  7.3 0.0 reduce-scatter.2.cloned.1.call-start
  7.3 0.8 slice.31
  8.1 4.0 %collective-permute-start = (bf16[2,3,1024]{2,0,1:T(2,128)(2,1)S(1)}, bf16[2,3,1024]{2,0,1:T(2,128)(2,1)S(1)}, u32[]{:S(2)}, u32[]{:S(2)}) collective-permute-start(bf16[2,3,1024]{2,0,1:T(2,128)(2,1)S(1)} %slice.31), channel_id=1, source_target_pairs={{0,4},{4,8},{8,12},{12,16},{16,20},{20,24},{24,28},{1,5},{5,9},{9,... | collective-permute-start | bytes 36872 | tf_op jit(solution)/shard_map/ppermute | solution.py:12
  12.1 0.8 negate_bitcast_fusion
  13.0 0.2 copy.22
  13.2 1.0 copy.21
  14.2 0.0 copy-start.3
  14.2 0.0 copy-done.9
  14.2 0.7 dynamic-slice
  14.9 0.8 dynamic-update-slice
  15.7 0.0 copy-done.7
  15.8 0.0 copy-done.5
  15.8 11.8 %multiply_reduce_fusion = f32[32,1024]{0,1:T(8,128)S(1)} fusion(f32[32]{0:T(128)S(1)} %iota_convert_fusion.1, f32[16,1024]{0,1:T(8,128)S(1)} %copy.22, f32[16,1024]{0,1:T(8,128)S(1)} %copy.21), kind=kLoop, calls=%fused_computation.11 | loop fusion | flops 1540096 | bytes 262272 | tf_op jit(solution)/shard_map/reduce_sum | solution.py:53
  27.6 3.8 %fusion.22 = f32[32,32,1024]{2,1,0:T(8,128)} fusion(f32[32,1024]{0,1:T(8,128)S(1)} %multiply_reduce_fusion, s32[32,32]{1,0:T(8,128)S(1)} %iota_subtract_fusion), kind=kOutput, calls=%fused_computation.32 | convolution fusion | flops 402685952 | bytes 4329472 | tf_op jit(solution)/shard_map/lc,lts->tsc/dot_general | solution.py:60
  31.4 0.0 copy-done.3
  31.4 17.0 %all-reduce = bf16[8]{0:T(256)(128)(2,1)S(1)} all-reduce(bf16[8]{0:T(256)(128)(2,1)S(1)} %dynamic-update-slice), channel_id=1, replica_groups=mesh['seq'=8,'tp'=4] {'seq'}, use_global_device_ids=true, to_apply=%add | all-reduce | flops 8 | bytes 32
  48.4 14.3 %copy.25 = f32[32,32,1024]{1,0,2:T(8,128)} copy(f32[32,32,1024]{2,1,0:T(8,128)} %fusion.22) | data formatting | bytes 8388608 | tf_op jit(solution)/shard_map/lc,lts->tsc/dot_general | solution.py:60
  62.8 0.0 collective-permute-done
  62.8 1.5 maximum_convert_fusion
  64.3 0.5 fusion.17
  64.8 0.0 copy-start
  64.8 0.1 slice_multiply_fusion.3
  64.8 1.1 copy-done
  65.9 0.8 copy.24
  66.8 14.8 %fusion.12 = f32[4,16,1024]{1,0,2:T(4,128)} fusion(f32[4,32,1024]{1,0,2:T(4,128)S(1)} %copy.24, f32[32]{0:T(128)S(1)} %broadcast_subtract_fusion, f32[16,1024]{0,1:T(8,128)S(1)} %copy.22), kind=kOutput, calls=%fused_computation.19 | convolution fusion | flops 25690112 | bytes 852096 | tf_op jit(solution)/shard_map/src,msc->mrc/dot_general | solution.py:64
  81.6 1.9 copy.27
  83.5 0.0 copy-done.6
  83.5 0.3 while.28
  83.8 26.4 %all-gather = bf16[128,1024]{1,0:T(8,128)(2,1)S(1)} all-gather(bf16[16,1024]{1,0:T(8,128)(2,1)S(1)} %convert_element_type.58), channel_id=2, replica_groups=mesh['seq'=8,'tp'=4] {'seq'}, dimensions={0}, use_global_device_ids=true | all-gather | bytes 294912 | tf_op jit(solution)/shard_map/all_gather | solution.py:18
  110.2 0.2 while.27
  110.4 0.1 multiply_add_fusion
  110.5 1.7 copy.28
  112.3 29.2 %fusion.27 = f32[1024,4,32]{2,1,0:T(4,128)S(1)} fusion(f32[4,32,1024]{1,0,2:T(4,128)S(1)} %copy.24, f32[32,32,1024]{1,0,2:T(8,128)} %copy.25), kind=kOutput, calls=%fused_computation.49 | convolution fusion | flops 50331648 | bytes 5242880 | tf_op jit(solution)/shard_map/tsc,msc->mtc/dot_general | solution.py:62
  141.4 0.0 copy-done.2
  141.4 0.0 copy-done.4
  141.4 12.0 %add_bitcast_fusion = f32[4,32,1024]{1,0,2:T(4,128)} fusion(f32[1024,4,32]{2,1,0:T(4,128)S(1)} %fusion.27, f32[4,16,1024]{1,0,2:T(4,128)S(1)} %copy-done.2, f32[32]{0:T(128)S(1)} %broadcast_add_fusion, f32[16,1024]{0,1:T(8,128)S(1)} %copy.22, f32[16,1024]{0,1:T(8,128)S(1)} %copy-done.4), kind=kOutput, calls=%fused_computation.18 | convolution fusion | flops 26345472 | bytes 1441920 | tf_op jit(solution)/shard_map/trc,mrc->mtc/dot_general | solution.py:87
  153.5 2.0 copy.29
  155.5 0.1 copy-done.1
  155.5 0.0 copy-done.8
  155.5 0.2 fusion.20
  155.7 0.0 all-gather.3.cloned.1.call-done
  155.7 7.2 %convolution_convert_fusion = bf16[128,4096]{1,0:T(8,128)(2,1)} fusion(bf16[128,1024]{1,0:T(8,128)(2,1)S(1)} %fusion.20, bf16[4096,1024]{1,0:T(8,128)(2,1)} %all-gather.3.cloned.1.call-done), kind=kOutput, calls=%fused_computation.12 | convolution fusion | flops 1074266112 | bytes 9699328 | tf_op jit(solution)/shard_map/dot_general | solution.py:90
  163.0 0.0 reduce-scatter.2.cloned.1.call-update
  163.0 39.7 %reduce-scatter.2.cloned.1.call-done = bf16[128,1024]{1,0:T(8,128)(2,1)} async-done(((bf16[128,4096]{1,0:T(8,128)(2,1)}), bf16[128,1024]{1,0:T(8,128)(2,1)}) %reduce-scatter.2.cloned.1.call-update) | async-done | bytes 262160 | tf_op jit(solution)/shard_map/reduce_scatter | solution.py:96
  (28 shorter events, 0.2 us)
Async XLA Ops:
  6.5 7.7 %copy-start.9 = (u32[32]{0:T(128)S(1)}, u32[32]{0:T(128)}, u32[]{:S(2)}) copy-start(u32[32]{0:T(128)} %constant.55) | copy-start | bytes 388
  6.5 9.2 %copy-start.5 = (f32[1024,16]{0,1:T(8,128)S(1)}, f32[1024,16]{0,1:T(8,128)}, u32[]{:S(2)}) copy-start(f32[1024,16]{0,1:T(8,128)} %param.12) | copy-start | bytes 196612
  6.5 9.1 %copy-start.7 = (bf16[3,3,1024]{2,1,0:T(4,128)(2,1)S(1)}, bf16[3,3,1024]{2,1,0:T(4,128)(2,1)}, u32[]{:S(2)}) copy-start(bf16[3,3,1024]{2,1,0:T(4,128)(2,1)} %param.11) | copy-start | bytes 55300
  6.5 149.2 %all-gather.3.cloned.1.call-start = ((), (), s32[]{:S(2)}) async-start(), calls=%async_computation.1 | async-start | bytes 9437184 | tf_op jit(solution)/shard_map/all_gather | solution.py:92
  7.3 195.5 %reduce-scatter.2.cloned.1.call-start = ((), (), s32[]{:S(2)}) async-start(), calls=%async_computation.2 | async-start | bytes 1310720 | tf_op jit(solution)/shard_map/reduce_scatter | solution.py:96
  8.1 54.7 %collective-permute-start = (bf16[2,3,1024]{2,0,1:T(2,128)(2,1)S(1)}, bf16[2,3,1024]{2,0,1:T(2,128)(2,1)S(1)}, u32[]{:S(2)}, u32[]{:S(2)}) collective-permute-start(bf16[2,3,1024]{2,0,1:T(2,128)(2,1)S(1)} %slice.31), channel_id=1, source_target_pairs={{0,4},{4,8},{8,12},{12,16},{16,20},{20,24},{24,28},{1,5},{5,9},{9,... | collective-permute-start | bytes 36872 | tf_op jit(solution)/shard_map/ppermute | solution.py:12
  14.2 17.2 %copy-start.3 = (f32[16,1024]{0,1:T(8,128)}, f32[16,1024]{0,1:T(8,128)S(1)}, u32[]{:S(2)}) copy-start(f32[16,1024]{0,1:T(8,128)S(1)} %copy.21) | copy-start | bytes 196612
  64.8 1.2 copy-start
  81.6 1.9 copy-start.6
  112.3 29.2 %copy-start.2 = (f32[4,16,1024]{1,0,2:T(4,128)S(1)}, f32[4,16,1024]{1,0,2:T(4,128)}, u32[]{:S(2)}) copy-start(f32[4,16,1024]{1,0,2:T(4,128)} %copy.28) | copy-start | bytes 786436
  112.3 29.2 %copy-start.4 = (f32[16,1024]{0,1:T(8,128)S(1)}, f32[16,1024]{0,1:T(8,128)}, u32[]{:S(2)}) copy-start(f32[16,1024]{0,1:T(8,128)} %copy-done.3) | copy-start | bytes 196612
  153.5 2.0 copy-start.1
  153.5 2.0 copy-start.8
Sparse Core Ops, SparseCore 0:
  9.5 131.8 all-gather.2
  163.1 39.5 reduce-scatter.1
where the time goes:
time: 211 us; the launch traced here: 210 us
  matrix products  67.1 us (32%)
  blocking collectives  43.4 us (21%)
  waiting for transfers between devices  40.5 us (19%)
  local copies, waits for them, and re-layouts  25.5 us (12%)
  other arithmetic  15.1 us (7%)
  between operations  13.6 us (6%)
  starting transfers between devices  4.01 us (2%)
    reduce_scatter x1, waiting for transfers between devices, per_device(): lax.psum_scatter(partial_value.astype(jnp.bfloat16), 'tp', scatter_dimens...  39.7 us
    dot_general x1, matrix products, per_device(): near_part = jnp.einsum('tsc,msc->mtc', toeplitz, blocks, precision=HIGH)  29.2 us
    all_gather x1, blocking collectives, prefix(): lax.all_gather(a.astype(kind), axis)  26.4 us
    unnamed x1, blocking collectives  17 us
    dot_general x1, matrix products, per_device(): block_ends = jnp.einsum('src,msc->mrc', end_weight, blocks, precision=HIGH)  14.8 us
    dot_general x1, local copies, waits for them, and re-layouts, per_device(): toeplitz = jnp.einsum('lc,lts->tsc', short_filter, onehot, precision=HIGH)  14.3 us
    dot_general x1, matrix products, per_device(): far_part = jnp.einsum('trc,mrc->mtc', gain_weight, incoming, precision=HIGH)  12 us
    reduce_sum x1, other arithmetic, per_device(): jnp.sum(residue_rows[None] * jnp.exp(-rate_rows[None] * offsets[:, None,...  11.8 us
  transfers between devices with their start and end apart: 3, of which 1 were waited for; matrix products, arithmetic and copies ran while one was open for 47% of the time, Pallas kernels for 0%

commit v1 on v0

v1 whole, which is shorter than its diff:
```python
import functools

import jax
import jax.numpy as jnp
from jax import lax
from jax.experimental import pallas as pl
from jax.experimental.pallas import tpu as pltpu
from jax.sharding import PartitionSpec as P

LANES = 128
F32 = jnp.float32
BF16 = jnp.bfloat16
VMEM = pl.BlockSpec(memory_space=pltpu.VMEM)
SMEM = pl.BlockSpec(memory_space=pltpu.SMEM)
AXES = ("seq", "tp")


def cost(flops, bytes_accessed):
    return pl.CostEstimate(flops=flops, bytes_accessed=bytes_accessed, transcendentals=0)


def params(**kw):
    return pltpu.CompilerParams(vmem_limit_bytes=40 * 1024 * 1024, **kw)


def local_kernel(
    q_ref, k_ref, v_ref, taps_ref, rates_ref, residues_ref, skip_ref,
    out_ref, message_ref, table_ref,
    signal_s, conv_s, gate_s, message_s,
):
    tokens, channels = q_ref.shape
    poles = rates_ref.shape[1]
    taps = taps_ref.shape[1]
    fold = channels // LANES
    edge = taps - 1
    tap_base = 2 * poles * fold
    skip_base = tap_base + 3 * taps * fold
    later = lax.broadcasted_iota(jnp.int32, (tokens, LANES), 0) >= edge
    table_ref[skip_base : skip_base + fold, :] = skip_ref[...]
    for j in range(fold):
        lanes = slice(j * LANES, (j + 1) * LANES)
        table_ref[pl.ds(j, poles, stride=fold), :] = rates_ref[lanes, :].T
        table_ref[pl.ds(poles * fold + j, poles, stride=fold), :] = residues_ref[lanes, :].T
        mixed = []
        for group, ref in enumerate((q_ref, k_ref, v_ref)):
            value = ref[:, lanes].astype(F32)
            total = None
            for shift in range(taps):
                tap = taps_ref[group, shift : shift + 1, lanes].astype(F32)
                row = tap_base + (group * taps + shift) * fold + j
                table_ref[row : row + 1, :] = tap
                moved = value if shift == 0 else pltpu.roll(value, shift, axis=0)
                total = tap * moved if total is None else total + tap * moved
            mixed.append(total)
            for place in range(2 * edge):
                source = place if place < edge else tokens - 2 * edge + place
                row = (poles + group * 2 * edge + place) * fold + j
                message_s[row : row + 1, :] = value[source : source + 1, :]
        gate_s[:, lanes] = mixed[0]
        signal = jnp.where(later, mixed[1] * mixed[2], 0.0)
        signal_s[pl.ds(j, tokens, stride=fold), :] = signal
    decay = [jnp.exp(-table_ref[r * fold : (r + 1) * fold, :]) for r in range(poles)]
    residue = [table_ref[(poles + r) * fold : (poles + r + 1) * fold, :] for r in range(poles)]
    skip = skip_ref[...]

    def step(t, modes):
        rows = pl.ds(pl.multiple_of(t * fold, fold), fold)
        value = signal_s[rows, :]
        modes = tuple(d * m + c * value for d, c, m in zip(decay, residue, modes))
        conv_s[rows, :] = tree_sum(modes + (skip * value,))
        return modes

    modes = lax.fori_loop(0, tokens, step, (jnp.zeros((fold, LANES), F32),) * poles, unroll=4)
    for r in range(poles):
        message_s[r * fold : (r + 1) * fold, :] = modes[r]
    message_ref[...] = message_s[...].astype(BF16)
    for j in range(fold):
        lanes = slice(j * LANES, (j + 1) * LANES)
        conv = conv_s[pl.ds(j, tokens, stride=fold), :]
        out_ref[:, lanes] = (gate_s[:, lanes] * conv).astype(BF16)


def tree_sum(values):
    values = list(values)
    while len(values) > 1:
        values = [a + b for a, b in zip(values[::2], values[1::2])] + (
            [values[-1]] if len(values) % 2 else []
        )
    return values[0]


def local_part(features, short_taps, rates, residues, skip):
    tokens, _, channels = features.shape
    poles, taps = rates.shape[1], short_taps.shape[1]
    fold = channels // LANES
    message_rows = (poles + 6 * (taps - 1)) * fold
    table_rows = (2 * poles + 3 * taps + 1) * fold
    return pl.pallas_call(
        local_kernel,
        out_shape=(
            jax.ShapeDtypeStruct((tokens, channels), BF16),
            jax.ShapeDtypeStruct((message_rows, LANES), BF16),
            jax.ShapeDtypeStruct((table_rows, LANES), F32),
        ),
        in_specs=[VMEM] * 7,
        out_specs=(VMEM,) * 3,
        scratch_shapes=[
            pltpu.VMEM((tokens * fold, LANES), F32),
            pltpu.VMEM((tokens * fold, LANES), F32),
            pltpu.VMEM((tokens, channels), F32),
            pltpu.VMEM((message_rows, LANES), F32),
        ],
        compiler_params=params(),
        cost_estimate=cost(4 * tokens * channels * poles, 3 << 20),
        name="local_filter",
    )(
        features[:, 0], features[:, 1], features[:, 2],
        short_taps, rates, residues, skip.reshape(fold, LANES),
    )


def far_kernel(poles, taps, count, place_ref, near_ref, q_ref, table_ref, *refs):
    message_refs, (out_ref, conv_s) = refs[:count], refs[count:]
    tokens, channels = near_ref.shape
    fold = channels // LANES
    edge = taps - 1
    shard = place_ref[0]
    tap_base = 2 * poles * fold
    skip_base = tap_base + 3 * taps * fold
    rates = table_ref[0 : poles * fold, :].reshape(poles, fold, LANES)
    residues = table_ref[poles * fold : 2 * poles * fold, :].reshape(poles, fold, LANES)
    skip = table_ref[skip_base : skip_base + fold, :]
    span = jnp.exp(-rates * float(tokens))
    lead = [jnp.exp(-rates * float(tokens - 1 - i)) * residues for i in range(edge)]

    def tap(group, shift):
        row = tap_base + (group * taps + shift) * fold
        return table_ref[row : row + fold, :]

    def message(index):
        if count == 1:
            value = message_refs[0][index]
        else:
            value = message_refs[0][...]
            for i in range(1, count):
                value = jnp.where(index == i, message_refs[i][...], value)
        return value.astype(F32).reshape(-1, fold, LANES)

    def edges(index):
        current = message(index)
        before = jnp.where(index > 0, message(jnp.maximum(index - 1, 0)), 0.0)
        mixed = []
        for group in range(3):
            base = poles + group * 2 * edge
            rows = [before[base + edge + i] for i in range(edge)] + [current[base + i] for i in range(edge)]
            mixed.append(
                [
                    sum(tap(group, shift) * rows[edge + i - shift] for shift in range(taps))
                    for i in range(edge)
                ]
            )
        return current, before, mixed

    def one(index, state):
        current, _, mixed = edges(index)
        state = span * state + current[:poles]
        for i in range(edge):
            state = state + lead[i] * (mixed[1][i] * mixed[2][i])[None]
        return state

    state = lax.fori_loop(0, shard, one, jnp.zeros((poles, fold, LANES), F32))
    _, before, mixed = edges(shard)
    decay = [jnp.exp(-rates[r]) for r in range(poles)]
    modes = tuple(state[r] for r in range(poles))
    for t in range(edge):
        value = mixed[1][t] * mixed[2][t]
        modes = tuple(decay[r] * modes[r] + residues[r] * value for r in range(poles))
        conv_s[t * fold : (t + 1) * fold, :] = tree_sum(modes + (skip * value,))

    def step(t, modes):
        modes = tuple(d * m for d, m in zip(decay, modes))
        conv_s[pl.ds(pl.multiple_of(t * fold, fold), fold), :] = tree_sum(modes)
        return modes

    lax.fori_loop(edge, tokens, step, modes, unroll=6)
    row_id = lax.broadcasted_iota(jnp.int32, (tokens, LANES), 0)
    for j in range(fold):
        lanes = slice(j * LANES, (j + 1) * LANES)
        value = q_ref[:, lanes].astype(F32)
        gate = None
        for shift in range(taps):
            row = tap_base + shift * fold + j
            moved = value if shift == 0 else pltpu.roll(value, shift, axis=0)
            for t in range(shift):
                halo = before[poles + 2 * edge - shift + t][j : j + 1, :]
                moved = jnp.where(row_id == t, halo, moved)
            term = table_ref[row : row + 1, :] * moved
            gate = term if gate is None else gate + term
        conv = conv_s[pl.ds(j, tokens, stride=fold), :]
        out_ref[:, lanes] = (near_ref[:, lanes].astype(F32) + gate * conv).astype(BF16)


def far_part(shard, near, q, table, messages, poles, taps):
    tokens, channels = near.shape
    fold = channels // LANES
    count = len(messages)
    return pl.pallas_call(
        functools.partial(far_kernel, poles, taps, count),
        out_shape=jax.ShapeDtypeStruct((tokens, channels), BF16),
        in_specs=[SMEM] + [VMEM] * (3 + count),
        out_specs=VMEM,
        scratch_shapes=[pltpu.VMEM((tokens * fold, LANES), F32)],
        compiler_params=params(),
        cost_estimate=cost(4 * tokens * channels * poles, 3 << 20),
        name="far_filter",
    )(shard.reshape(1).astype(jnp.int32), near, q, table, *messages)


def project_kernel(place_ref, own_ref, other_ref, w00, w01, w10, w11, out_ref, rows_s):
    z0, y, core = place_ref[0], place_ref[1], place_ref[2]
    tokens = own_ref.shape[0]
    rows_s[:tokens] = own_ref[...]
    rows_s[tokens:] = other_ref[...]
    for dz, dy, ref in ((0, 0, w00), (0, 1, w01), (1, 0, w10), (1, 1, w11)):
        part = lax.dot_general(
            rows_s[...], ref[...], (((1,), (1,)), ((), ())), preferred_element_type=F32
        ).astype(BF16)
        which = (z0 ^ dz) ^ core
        half = y ^ dy
        out_ref[which, 0, half] = part[:tokens]
        out_ref[which, 1, half] = part[tokens:]


def finish_kernel(place_ref, own_ref, side_ref, straight_ref, across_ref, out_ref):
    width = own_ref.shape[2]

    @pl.when(place_ref[0] == 0)
    def _():
        for h in range(2):
            total = own_ref[h].astype(F32) + side_ref[h].astype(F32)
            out_ref[:, h * width : (h + 1) * width] = total.astype(BF16)

    @pl.when(place_ref[0] != 0)
    def _():
        for h in range(2):
            total = straight_ref[h].astype(F32) + across_ref[h].astype(F32)
            out_ref[:, h * width : (h + 1) * width] = total.astype(BF16)


def permute(x, move, keep=None):
    pairs = []
    for index in range(32):
        place = (index // 8, index // 4 % 2, index // 2 % 2, index % 2)
        if keep is None or keep(*place):
            z, y, x_, c = move(*place)
            pairs.append((index, ((z * 2 + y) * 2 + x_) * 2 + c))
    return lax.ppermute(x, AXES, pairs)


def over_y(z, y, x, c):
    return z, 1 - y, x, c


def over_z0(z, y, x, c):
    return z ^ 1, y, x, c


def over_z1(z, y, x, c):
    return z ^ 2, y, x, c


def over_core(z, y, x, c):
    return z, y, x, 1 - c


def per_device_32(features, short_taps, rates, residues, skip, out_weight):
    tokens, _, channels = features.shape
    poles, taps = rates.shape[1], short_taps.shape[1]
    seq, tp = lax.axis_index("seq"), lax.axis_index("tp")
    z, y, x, core = seq // 2, seq % 2, tp // 2, tp % 2
    z1, z0 = z // 2, z % 2
    near, message, table = local_part(features, short_taps, rates, residues, skip)
    pair = jnp.stack([message, permute(message, over_y)])
    by_z = [pair] + [permute(pair, lambda z, y, x, c, k=k: ((z + k) % 4, y, x, c)) for k in (1, 2, 3)]
    table_all = jnp.stack(by_z)
    order = jnp.arange(8)
    messages = table_all[(z - order // 2) % 4, (order % 2) ^ y]
    half_rows = out_weight.shape[0] // 2
    w_y = permute(out_weight, over_y)
    w_z = permute(out_weight, over_z0)
    w_zy = jnp.concatenate(
        [permute(w_z[:half_rows], over_y), permute(w_y[half_rows:], over_z0)], axis=0
    )
    gated = far_part(seq, near, features[:, 0], table, [messages], poles, taps)
    other = permute(gated, over_z1)
    rows = out_weight.shape[0]
    place = jnp.stack([z0, y, core]).astype(jnp.int32)
    partial = pl.pallas_call(
        project_kernel,
        out_shape=jax.ShapeDtypeStruct((2, 2, 2, tokens, rows), BF16),
        in_specs=[SMEM] + [VMEM] * 6,
        out_specs=VMEM,
        scratch_shapes=[pltpu.VMEM((2 * tokens, channels), BF16)],
        compiler_params=params(),
        cost_estimate=cost(16 * tokens * channels * rows, 6 << 20),
        name="project",
    )(place, gated, other, out_weight, w_y, w_z, w_zy)
    from_core = permute(partial[1], over_core)
    summed = (partial[0].astype(F32) + from_core.astype(F32)).astype(BF16)
    own, away = summed[0], summed[1]
    side = permute(own, lambda z, y, x, c: (z, y, 1 - x, c), lambda z, y, x, c: x != z // 2)
    straight = permute(away, over_z1, lambda z, y, x, c: x == z // 2)
    across = permute(
        away, lambda z, y, x, c: (z ^ 2, y, 1 - x, c), lambda z, y, x, c: x != z // 2
    )
    return pl.pallas_call(
        finish_kernel,
        out_shape=jax.ShapeDtypeStruct((tokens, 2 * rows), BF16),
        in_specs=[SMEM] + [VMEM] * 4,
        out_specs=VMEM,
        compiler_params=params(),
        cost_estimate=cost(4 * tokens * rows, 2 << 20),
        name="finish",
    )((x ^ z1).reshape(1).astype(jnp.int32), own, side, straight, across)


def per_device(features, short_taps, rates, residues, skip, out_weight):
    poles, taps = rates.shape[1], short_taps.shape[1]
    near, message, table = local_part(features, short_taps, rates, residues, skip)
    messages = lax.all_gather(message, "seq")
    gated = far_part(
        lax.axis_index("seq"), near, features[:, 0], table, [messages], poles, taps
    )
    partial = lax.dot_general(
        gated,
        lax.all_gather(out_weight, "seq", axis=0, tiled=True),
        (((1,), (1,)), ((), ())),
        preferred_element_type=F32,
    )
    return lax.psum_scatter(partial.astype(BF16), "tp", scatter_dimension=1, tiled=True)


def solution(mesh):
    in_specs = (
        P("seq", None, "tp"),
        P(None, None, "tp"),
        P("tp", None),
        P("tp", None),
        P("tp"),
        P("seq", "tp"),
    )
    out_specs = P("seq", "tp")
    body = per_device_32 if (mesh.shape["seq"], mesh.shape["tp"]) == (8, 4) else per_device
    return jax.shard_map(body, mesh=mesh, in_specs=in_specs, out_specs=out_specs, check_vma=False)
```

time: 211 us -> 86 us (0.41)
  the two profiles are of different devices: /device:TPU:1 before, /device:TPU:0 now
where the time goes in v1:
time: 86 us; the launch traced here: 85.7 us
  waiting for transfers between devices  44.4 us (52%)
  starting transfers between devices  25.9 us (30%)
  local copies, waits for them, and re-layouts  6.68 us (8%)
  Pallas kernels  5.99 us (7%)
  other arithmetic  2.43 us (3%)
    ppermute x13, waiting for transfers between devices, permute(): return lax.ppermute(x, AXES, pairs)  44.4 us
    ppermute x13, starting transfers between devices, permute(): return lax.ppermute(x, AXES, pairs)  25.9 us
    pallas_call x1, Pallas kernels, local_part(): pl.pallas_call(local_kernel, out_shape=(jax.ShapeDtypeStruct((tokens, cha...  2.48 us
    unnamed x16, local copies, waits for them, and re-layouts  2.11 us
    pallas_call x1, Pallas kernels, per_device_32(): pl.pallas_call(project_kernel, out_shape=jax.ShapeDtypeStruct((2, 2, 2, t...  1.82 us
  transfers between devices with their start and end apart: 13, of which 7 were waited for; matrix products, arithmetic and copies ran while one was open for 10% of the time, Pallas kernels for 4%

profile of v1, /device:TPU:0, one launch (start us, length us, event | category | flops | bytes accessed | tf_op | source)
XLA Modules:
  0.0 85.7 jit_solution(18098841966014459577)
XLA Ops:
  0.0 3.0 %collective-permute-start.5 = (bf16[512,1024]{1,0:T(8,128)(2,1)}, bf16[512,1024]{1,0:T(8,128)(2,1)S(1)}, u32[]{:S(2)}, u32[]{:S(2)}) collective-permute-start(bf16[512,1024]{1,0:T(8,128)(2,1)} %w00.1), channel_id=1, source_target_pairs={{0,4},{1,5},{2,6},{3,7},{4,0},{5,1},{6,2},{7,3},{8,12},{9,13},{10,... | collective-permute-start | bytes 3145736 | tf_op jit(solution)/shard_map/ppermute | solution.py:257
  3.0 1.6 %collective-permute-start.6 = (bf16[512,1024]{1,0:T(8,128)(2,1)}, bf16[512,1024]{1,0:T(8,128)(2,1)S(1)}, u32[]{:S(2)}, u32[]{:S(2)}) collective-permute-start(bf16[512,1024]{1,0:T(8,128)(2,1)} %w00.1), channel_id=1, source_target_pairs={{0,8},{1,9},{2,10},{3,11},{4,12},{5,13},{6,14},{7,15},{8,0},{9,1},... | collective-permute-start | bytes 3145736 | tf_op jit(solution)/shard_map/ppermute | solution.py:257
  4.5 1.0 %copy.7.rates_ref = f32[1024,16]{1,0:T(8,128)S(1)} copy(f32[1024,16]{0,1:T(8,128)} %param.8) | data formatting | bytes 131072 | tf_op args[2]
  5.6 0.0 copy-start.5
  5.6 0.0 copy-start.6
  5.6 1.0 %copy.8.residues_ref = f32[1024,16]{1,0:T(8,128)S(1)} copy(f32[1024,16]{0,1:T(8,128)} %param.9) | data formatting | bytes 131072 | tf_op args[3]
  6.7 1.2 %slice_bitcast_fusion.4 = (bf16[128,1024]{1,0:T(8,128)(2,1)S(1)}, bf16[128,1024]{1,0:T(8,128)(2,1)S(1)}, bf16[128,1024]{1,0:T(8,128)(2,1)S(1)}) fusion(bf16[128,3,1024]{2,0,1:T(8,128)(2,1)} %param.6), kind=kLoop, calls=%fused_computation.9 | loop fusion | bytes 1572864 | tf_op jit(solution)/shard_map/squeeze | solution.py:117
  7.8 0.0 copy-done.5
  7.8 0.0 copy-done.6
  7.9 2.5 %local_filter.1 = (bf16[128,1024]{1,0:T(8,128)(2,1)S(1)}, bf16[224,128]{1,0:T(8,128)(2,1)S(1)}, f32[336,128]{1,0:T(8,128)S(1)}) custom-call(bf16[128,1024]{1,0:T(8,128)(2,1)S(1)} %get-tuple-element.12.q_ref, bf16[128,1024]{1,0:T(8,128)(2,1)S(1)} %get-tuple-element.13.k_ref, bf16[128,1024]{1,0:T(8,128)(2,1)S(1)} %get-tuple-element.11.v_ref, ...), custom_call_target="tpu_custom_call" | custom-call | flops 8388608 | bytes 3145728 | tf_op jit(solution)/shard_map/local_filter/pallas_call | solution.py:98
  10.3 0.0 copy-start.1
  10.4 0.0 copy-start.3
  10.4 0.6 collective-permute-start
  10.9 16.0 %collective-permute-done.5.w01 = bf16[512,1024]{1,0:T(8,128)(2,1)S(1)} collective-permute-done((bf16[512,1024]{1,0:T(8,128)(2,1)}, bf16[512,1024]{1,0:T(8,128)(2,1)S(1)}, u32[]{:S(2)}, u32[]{:S(2)}) %collective-permute-start.5) | collective-permute-done | bytes 1048608 | tf_op jit(solution)/shard_map/ppermute | solution.py:257
  26.9 0.8 slice.40
  27.8 1.8 %collective-permute-start.8 = (bf16[256,1024]{1,0:T(8,128)(2,1)}, bf16[256,1024]{1,0:T(8,128)(2,1)}, u32[]{:S(2)}, u32[]{:S(2)}) collective-permute-start(bf16[256,1024]{1,0:T(8,128)(2,1)} %slice.40), channel_id=1, source_target_pairs={{0,8},{1,9},{2,10},{3,11},{4,12},{5,13},{6,14},{7,15},{8,0},{9,1},... | collective-permute-start | bytes 1572872 | tf_op jit(solution)/shard_map/ppermute | solution.py:257
  29.6 0.0 collective-permute-done.6.w10
  29.6 0.8 slice.39
  30.4 0.0 copy-done.1
  30.4 0.0 copy-done.3
  30.4 1.5 %collective-permute-start.7 = (bf16[256,1024]{1,0:T(8,128)(2,1)}, bf16[256,1024]{1,0:T(8,128)(2,1)}, u32[]{:S(2)}, u32[]{:S(2)}) collective-permute-start(bf16[256,1024]{1,0:T(8,128)(2,1)} %slice.39), channel_id=1, source_target_pairs={{0,4},{1,5},{2,6},{3,7},{4,0},{5,1},{6,2},{7,3},{8,12},{9,13},{10,... | collective-permute-start | bytes 1572872 | tf_op jit(solution)/shard_map/ppermute | solution.py:257
  31.9 0.0 collective-permute-done
  32.0 2.7 %collective-permute-start.2 = (bf16[2,224,128]{2,1,0:T(8,128)(2,1)S(1)}, bf16[2,224,128]{2,1,0:T(8,128)(2,1)S(1)}, u32[]{:S(2)}, u32[]{:S(2)}) collective-permute-start(bf16[2,224,128]{2,1,0:T(8,128)(2,1)S(1)} %get-tuple-element.17), channel_id=1, source_target_pairs={{0,16},{1,17},{2,18},{3,19},{4,20},{5,21},{6,22},{7,23},{8,24},{9,... | collective-permute-start | bytes 344072 | tf_op jit(solution)/shard_map/ppermute | solution.py:257
  34.6 0.4 collective-permute-start.1
  35.1 3.4 %collective-permute-start.3 = (bf16[2,224,128]{2,1,0:T(8,128)(2,1)S(1)}, bf16[2,224,128]{2,1,0:T(8,128)(2,1)S(1)}, u32[]{:S(2)}, u32[]{:S(2)}) collective-permute-start(bf16[2,224,128]{2,1,0:T(8,128)(2,1)S(1)} %get-tuple-element.17), channel_id=1, source_target_pairs={{0,24},{1,25},{2,26},{3,27},{4,28},{5,29},{6,30},{7,31},{8,0},{9,1... | collective-permute-start | bytes 344072 | tf_op jit(solution)/shard_map/ppermute | solution.py:257
  38.5 5.9 %collective-permute-done.2 = bf16[2,224,128]{2,1,0:T(8,128)(2,1)S(1)} collective-permute-done((bf16[2,224,128]{2,1,0:T(8,128)(2,1)S(1)}, bf16[2,224,128]{2,1,0:T(8,128)(2,1)S(1)}, u32[]{:S(2)}, u32[]{:S(2)}) %collective-permute-start.2) | collective-permute-done | bytes 114720 | tf_op jit(solution)/shard_map/ppermute | solution.py:257
  44.4 4.2 %collective-permute-done.1 = bf16[2,224,128]{2,1,0:T(8,128)(2,1)S(1)} collective-permute-done((bf16[2,224,128]{2,1,0:T(8,128)(2,1)S(1)}, bf16[2,224,128]{2,1,0:T(8,128)(2,1)S(1)}, u32[]{:S(2)}, u32[]{:S(2)}) %collective-permute-start.1) | collective-permute-done | bytes 114720 | tf_op jit(solution)/shard_map/ppermute | solution.py:257
  48.6 0.0 collective-permute-done.3
  48.6 0.8 pad_maximum_fusion.1
  49.4 1.7 %gather_fusion = bf16[8,224,128]{2,1,0:T(8,128)(2,1)S(1)} fusion(bf16[4,2,224,128]{3,2,1,0:T(8,128)(2,1)} %pad_maximum_fusion.1, s32[8]{0:T(128)S(1)} %fusion.5), kind=kCustom, calls=%fused_computation | custom fusion | bytes 917568 | tf_op jit(solution)/shard_map/gather | solution.py:287
  51.1 0.9 %far_filter.1.own_ref = bf16[128,1024]{1,0:T(8,128)(2,1)S(1)} custom-call(s32[1]{0:T(128)} %bitcast.4.place_ref, bf16[128,1024]{1,0:T(8,128)(2,1)S(1)} %copy-done.2, bf16[128,1024]{1,0:T(8,128)(2,1)S(1)} %get-tuple-element.12.q_ref, f32[336,128]{1,0:T(8,128)S(1)} %copy-done.4, bf16[8,224,128]{2,1,0:T(8,128)(2,1)S(1)} %gather_fusion), custom_call_target="tpu_custom_call" | custom-call | flops 8388608 | bytes 3145728 | tf_op jit(solution)/shard_map/far_filter/pallas_call | solution.py:207
  52.0 2.0 %collective-permute-start.4 = (bf16[128,1024]{1,0:T(8,128)(2,1)S(1)}, bf16[128,1024]{1,0:T(8,128)(2,1)S(1)}, u32[]{:S(2)}, u32[]{:S(2)}) collective-permute-start(bf16[128,1024]{1,0:T(8,128)(2,1)S(1)} %far_filter.1.own_ref), channel_id=1, source_target_pairs={{0,16},{1,17},{2,18},{3,19},{4,20},{5,21},{6,22},{7,23},{8,24},{9,... | collective-permute-start | bytes 786440 | tf_op jit(solution)/shard_map/ppermute | solution.py:257
  54.0 0.1 pad_add_fusion.place_ref
  54.0 0.0 collective-permute-done.8
  54.0 0.0 collective-permute-done.7
  54.0 1.4 %pad_maximum_fusion.w11 = bf16[512,1024]{1,0:T(8,128)(2,1)S(1)} fusion(bf16[256,1024]{1,0:T(8,128)(2,1)} %collective-permute-done.8, bf16[256,1024]{1,0:T(8,128)(2,1)} %collective-permute-done.7), kind=kLoop, calls=%fused_computation.1 | loop fusion | flops 2097152 | bytes 2097152 | tf_op jit(solution)/shard_map/concatenate | solution.py:291
  55.4 8.1 %collective-permute-done.4.other_ref = bf16[128,1024]{1,0:T(8,128)(2,1)S(1)} collective-permute-done((bf16[128,1024]{1,0:T(8,128)(2,1)S(1)}, bf16[128,1024]{1,0:T(8,128)(2,1)S(1)}, u32[]{:S(2)}, u32[]{:S(2)}) %collective-permute-start.4) | collective-permute-done | bytes 262176 | tf_op jit(solution)/shard_map/ppermute | solution.py:257
  63.5 1.8 %project.1 = bf16[2,2,2,128,512]{4,3,2,1,0:T(8,128)(2,1)S(1)} custom-call(s32[3]{0:T(128)S(1)} %pad_add_fusion.place_ref, bf16[128,1024]{1,0:T(8,128)(2,1)S(1)} %far_filter.1.own_ref, bf16[128,1024]{1,0:T(8,128)(2,1)S(1)} %collective-permute-done.4.other_ref, bf16[512,1024]{1,0:T(8,128)(2,1)S(1)} %copy-done, ...), custom_call_target="tpu_custom_call" | custom-call | flops 1073741824 | bytes 6291456 | tf_op jit(solution)/shard_map/project/pallas_call | solution.py:298
  65.3 0.1 collective-permute-start.9
  65.4 1.9 %collective-permute-done.9 = bf16[2,2,128,512]{3,2,1,0:T(8,128)(2,1)S(1)} collective-permute-done((bf16[2,2,128,512]{3,2,1,0:T(8,128)(2,1)S(1)}, bf16[2,2,128,512]{3,2,1,0:T(8,128)(2,1)S(1)}, u32[]{:S(2)}, u32[]{:S(2)}) %collective-permute-start.9) | collective-permute-done | bytes 524320 | tf_op jit(solution)/shard_map/ppermute | solution.py:257
  67.3 0.1 fusion
  67.5 0.7 collective-permute-start.12
  68.2 7.0 %collective-permute-start.11 = (bf16[2,128,512]{2,1,0:T(8,128)(2,1)S(1)}, bf16[2,128,512]{2,1,0:T(8,128)(2,1)S(1)}, u32[]{:S(2)}, u32[]{:S(2)}) collective-permute-start(bf16[2,128,512]{2,1,0:T(8,128)(2,1)S(1)} %get-tuple-element.14), channel_id=1, source_target_pairs={{0,16},{1,17},{4,20},{5,21},{8,24},{9,25},{12,28},{13,29},{18,2},{... | collective-permute-start | bytes 786440 | tf_op jit(solution)/shard_map/ppermute | solution.py:257
  75.2 1.3 %collective-permute-start.10 = (bf16[2,128,512]{2,1,0:T(8,128)(2,1)S(1)}, bf16[2,128,512]{2,1,0:T(8,128)(2,1)S(1)}, u32[]{:S(2)}, u32[]{:S(2)}) collective-permute-start(bf16[2,128,512]{2,1,0:T(8,128)(2,1)S(1)} %get-tuple-element.15.own_ref), channel_id=1, source_target_pairs={{2,0},{3,1},{6,4},{7,5},{10,8},{11,9},{14,12},{15,13},{16,18},{17,... | collective-permute-start | bytes 786440 | tf_op jit(solution)/shard_map/ppermute | solution.py:257
  76.5 0.0 collective-permute-done.12.across_ref
  76.5 4.2 %collective-permute-done.11.straight_ref = bf16[2,128,512]{2,1,0:T(8,128)(2,1)S(1)} collective-permute-done((bf16[2,128,512]{2,1,0:T(8,128)(2,1)S(1)}, bf16[2,128,512]{2,1,0:T(8,128)(2,1)S(1)}, u32[]{:S(2)}, u32[]{:S(2)}) %collective-permute-start.11) | collective-permute-done | bytes 262176 | tf_op jit(solution)/shard_map/ppermute | solution.py:257
  80.8 4.1 %collective-permute-done.10.side_ref = bf16[2,128,512]{2,1,0:T(8,128)(2,1)S(1)} collective-permute-done((bf16[2,128,512]{2,1,0:T(8,128)(2,1)S(1)}, bf16[2,128,512]{2,1,0:T(8,128)(2,1)S(1)}, u32[]{:S(2)}, u32[]{:S(2)}) %collective-permute-start.10) | collective-permute-done | bytes 262176 | tf_op jit(solution)/shard_map/ppermute | solution.py:257
  84.9 0.8 finish.1
  (10 shorter events, 0.1 us)
Async XLA Ops:
  0.0 26.9 %collective-permute-start.5 = (bf16[512,1024]{1,0:T(8,128)(2,1)}, bf16[512,1024]{1,0:T(8,128)(2,1)S(1)}, u32[]{:S(2)}, u32[]{:S(2)}) collective-permute-start(bf16[512,1024]{1,0:T(8,128)(2,1)} %w00.1), channel_id=1, source_target_pairs={{0,4},{1,5},{2,6},{3,7},{4,0},{5,1},{6,2},{7,3},{8,12},{9,13},{10,... | collective-permute-start | bytes 3145736 | tf_op jit(solution)/shard_map/ppermute | solution.py:257
  3.0 26.6 %collective-permute-start.6 = (bf16[512,1024]{1,0:T(8,128)(2,1)}, bf16[512,1024]{1,0:T(8,128)(2,1)S(1)}, u32[]{:S(2)}, u32[]{:S(2)}) collective-permute-start(bf16[512,1024]{1,0:T(8,128)(2,1)} %w00.1), channel_id=1, source_target_pairs={{0,8},{1,9},{2,10},{3,11},{4,12},{5,13},{6,14},{7,15},{8,0},{9,1},... | collective-permute-start | bytes 3145736 | tf_op jit(solution)/shard_map/ppermute | solution.py:257
  5.6 2.3 %copy-start.5 = (bf16[3,3,1024]{2,1,0:T(4,128)(2,1)S(1)}, bf16[3,3,1024]{2,1,0:T(4,128)(2,1)}, u32[]{:S(2)}) copy-start(bf16[3,3,1024]{2,1,0:T(4,128)(2,1)} %taps_ref.1) | copy-start | bytes 55300
  5.6 2.3 %copy-start.6 = (f32[1024]{0:T(1024)S(1)}, f32[1024]{0:T(1024)}, u32[]{:S(2)}) copy-start(f32[1024]{0:T(1024)} %param.10) | copy-start | bytes 12292
  10.3 20.1 %copy-start.1 = (bf16[128,1024]{1,0:T(8,128)(2,1)}, bf16[128,1024]{1,0:T(8,128)(2,1)S(1)}, u32[]{:S(2)}) copy-start(bf16[128,1024]{1,0:T(8,128)(2,1)S(1)} %get-tuple-element.8.near_ref) | copy-start | bytes 786436
  10.4 20.1 %copy-start.3 = (f32[336,128]{1,0:T(8,128)}, f32[336,128]{1,0:T(8,128)S(1)}, u32[]{:S(2)}) copy-start(f32[336,128]{1,0:T(8,128)S(1)} %get-tuple-element.9.table_ref) | copy-start | bytes 516100
  10.4 21.6 %collective-permute-start = (bf16[224,128]{1,0:T(8,128)(2,1)S(1)}, bf16[224,128]{1,0:T(8,128)(2,1)S(1)}, u32[]{:S(2)}, u32[]{:S(2)}) collective-permute-start(bf16[224,128]{1,0:T(8,128)(2,1)S(1)} %get-tuple-element.10), channel_id=1, source_target_pairs={{0,4},{1,5},{2,6},{3,7},{4,0},{5,1},{6,2},{7,3},{8,12},{9,13},{10,... | collective-permute-start | bytes 172040 | tf_op jit(solution)/shard_map/ppermute | solution.py:257
  27.8 26.3 %collective-permute-start.8 = (bf16[256,1024]{1,0:T(8,128)(2,1)}, bf16[256,1024]{1,0:T(8,128)(2,1)}, u32[]{:S(2)}, u32[]{:S(2)}) collective-permute-start(bf16[256,1024]{1,0:T(8,128)(2,1)} %slice.40), channel_id=1, source_target_pairs={{0,8},{1,9},{2,10},{3,11},{4,12},{5,13},{6,14},{7,15},{8,0},{9,1},... | collective-permute-start | bytes 1572872 | tf_op jit(solution)/shard_map/ppermute | solution.py:257
  30.4 23.6 %collective-permute-start.7 = (bf16[256,1024]{1,0:T(8,128)(2,1)}, bf16[256,1024]{1,0:T(8,128)(2,1)}, u32[]{:S(2)}, u32[]{:S(2)}) collective-permute-start(bf16[256,1024]{1,0:T(8,128)(2,1)} %slice.39), channel_id=1, source_target_pairs={{0,4},{1,5},{2,6},{3,7},{4,0},{5,1},{6,2},{7,3},{8,12},{9,13},{10,... | collective-permute-start | bytes 1572872 | tf_op jit(solution)/shard_map/ppermute | solution.py:257
  32.0 19.1 %copy-start.2 = (bf16[128,1024]{1,0:T(8,128)(2,1)S(1)}, bf16[128,1024]{1,0:T(8,128)(2,1)}, u32[]{:S(2)}) copy-start(bf16[128,1024]{1,0:T(8,128)(2,1)} %copy-done.1) | copy-start | bytes 786436
  32.0 19.1 %copy-start.4 = (f32[336,128]{1,0:T(8,128)S(1)}, f32[336,128]{1,0:T(8,128)}, u32[]{:S(2)}) copy-start(f32[336,128]{1,0:T(8,128)} %copy-done.3) | copy-start | bytes 516100
  32.0 12.4 %collective-permute-start.2 = (bf16[2,224,128]{2,1,0:T(8,128)(2,1)S(1)}, bf16[2,224,128]{2,1,0:T(8,128)(2,1)S(1)}, u32[]{:S(2)}, u32[]{:S(2)}) collective-permute-start(bf16[2,224,128]{2,1,0:T(8,128)(2,1)S(1)} %get-tuple-element.17), channel_id=1, source_target_pairs={{0,16},{1,17},{2,18},{3,19},{4,20},{5,21},{6,22},{7,23},{8,24},{9,... | collective-permute-start | bytes 344072 | tf_op jit(solution)/shard_map/ppermute | solution.py:257
  34.6 13.9 %collective-permute-start.1 = (bf16[2,224,128]{2,1,0:T(8,128)(2,1)S(1)}, bf16[2,224,128]{2,1,0:T(8,128)(2,1)S(1)}, u32[]{:S(2)}, u32[]{:S(2)}) collective-permute-start(bf16[2,224,128]{2,1,0:T(8,128)(2,1)S(1)} %get-tuple-element.17), channel_id=1, source_target_pairs={{0,8},{1,9},{2,10},{3,11},{4,12},{5,13},{6,14},{7,15},{8,16},{9,17... | collective-permute-start | bytes 344072 | tf_op jit(solution)/shard_map/ppermute | solution.py:257
  35.1 13.5 %collective-permute-start.3 = (bf16[2,224,128]{2,1,0:T(8,128)(2,1)S(1)}, bf16[2,224,128]{2,1,0:T(8,128)(2,1)S(1)}, u32[]{:S(2)}, u32[]{:S(2)}) collective-permute-start(bf16[2,224,128]{2,1,0:T(8,128)(2,1)S(1)} %get-tuple-element.17), channel_id=1, source_target_pairs={{0,24},{1,25},{2,26},{3,27},{4,28},{5,29},{6,30},{7,31},{8,0},{9,1... | collective-permute-start | bytes 344072 | tf_op jit(solution)/shard_map/ppermute | solution.py:257
  52.0 11.5 %collective-permute-start.4 = (bf16[128,1024]{1,0:T(8,128)(2,1)S(1)}, bf16[128,1024]{1,0:T(8,128)(2,1)S(1)}, u32[]{:S(2)}, u32[]{:S(2)}) collective-permute-start(bf16[128,1024]{1,0:T(8,128)(2,1)S(1)} %far_filter.1.own_ref), channel_id=1, source_target_pairs={{0,16},{1,17},{2,18},{3,19},{4,20},{5,21},{6,22},{7,23},{8,24},{9,... | collective-permute-start | bytes 786440 | tf_op jit(solution)/shard_map/ppermute | solution.py:257
  54.0 9.4 %copy-start = (bf16[512,1024]{1,0:T(8,128)(2,1)S(1)}, bf16[512,1024]{1,0:T(8,128)(2,1)}, u32[]{:S(2)}) copy-start(bf16[512,1024]{1,0:T(8,128)(2,1)} %w00.1) | copy-start | bytes 3145732
  65.3 2.0 %collective-permute-start.9 = (bf16[2,2,128,512]{3,2,1,0:T(8,128)(2,1)S(1)}, bf16[2,2,128,512]{3,2,1,0:T(8,128)(2,1)S(1)}, u32[]{:S(2)}, u32[]{:S(2)}) collective-permute-start(bf16[2,2,128,512]{3,2,1,0:T(8,128)(2,1)S(1)} %slice_bitcast_fusion), channel_id=1, source_target_pairs={{0,1},{1,0},{2,3},{3,2},{4,5},{5,4},{6,7},{7,6},{8,9},{9,8},{10,11... | collective-permute-start | bytes 1572872 | tf_op jit(solution)/shard_map/ppermute | solution.py:257
  67.5 9.0 %collective-permute-start.12 = (bf16[2,128,512]{2,1,0:T(8,128)(2,1)S(1)}, bf16[2,128,512]{2,1,0:T(8,128)(2,1)S(1)}, u32[]{:S(2)}, u32[]{:S(2)}) collective-permute-start(bf16[2,128,512]{2,1,0:T(8,128)(2,1)S(1)} %get-tuple-element.14), channel_id=1, source_target_pairs={{2,16},{3,17},{6,20},{7,21},{10,24},{11,25},{14,28},{15,29},{16,2}... | collective-permute-start | bytes 786440 | tf_op jit(solution)/shard_map/ppermute | solution.py:257
  68.2 12.6 %collective-permute-start.11 = (bf16[2,128,512]{2,1,0:T(8,128)(2,1)S(1)}, bf16[2,128,512]{2,1,0:T(8,128)(2,1)S(1)}, u32[]{:S(2)}, u32[]{:S(2)}) collective-permute-start(bf16[2,128,512]{2,1,0:T(8,128)(2,1)S(1)} %get-tuple-element.14), channel_id=1, source_target_pairs={{0,16},{1,17},{4,20},{5,21},{8,24},{9,25},{12,28},{13,29},{18,2},{... | collective-permute-start | bytes 786440 | tf_op jit(solution)/shard_map/ppermute | solution.py:257
  75.2 9.7 %collective-permute-start.10 = (bf16[2,128,512]{2,1,0:T(8,128)(2,1)S(1)}, bf16[2,128,512]{2,1,0:T(8,128)(2,1)S(1)}, u32[]{:S(2)}, u32[]{:S(2)}) collective-permute-start(bf16[2,128,512]{2,1,0:T(8,128)(2,1)S(1)} %get-tuple-element.15.own_ref), channel_id=1, source_target_pairs={{2,0},{3,1},{6,4},{7,5},{10,8},{11,9},{14,12},{15,13},{16,18},{17,... | collective-permute-start | bytes 786440 | tf_op jit(solution)/shard_map/ppermute | solution.py:257

commit v2 on v1

v2 whole, which is shorter than its diff:
```python
import functools

import jax
import jax.numpy as jnp
from jax import lax
from jax.experimental import pallas as pl
from jax.experimental.pallas import tpu as pltpu
from jax.sharding import PartitionSpec as P

LANES = 128
F32 = jnp.float32
BF16 = jnp.bfloat16
VMEM = pl.BlockSpec(memory_space=pltpu.VMEM)
SMEM = pl.BlockSpec(memory_space=pltpu.SMEM)
AXES = ("seq", "tp")


def cost(flops, bytes_accessed):
    return pl.CostEstimate(flops=flops, bytes_accessed=bytes_accessed, transcendentals=0)


def params(**kw):
    return pltpu.CompilerParams(vmem_limit_bytes=40 * 1024 * 1024, **kw)


def local_kernel(
    q_ref, k_ref, v_ref, taps_ref, rates_ref, residues_ref, skip_ref,
    out_ref, message_ref, table_ref,
    signal_s, conv_s, gate_s, message_s,
):
    tokens, channels = q_ref.shape
    poles = rates_ref.shape[0]
    taps = taps_ref.shape[1]
    fold = channels // LANES
    edge = taps - 1
    tap_base = 2 * poles * fold
    skip_base = tap_base + 3 * taps * fold
    later = lax.broadcasted_iota(jnp.int32, (tokens, LANES), 0) >= edge
    table_ref[skip_base : skip_base + fold, :] = skip_ref[...]
    for j in range(fold):
        lanes = slice(j * LANES, (j + 1) * LANES)
        table_ref[pl.ds(j, poles, stride=fold), :] = rates_ref[:, lanes]
        table_ref[pl.ds(poles * fold + j, poles, stride=fold), :] = residues_ref[:, lanes]
        mixed = []
        for group, ref in enumerate((q_ref, k_ref, v_ref)):
            value = ref[:, lanes].astype(F32)
            total = None
            for shift in range(taps):
                tap = taps_ref[group, shift : shift + 1, lanes].astype(F32)
                row = tap_base + (group * taps + shift) * fold + j
                table_ref[row : row + 1, :] = tap
                moved = value if shift == 0 else pltpu.roll(value, shift, axis=0)
                total = tap * moved if total is None else total + tap * moved
            mixed.append(total)
            for place in range(2 * edge):
                source = place if place < edge else tokens - 2 * edge + place
                row = (poles + group * 2 * edge + place) * fold + j
                message_s[row : row + 1, :] = value[source : source + 1, :]
        gate_s[:, lanes] = mixed[0]
        signal = jnp.where(later, mixed[1] * mixed[2], 0.0)
        signal_s[pl.ds(j, tokens, stride=fold), :] = signal
    decay = [jnp.exp(-table_ref[r * fold : (r + 1) * fold, :]) for r in range(poles)]
    residue = [table_ref[(poles + r) * fold : (poles + r + 1) * fold, :] for r in range(poles)]
    skip = skip_ref[...]

    def step(t, modes):
        rows = pl.ds(pl.multiple_of(t * fold, fold), fold)
        value = signal_s[rows, :]
        modes = tuple(d * m + c * value for d, c, m in zip(decay, residue, modes))
        conv_s[rows, :] = tree_sum(modes + (skip * value,))
        return modes

    modes = lax.fori_loop(0, tokens, step, (jnp.zeros((fold, LANES), F32),) * poles, unroll=4)
    for r in range(poles):
        message_s[r * fold : (r + 1) * fold, :] = modes[r]
    message_ref[...] = message_s[...].astype(BF16)
    for j in range(fold):
        lanes = slice(j * LANES, (j + 1) * LANES)
        conv = conv_s[pl.ds(j, tokens, stride=fold), :]
        out_ref[:, lanes] = (gate_s[:, lanes] * conv).astype(BF16)


def tree_sum(values):
    values = list(values)
    while len(values) > 1:
        values = [a + b for a, b in zip(values[::2], values[1::2])] + (
            [values[-1]] if len(values) % 2 else []
        )
    return values[0]


def local_part(features, short_taps, rates, residues, skip):
    tokens, _, channels = features.shape
    poles, taps = rates.shape[1], short_taps.shape[1]
    fold = channels // LANES
    message_rows = (poles + 6 * (taps - 1)) * fold
    table_rows = (2 * poles + 3 * taps + 1) * fold
    return pl.pallas_call(
        local_kernel,
        out_shape=(
            jax.ShapeDtypeStruct((tokens, channels), BF16),
            jax.ShapeDtypeStruct((message_rows, LANES), BF16),
            jax.ShapeDtypeStruct((table_rows, LANES), F32),
        ),
        in_specs=[VMEM] * 7,
        out_specs=(VMEM,) * 3,
        scratch_shapes=[
            pltpu.VMEM((tokens * fold, LANES), F32),
            pltpu.VMEM((tokens * fold, LANES), F32),
            pltpu.VMEM((tokens, channels), F32),
            pltpu.VMEM((message_rows, LANES), F32),
        ],
        compiler_params=params(),
        cost_estimate=cost(4 * tokens * channels * poles, 3 << 20),
        name="local_filter",
    )(
        features[:, 0], features[:, 1], features[:, 2],
        short_taps, rates.T, residues.T, skip.reshape(fold, LANES),
    )


class Table:
    def __init__(self, ref, poles, taps, fold, tokens):
        self.ref, self.poles, self.taps, self.fold, self.edge = ref, poles, taps, fold, taps - 1
        self.rates = ref[0 : poles * fold, :].reshape(poles, fold, LANES)
        self.residues = ref[poles * fold : 2 * poles * fold, :].reshape(poles, fold, LANES)
        self.tap_base = 2 * poles * fold
        skip_base = self.tap_base + 3 * taps * fold
        self.skip = ref[skip_base : skip_base + fold, :]
        self.tokens = tokens

    def span(self, shards):
        return jnp.exp(-self.rates * float(shards * self.tokens))

    def tap(self, group, shift):
        row = self.tap_base + (group * self.taps + shift) * self.fold
        return self.ref[row : row + self.fold, :]

    def message(self, value):
        return value.astype(F32).reshape(-1, self.fold, LANES)

    def first(self, message, group):
        base = self.poles + group * 2 * self.edge
        return [message[base + i] for i in range(self.edge)]

    def last(self, message, group):
        base = self.poles + group * 2 * self.edge + self.edge
        return [message[base + i] for i in range(self.edge)]

    def mixed(self, before, current, group):
        rows = self.last(before, group) + self.first(current, group)
        return [
            sum(self.tap(group, shift) * rows[self.edge + i - shift] for shift in range(self.taps))
            for i in range(self.edge)
        ]

    def signals(self, before, current):
        pairs = zip(self.mixed(before, current, 1), self.mixed(before, current, 2))
        return [k * v for k, v in pairs]

    def lead(self, shards):
        last = shards * self.tokens - 1
        return [jnp.exp(-self.rates * float(last - i)) * self.residues for i in range(self.edge)]

    def enter(self, state, span, lead, before, current):
        state = span * state + current[: self.poles]
        for weight, value in zip(lead, self.signals(before, current)):
            state = state + weight * value[None]
        return state


def enter_any(table, place_ref, messages_ref):
    span, lead = table.span(1), table.lead(1)

    def pick(index):
        current = table.message(messages_ref[index])
        before = table.message(messages_ref[jnp.maximum(index - 1, 0)])
        return jnp.where(index > 0, before, 0.0), current

    def one(index, state):
        return table.enter(state, span, lead, *pick(index))

    zero = jnp.zeros((table.poles, table.fold, LANES), F32)
    state = lax.fori_loop(0, place_ref[0], one, zero)
    return (state,) + pick(place_ref[0])


def enter_joined(spans, table, place_ref, own_ref, other_ref, *refs):
    joined = [table.message(ref[...]) for ref in refs]
    own, other = table.message(own_ref[...]), table.message(other_ref[...])
    before = jnp.zeros_like(own)
    state = before[: table.poles]
    for shards, current in zip(spans[::-1], joined[::-1]):
        state = table.enter(state, table.span(shards), table.lead(shards), before, current)
        before = current
    second = place_ref[0] == 1
    behind = table.enter(state, table.span(1), table.lead(1), before, other)
    return jnp.where(second, behind, state), jnp.where(second, other, before), own


def join_kernel(poles, taps, tokens, place_ref, own_ref, other_ref, table_ref, out_ref):
    fold = own_ref.shape[0] // (poles + 6 * (taps - 1))
    table = Table(table_ref, poles, taps, fold, tokens)
    own, other = table.message(own_ref[...]), table.message(other_ref[...])
    second = place_ref[0] == 1
    before, current = jnp.where(second, other, own), jnp.where(second, own, other)
    state = table.enter(before[:poles], table.span(1), table.lead(1), before, current)
    out = [state[r] for r in range(poles)]
    for group in range(3):
        out += table.first(before, group) + table.last(current, group)
    out_ref[...] = jnp.concatenate(out, axis=0).astype(BF16)


def join_part(place, own, other, table, tokens, poles, taps):
    return pl.pallas_call(
        functools.partial(join_kernel, poles, taps, tokens),
        out_shape=jax.ShapeDtypeStruct(own.shape, BF16),
        in_specs=[SMEM] + [VMEM] * 3,
        out_specs=VMEM,
        compiler_params=params(),
        cost_estimate=cost(1 << 20, 1 << 18),
        name="join_state",
    )(place.reshape(1).astype(jnp.int32), own, other, table)


def far_kernel(poles, taps, count, enter, place_ref, near_ref, q_ref, table_ref, *refs):
    message_refs, (out_ref, conv_s) = refs[:count], refs[count:]
    tokens, channels = near_ref.shape
    fold = channels // LANES
    table = Table(table_ref, poles, taps, fold, tokens)
    edge = table.edge
    state, before, current = enter(table, place_ref, *message_refs)
    decay = [jnp.exp(-table.rates[r]) for r in range(poles)]
    modes = tuple(state[r] for r in range(poles))
    for t, value in enumerate(table.signals(before, current)):
        modes = tuple(decay[r] * modes[r] + table.residues[r] * value for r in range(poles))
        conv_s[t * fold : (t + 1) * fold, :] = tree_sum(modes + (table.skip * value,))

    def step(t, modes):
        modes = tuple(d * m for d, m in zip(decay, modes))
        conv_s[pl.ds(pl.multiple_of(t * fold, fold), fold), :] = tree_sum(modes)
        return modes

    lax.fori_loop(edge, tokens, step, modes, unroll=6)
    row_id = lax.broadcasted_iota(jnp.int32, (tokens, LANES), 0)
    halo = table.last(before, 0)
    for j in range(fold):
        lanes = slice(j * LANES, (j + 1) * LANES)
        value = q_ref[:, lanes].astype(F32)
        gate = None
        for shift in range(taps):
            moved = value if shift == 0 else pltpu.roll(value, shift, axis=0)
            for t in range(shift):
                moved = jnp.where(row_id == t, halo[edge - shift + t][j : j + 1, :], moved)
            row = table.tap_base + shift * fold + j
            term = table_ref[row : row + 1, :] * moved
            gate = term if gate is None else gate + term
        conv = conv_s[pl.ds(j, tokens, stride=fold), :]
        out_ref[:, lanes] = (near_ref[:, lanes].astype(F32) + gate * conv).astype(BF16)


def far_part(enter, place, near, q, table, messages, poles, taps):
    tokens, channels = near.shape
    fold = channels // LANES
    count = len(messages)
    return pl.pallas_call(
        functools.partial(far_kernel, poles, taps, count, enter),
        out_shape=jax.ShapeDtypeStruct((tokens, channels), BF16),
        in_specs=[SMEM] + [VMEM] * (3 + count),
        out_specs=VMEM,
        scratch_shapes=[pltpu.VMEM((tokens * fold, LANES), F32)],
        compiler_params=params(),
        cost_estimate=cost(4 * tokens * channels * poles, 3 << 20),
        name="far_filter",
    )(place.reshape(1).astype(jnp.int32), near, q, table, *messages)


def project_kernel(count, place_ref, *refs):
    rows_refs, (own_ref, other_ref, out_ref) = refs[:count], refs[count:]
    y, first = place_ref[0], place_ref[1]
    for i, rows_ref in enumerate(rows_refs):
        for half, ref in ((y, own_ref), (1 - y, other_ref)):
            part = lax.dot_general(
                rows_ref[...], ref[...], (((1,), (1,)), ((), ())), preferred_element_type=F32
            )
            out_ref[(first ^ i) if count > 1 else 0, half] = part.astype(BF16)


def project_part(place, rows, own, other):
    tokens, channels = rows[0].shape
    width = own.shape[0]
    count = len(rows)
    return pl.pallas_call(
        functools.partial(project_kernel, count),
        out_shape=jax.ShapeDtypeStruct((count, 2, tokens, width), BF16),
        in_specs=[SMEM] + [VMEM] * (2 + count),
        out_specs=VMEM,
        compiler_params=params(),
        cost_estimate=cost(4 * count * tokens * channels * width, 3 << 20),
        name="project",
    )(place, *rows, own, other)


def finish_kernel(place_ref, *refs):
    out_ref = refs[-1]
    width = refs[0].shape[2]
    for pair in range((len(refs) - 1) // 2):

        @pl.when(place_ref[0] == pair)
        def _(pair=pair):
            for h in range(2):
                total = refs[2 * pair][h].astype(F32) + refs[2 * pair + 1][h].astype(F32)
                out_ref[:, h * width : (h + 1) * width] = total.astype(BF16)


def permute(x, move, keep=None):
    pairs = []
    for index in range(32):
        place = (index // 8, index // 4 % 2, index // 2 % 2, index % 2)
        if keep is None or keep(*place):
            z, y, x_, c = move(*place)
            pairs.append((index, ((z * 2 + y) * 2 + x_) * 2 + c))
    return lax.ppermute(x, AXES, pairs)


def over_y(z, y, x, c):
    return z, 1 - y, x, c


def over_z0(z, y, x, c):
    return z ^ 1, y, x, c


def over_z1(z, y, x, c):
    return z ^ 2, y, x, c


def over_core(z, y, x, c):
    return z, y, x, 1 - c


def after(x, *others):
    return lax.optimization_barrier((x,) + others)[0]


def per_device_32(features, short_taps, rates, residues, skip, out_weight):
    tokens, _, channels = features.shape
    poles, taps = rates.shape[1], short_taps.shape[1]
    seq, tp = lax.axis_index("seq"), lax.axis_index("tp")
    z, y = seq // 2, seq % 2
    near, message, table = local_part(features, short_taps, rates, residues, skip)
    message_y = permute(message, over_y)
    w_y = permute(after(out_weight, message_y), over_y)
    pair = join_part(y, message, message_y, table, tokens, poles, taps)
    pair_z = permute(pair, lambda z, y, x, c: (z + 1, y, x, c), lambda z, y, x, c: z + 1 < 4)
    four = join_part(jnp.ones((), jnp.int32), pair, pair_z, table, 2 * tokens, poles, taps)
    four_z = permute(four, lambda z, y, x, c: (z + 2, y, x, c), lambda z, y, x, c: z + 2 < 4)
    enter = functools.partial(enter_joined, (2, 4))
    gated = far_part(
        enter, y, near, features[:, 0], table, [message, message_y, pair_z, four_z], poles, taps
    )
    two = permute(gated, over_z1)
    one = permute(gated, over_z0)
    three = permute(two, over_z0)
    odd = (z ^ tp) % 2
    place = jnp.stack([y, odd]).astype(jnp.int32)

    def odd_of(z, y, x, c):
        return (z ^ c) % 2

    def home(summed, far):
        def move(z, y, x, c):
            return z ^ far ^ odd_of(z, y, x, c), y, z // 2, z % 2

        return [
            permute(summed, move, lambda z, y, x, c: x != z // 2),
            permute(summed, move, lambda z, y, x, c: x == z // 2),
        ]

    parts = []
    for far, rows in ((0, [gated, one]), (2, [two, three])):
        kept, sent = project_part(place, rows, out_weight, w_y)
        from_core = permute(sent, over_core)
        parts += home((kept.astype(F32) + from_core.astype(F32)).astype(BF16), far)
    kind = (z ^ tp) // 2
    return pl.pallas_call(
        finish_kernel,
        out_shape=jax.ShapeDtypeStruct((tokens, 2 * out_weight.shape[0]), BF16),
        in_specs=[SMEM] + [VMEM] * len(parts),
        out_specs=VMEM,
        compiler_params=params(),
        cost_estimate=cost(4 * tokens * out_weight.shape[0], 2 << 20),
        name="finish",
    )(kind.reshape(1).astype(jnp.int32), *parts)


def per_device(features, short_taps, rates, residues, skip, out_weight):
    poles, taps = rates.shape[1], short_taps.shape[1]
    near, message, table = local_part(features, short_taps, rates, residues, skip)
    messages = lax.all_gather(message, "seq")
    place, q = lax.axis_index("seq"), features[:, 0]
    gated = far_part(enter_any, place, near, q, table, [messages], poles, taps)
    partial = lax.dot_general(
        gated,
        lax.all_gather(out_weight, "seq", axis=0, tiled=True),
        (((1,), (1,)), ((), ())),
        preferred_element_type=F32,
    )
    return lax.psum_scatter(partial.astype(BF16), "tp", scatter_dimension=1, tiled=True)


def solution(mesh):
    in_specs = (
        P("seq", None, "tp"),
        P(None, None, "tp"),
        P("tp", None),
        P("tp", None),
        P("tp"),
        P("seq", "tp"),
    )
    out_specs = P("seq", "tp")
    body = per_device_32 if (mesh.shape["seq"], mesh.shape["tp"]) == (8, 4) else per_device
    return jax.shard_map(body, mesh=mesh, in_specs=in_specs, out_specs=out_specs, check_vma=False)
```

time: 86 us -> 70.6 us (0.82)
  the two profiles are of different devices: /device:TPU:0 before, /device:TPU:1 now
where the time goes in v2:
time: 70.6 us; the launch traced here: 70.4 us
  starting transfers between devices  31.3 us (44%)
  waiting for transfers between devices  28.5 us (40%)
  Pallas kernels  8.22 us (12%)
  local copies, waits for them, and re-layouts  1.97 us (3%)
    ppermute x13, starting transfers between devices, permute(): return lax.ppermute(x, AXES, pairs)  31.3 us
    ppermute x13, waiting for transfers between devices, permute(): return lax.ppermute(x, AXES, pairs)  28.5 us
    pallas_call x2, Pallas kernels, project_part(): pl.pallas_call(functools.partial(project_kernel, count), out_shape=jax.Sh...  4.1 us
    pallas_call x1, Pallas kernels, local_part(): pl.pallas_call(local_kernel, out_shape=(jax.ShapeDtypeStruct((tokens, cha...  2.19 us
  transfers between devices with their start and end apart: 13, of which 7 were waited for; matrix products, arithmetic and copies ran while one was open for 0% of the time, Pallas kernels for 7%

profile of v2, /device:TPU:1, one launch (start us, length us, event | category | flops | bytes accessed | tf_op | source)
XLA Modules:
  0.0 70.4 jit_solution(2897489291596763991)
XLA Ops:
  0.0 0.0 copy-start.2
  0.0 0.0 copy-start.1
  0.0 0.0 copy-start.3
  0.0 0.0 copy-start
  0.0 1.3 %slice_bitcast_fusion.4 = (bf16[128,1024]{1,0:T(8,128)(2,1)S(1)}, bf16[128,1024]{1,0:T(8,128)(2,1)S(1)}, bf16[128,1024]{1,0:T(8,128)(2,1)S(1)}) fusion(bf16[128,3,1024]{2,0,1:T(8,128)(2,1)} %param.6), kind=kLoop, calls=%fused_computation.8 | loop fusion | bytes 1572864 | tf_op jit(solution)/shard_map/squeeze | solution.py:117
  1.3 0.0 copy-start.4
  1.3 0.0 copy-done.2
  1.3 0.0 copy-done.1
  1.3 0.0 copy-done.3
  1.3 0.6 copy-done.4
  2.0 2.2 %local_filter.1 = (bf16[128,1024]{1,0:T(8,128)(2,1)S(1)}, bf16[224,128]{1,0:T(8,128)(2,1)S(1)}, f32[336,128]{1,0:T(8,128)S(1)}) custom-call(bf16[128,1024]{1,0:T(8,128)(2,1)S(1)} %get-tuple-element.14.q_ref, bf16[128,1024]{1,0:T(8,128)(2,1)S(1)} %get-tuple-element.15.k_ref, bf16[128,1024]{1,0:T(8,128)(2,1)S(1)} %get-tuple-element.13.v_ref, ...), custom_call_target="tpu_custom_call" | custom-call | flops 8388608 | bytes 3145728 | tf_op jit(solution)/shard_map/local_filter/pallas_call | solution.py:98
  4.2 2.1 %collective-permute-start = (bf16[224,128]{1,0:T(8,128)(2,1)S(1)}, bf16[224,128]{1,0:T(8,128)(2,1)S(1)}, u32[]{:S(2)}, u32[]{:S(2)}) collective-permute-start(bf16[224,128]{1,0:T(8,128)(2,1)S(1)} %get-tuple-element.11.own_ref.refs_0_), channel_id=1, source_target_pairs={{0,4},{1,5},{2,6},{3,7},{4,0},{5,1},{6,2},{7,3},{8,12},{9,13},{10,... | collective-permute-start | bytes 172040 | tf_op jit(solution)/shard_map/ppermute | solution.py:323
  6.3 1.6 %collective-permute-done.other_ref.refs_1_ = bf16[224,128]{1,0:T(8,128)(2,1)S(1)} collective-permute-done((bf16[224,128]{1,0:T(8,128)(2,1)S(1)}, bf16[224,128]{1,0:T(8,128)(2,1)S(1)}, u32[]{:S(2)}, u32[]{:S(2)}) %collective-permute-start) | collective-permute-done | bytes 57376 | tf_op jit(solution)/shard_map/ppermute | solution.py:323
  7.9 0.0 copy-done
  7.9 1.5 %collective-permute-start.4 = (bf16[512,1024]{1,0:T(8,128)(2,1)S(1)}, bf16[512,1024]{1,0:T(8,128)(2,1)S(1)}, u32[]{:S(2)}, u32[]{:S(2)}) collective-permute-start(bf16[512,1024]{1,0:T(8,128)(2,1)S(1)} %copy-done), channel_id=1, source_target_pairs={{0,4},{1,5},{2,6},{3,7},{4,0},{5,1},{6,2},{7,3},{8,12},{9,13},{10,... | collective-permute-start | bytes 3145736 | tf_op jit(solution)/shard_map/ppermute | solution.py:323
  9.3 0.1 join_state.2.own_ref
  9.4 3.2 %collective-permute-start.1 = (bf16[224,128]{1,0:T(8,128)(2,1)S(1)}, bf16[224,128]{1,0:T(8,128)(2,1)S(1)}, u32[]{:S(2)}, u32[]{:S(2)}) collective-permute-start(bf16[224,128]{1,0:T(8,128)(2,1)S(1)} %join_state.2.own_ref), channel_id=1, source_target_pairs={{0,8},{1,9},{2,10},{3,11},{4,12},{5,13},{6,14},{7,15},{8,16},{9,17... | collective-permute-start | bytes 172040 | tf_op jit(solution)/shard_map/ppermute | solution.py:323
  12.6 1.2 %collective-permute-done.1.other_ref.refs_2_ = bf16[224,128]{1,0:T(8,128)(2,1)S(1)} collective-permute-done((bf16[224,128]{1,0:T(8,128)(2,1)S(1)}, bf16[224,128]{1,0:T(8,128)(2,1)S(1)}, u32[]{:S(2)}, u32[]{:S(2)}) %collective-permute-start.1) | collective-permute-done | bytes 57376 | tf_op jit(solution)/shard_map/ppermute | solution.py:323
  13.9 0.1 join_state.3
  13.9 5.0 %collective-permute-start.2 = (bf16[224,128]{1,0:T(8,128)(2,1)S(1)}, bf16[224,128]{1,0:T(8,128)(2,1)S(1)}, u32[]{:S(2)}, u32[]{:S(2)}) collective-permute-start(bf16[224,128]{1,0:T(8,128)(2,1)S(1)} %join_state.3), channel_id=1, source_target_pairs={{0,16},{1,17},{2,18},{3,19},{4,20},{5,21},{6,22},{7,23},{8,24},{9,... | collective-permute-start | bytes 172040 | tf_op jit(solution)/shard_map/ppermute | solution.py:323
  18.9 1.2 %collective-permute-done.2.refs_3_ = bf16[224,128]{1,0:T(8,128)(2,1)S(1)} collective-permute-done((bf16[224,128]{1,0:T(8,128)(2,1)S(1)}, bf16[224,128]{1,0:T(8,128)(2,1)S(1)}, u32[]{:S(2)}, u32[]{:S(2)}) %collective-permute-start.2) | collective-permute-done | bytes 57376 | tf_op jit(solution)/shard_map/ppermute | solution.py:323
  20.2 1.0 %far_filter.1.refs_0_ = bf16[128,1024]{1,0:T(8,128)(2,1)S(1)} custom-call(s32[1]{0:T(128)} %bitcast.1.place_ref, bf16[128,1024]{1,0:T(8,128)(2,1)S(1)} %get-tuple-element.9.near_ref, bf16[128,1024]{1,0:T(8,128)(2,1)S(1)} %get-tuple-element.14.q_ref, f32[336,128]{1,0:T(8,128)S(1)} %get-tuple-element.10.table_ref, ...), custom_call_target="tpu_custom_call" | custom-call | flops 8388608 | bytes 3145728 | tf_op jit(solution)/shard_map/far_filter/pallas_call | solution.py:266
  21.2 2.8 %collective-permute-start.8 = (bf16[128,1024]{1,0:T(8,128)(2,1)S(1)}, bf16[128,1024]{1,0:T(8,128)(2,1)S(1)}, u32[]{:S(2)}, u32[]{:S(2)}) collective-permute-start(bf16[128,1024]{1,0:T(8,128)(2,1)S(1)} %far_filter.1.refs_0_), channel_id=1, source_target_pairs={{0,16},{1,17},{2,18},{3,19},{4,20},{5,21},{6,22},{7,23},{8,24},{9,... | collective-permute-start | bytes 786440 | tf_op jit(solution)/shard_map/ppermute | solution.py:323
  24.0 10.9 %collective-permute-done.8.refs_0_ = bf16[128,1024]{1,0:T(8,128)(2,1)S(1)} collective-permute-done((bf16[128,1024]{1,0:T(8,128)(2,1)S(1)}, bf16[128,1024]{1,0:T(8,128)(2,1)S(1)}, u32[]{:S(2)}, u32[]{:S(2)}) %collective-permute-start.8) | collective-permute-done | bytes 262176 | tf_op jit(solution)/shard_map/ppermute | solution.py:323
  34.8 0.1 collective-permute-start.9
  35.0 0.1 pad_add_fusion.place_ref
  35.0 1.3 %collective-permute-start.3 = (bf16[128,1024]{1,0:T(8,128)(2,1)S(1)}, bf16[128,1024]{1,0:T(8,128)(2,1)S(1)}, u32[]{:S(2)}, u32[]{:S(2)}) collective-permute-start(bf16[128,1024]{1,0:T(8,128)(2,1)S(1)} %far_filter.1.refs_0_), channel_id=1, source_target_pairs={{0,8},{1,9},{2,10},{3,11},{4,12},{5,13},{6,14},{7,15},{8,0},{9,1},... | collective-permute-start | bytes 786440 | tf_op jit(solution)/shard_map/ppermute | solution.py:323
  36.4 4.2 %collective-permute-done.9.refs_1_ = bf16[128,1024]{1,0:T(8,128)(2,1)S(1)} collective-permute-done((bf16[128,1024]{1,0:T(8,128)(2,1)S(1)}, bf16[128,1024]{1,0:T(8,128)(2,1)S(1)}, u32[]{:S(2)}, u32[]{:S(2)}) %collective-permute-start.9) | collective-permute-done | bytes 262176 | tf_op jit(solution)/shard_map/ppermute | solution.py:323
  40.6 0.0 collective-permute-done.4.refs_3_
  40.6 2.0 %project.3 = bf16[2,2,128,512]{3,2,1,0:T(8,128)(2,1)S(1)} custom-call(s32[2]{0:T(128)S(1)} %pad_add_fusion.place_ref, bf16[128,1024]{1,0:T(8,128)(2,1)S(1)} %collective-permute-done.8.refs_0_, bf16[128,1024]{1,0:T(8,128)(2,1)S(1)} %collective-permute-done.9.refs_1_, bf16[512,1024]{1,0:T(8,128)(2,1)S(1)} %copy-done, ...), custom_call_target="tpu_custom_call" | custom-call | flops 536870912 | bytes 3145728 | tf_op jit(solution)/shard_map/project/pallas_call | solution.py:293
  42.7 5.6 %collective-permute-start.10 = (bf16[2,128,512]{2,1,0:T(8,128)(2,1)S(1)}, bf16[2,128,512]{2,1,0:T(8,128)(2,1)S(1)}, u32[]{:S(2)}, u32[]{:S(2)}) collective-permute-start(bf16[2,128,512]{2,1,0:T(8,128)(2,1)S(1)} %slice_bitcast_fusion), channel_id=1, source_target_pairs={{0,1},{1,0},{2,3},{3,2},{4,5},{5,4},{6,7},{7,6},{8,9},{9,8},{10,11... | collective-permute-start | bytes 786440 | tf_op jit(solution)/shard_map/ppermute | solution.py:323
  48.2 0.0 collective-permute-done.3.refs_1_
  48.2 2.1 %project.2 = bf16[2,2,128,512]{3,2,1,0:T(8,128)(2,1)S(1)} custom-call(s32[2]{0:T(128)S(1)} %pad_add_fusion.place_ref, bf16[128,1024]{1,0:T(8,128)(2,1)S(1)} %far_filter.1.refs_0_, bf16[128,1024]{1,0:T(8,128)(2,1)S(1)} %collective-permute-done.3.refs_1_, bf16[512,1024]{1,0:T(8,128)(2,1)S(1)} %copy-done, bf16[512,1024]{1,0:T(8,128)(2,1)S(1)} %collective-permute-done.4.refs_3_), custom_call_target="tpu_custom_call" | custom-call | flops 536870912 | bytes 3145728 | tf_op jit(solution)/shard_map/project/pallas_call | solution.py:293
  50.3 1.0 %collective-permute-start.5 = (bf16[2,128,512]{2,1,0:T(8,128)(2,1)S(1)}, bf16[2,128,512]{2,1,0:T(8,128)(2,1)S(1)}, u32[]{:S(2)}, u32[]{:S(2)}) collective-permute-start(bf16[2,128,512]{2,1,0:T(8,128)(2,1)S(1)} %slice_bitcast_fusion.2), channel_id=1, source_target_pairs={{0,1},{1,0},{2,3},{3,2},{4,5},{5,4},{6,7},{7,6},{8,9},{9,8},{10,11... | collective-permute-start | bytes 786440 | tf_op jit(solution)/shard_map/ppermute | solution.py:323
  51.3 0.0 collective-permute-done.10
  51.3 0.1 fusion
  51.4 4.8 %collective-permute-start.12 = (bf16[2,128,512]{2,1,0:T(8,128)(2,1)S(1)}, bf16[2,128,512]{2,1,0:T(8,128)(2,1)S(1)}, u32[]{:S(2)}, u32[]{:S(2)}) collective-permute-start(bf16[2,128,512]{2,1,0:T(8,128)(2,1)S(1)} %fusion), channel_id=1, source_target_pairs={{0,16},{1,24},{4,20},{5,28},{8,17},{9,25},{12,21},{13,29},{18,2},{... | collective-permute-start | bytes 786440 | tf_op jit(solution)/shard_map/ppermute | solution.py:323
  56.2 0.7 collective-permute-start.11
  56.9 0.0 collective-permute-done.5
  56.9 0.1 fusion.1
  57.0 1.9 %collective-permute-start.7 = (bf16[2,128,512]{2,1,0:T(8,128)(2,1)S(1)}, bf16[2,128,512]{2,1,0:T(8,128)(2,1)S(1)}, u32[]{:S(2)}, u32[]{:S(2)}) collective-permute-start(bf16[2,128,512]{2,1,0:T(8,128)(2,1)S(1)} %fusion.1), channel_id=1, source_target_pairs={{0,0},{1,8},{4,4},{5,12},{8,1},{9,9},{12,5},{13,13},{18,18},{19,26... | collective-permute-start | bytes 786440 | tf_op jit(solution)/shard_map/ppermute | solution.py:323
  58.9 1.3 %collective-permute-start.6 = (bf16[2,128,512]{2,1,0:T(8,128)(2,1)S(1)}, bf16[2,128,512]{2,1,0:T(8,128)(2,1)S(1)}, u32[]{:S(2)}, u32[]{:S(2)}) collective-permute-start(bf16[2,128,512]{2,1,0:T(8,128)(2,1)S(1)} %fusion.1), channel_id=1, source_target_pairs={{2,0},{3,8},{6,4},{7,12},{10,1},{11,9},{14,5},{15,13},{16,18},{17,... | collective-permute-start | bytes 786440 | tf_op jit(solution)/shard_map/ppermute | solution.py:323
  60.2 1.5 %collective-permute-done.12.refs_3_ = bf16[2,128,512]{2,1,0:T(8,128)(2,1)S(1)} collective-permute-done((bf16[2,128,512]{2,1,0:T(8,128)(2,1)S(1)}, bf16[2,128,512]{2,1,0:T(8,128)(2,1)S(1)}, u32[]{:S(2)}, u32[]{:S(2)}) %collective-permute-start.12) | collective-permute-done | bytes 262176 | tf_op jit(solution)/shard_map/ppermute | solution.py:323
  61.7 0.0 collective-permute-done.11.refs_2_
  61.7 7.8 %collective-permute-done.7.refs_1_ = bf16[2,128,512]{2,1,0:T(8,128)(2,1)S(1)} collective-permute-done((bf16[2,128,512]{2,1,0:T(8,128)(2,1)S(1)}, bf16[2,128,512]{2,1,0:T(8,128)(2,1)S(1)}, u32[]{:S(2)}, u32[]{:S(2)}) %collective-permute-start.7) | collective-permute-done | bytes 262176 | tf_op jit(solution)/shard_map/ppermute | solution.py:323
  69.6 0.0 collective-permute-done.6.refs_0_
  69.6 0.8 %finish.1 = bf16[128,1024]{1,0:T(8,128)(2,1)} custom-call(s32[1]{0:T(128)} %bitcast.place_ref, bf16[2,128,512]{2,1,0:T(8,128)(2,1)S(1)} %collective-permute-done.6.refs_0_, bf16[2,128,512]{2,1,0:T(8,128)(2,1)S(1)} %collective-permute-done.7.refs_1_, bf16[2,128,512]{2,1,0:T(8,128)(2,1)S(1)} %collective-permute-done.11.refs_2_, ...), custom_call_target="tpu_custom_call" | custom-call | flops 262144 | bytes 2097152 | tf_op jit(solution)/shard_map/finish/pallas_call | solution.py:386
  (2 shorter events, 0.0 us)
Async XLA Ops:
  0.0 1.3 %copy-start.2 = (f32[1024,16]{0,1:T(8,128)S(1)}, f32[1024,16]{0,1:T(8,128)}, u32[]{:S(2)}) copy-start(f32[1024,16]{0,1:T(8,128)} %param.9) | copy-start | bytes 196612
  0.0 1.3 %copy-start.1 = (f32[1024,16]{0,1:T(8,128)S(1)}, f32[1024,16]{0,1:T(8,128)}, u32[]{:S(2)}) copy-start(f32[1024,16]{0,1:T(8,128)} %param.8) | copy-start | bytes 196612
  0.0 1.3 %copy-start.3 = (bf16[3,3,1024]{2,1,0:T(4,128)(2,1)S(1)}, bf16[3,3,1024]{2,1,0:T(4,128)(2,1)}, u32[]{:S(2)}) copy-start(bf16[3,3,1024]{2,1,0:T(4,128)(2,1)} %taps_ref.1) | copy-start | bytes 55300
  0.0 7.9 %copy-start = (bf16[512,1024]{1,0:T(8,128)(2,1)S(1)}, bf16[512,1024]{1,0:T(8,128)(2,1)}, u32[]{:S(2)}) copy-start(bf16[512,1024]{1,0:T(8,128)(2,1)} %refs_2_.3) | copy-start | bytes 3145732
  1.3 0.7 copy-start.4
  4.2 3.7 %collective-permute-start = (bf16[224,128]{1,0:T(8,128)(2,1)S(1)}, bf16[224,128]{1,0:T(8,128)(2,1)S(1)}, u32[]{:S(2)}, u32[]{:S(2)}) collective-permute-start(bf16[224,128]{1,0:T(8,128)(2,1)S(1)} %get-tuple-element.11.own_ref.refs_0_), channel_id=1, source_target_pairs={{0,4},{1,5},{2,6},{3,7},{4,0},{5,1},{6,2},{7,3},{8,12},{9,13},{10,... | collective-permute-start | bytes 172040 | tf_op jit(solution)/shard_map/ppermute | solution.py:323
  7.9 32.7 %collective-permute-start.4 = (bf16[512,1024]{1,0:T(8,128)(2,1)S(1)}, bf16[512,1024]{1,0:T(8,128)(2,1)S(1)}, u32[]{:S(2)}, u32[]{:S(2)}) collective-permute-start(bf16[512,1024]{1,0:T(8,128)(2,1)S(1)} %copy-done), channel_id=1, source_target_pairs={{0,4},{1,5},{2,6},{3,7},{4,0},{5,1},{6,2},{7,3},{8,12},{9,13},{10,... | collective-permute-start | bytes 3145736 | tf_op jit(solution)/shard_map/ppermute | solution.py:323
  9.4 4.4 %collective-permute-start.1 = (bf16[224,128]{1,0:T(8,128)(2,1)S(1)}, bf16[224,128]{1,0:T(8,128)(2,1)S(1)}, u32[]{:S(2)}, u32[]{:S(2)}) collective-permute-start(bf16[224,128]{1,0:T(8,128)(2,1)S(1)} %join_state.2.own_ref), channel_id=1, source_target_pairs={{0,8},{1,9},{2,10},{3,11},{4,12},{5,13},{6,14},{7,15},{8,16},{9,17... | collective-permute-start | bytes 172040 | tf_op jit(solution)/shard_map/ppermute | solution.py:323
  13.9 6.2 %collective-permute-start.2 = (bf16[224,128]{1,0:T(8,128)(2,1)S(1)}, bf16[224,128]{1,0:T(8,128)(2,1)S(1)}, u32[]{:S(2)}, u32[]{:S(2)}) collective-permute-start(bf16[224,128]{1,0:T(8,128)(2,1)S(1)} %join_state.3), channel_id=1, source_target_pairs={{0,16},{1,17},{2,18},{3,19},{4,20},{5,21},{6,22},{7,23},{8,24},{9,... | collective-permute-start | bytes 172040 | tf_op jit(solution)/shard_map/ppermute | solution.py:323
  21.2 13.6 %collective-permute-start.8 = (bf16[128,1024]{1,0:T(8,128)(2,1)S(1)}, bf16[128,1024]{1,0:T(8,128)(2,1)S(1)}, u32[]{:S(2)}, u32[]{:S(2)}) collective-permute-start(bf16[128,1024]{1,0:T(8,128)(2,1)S(1)} %far_filter.1.refs_0_), channel_id=1, source_target_pairs={{0,16},{1,17},{2,18},{3,19},{4,20},{5,21},{6,22},{7,23},{8,24},{9,... | collective-permute-start | bytes 786440 | tf_op jit(solution)/shard_map/ppermute | solution.py:323
  34.8 5.8 %collective-permute-start.9 = (bf16[128,1024]{1,0:T(8,128)(2,1)S(1)}, bf16[128,1024]{1,0:T(8,128)(2,1)S(1)}, u32[]{:S(2)}, u32[]{:S(2)}) collective-permute-start(bf16[128,1024]{1,0:T(8,128)(2,1)S(1)} %collective-permute-done.8.refs_0_), channel_id=1, source_target_pairs={{0,8},{1,9},{2,10},{3,11},{4,12},{5,13},{6,14},{7,15},{8,0},{9,1},... | collective-permute-start | bytes 786440 | tf_op jit(solution)/shard_map/ppermute | solution.py:323
  35.0 13.2 %collective-permute-start.3 = (bf16[128,1024]{1,0:T(8,128)(2,1)S(1)}, bf16[128,1024]{1,0:T(8,128)(2,1)S(1)}, u32[]{:S(2)}, u32[]{:S(2)}) collective-permute-start(bf16[128,1024]{1,0:T(8,128)(2,1)S(1)} %far_filter.1.refs_0_), channel_id=1, source_target_pairs={{0,8},{1,9},{2,10},{3,11},{4,12},{5,13},{6,14},{7,15},{8,0},{9,1},... | collective-permute-start | bytes 786440 | tf_op jit(solution)/shard_map/ppermute | solution.py:323
  42.7 8.6 %collective-permute-start.10 = (bf16[2,128,512]{2,1,0:T(8,128)(2,1)S(1)}, bf16[2,128,512]{2,1,0:T(8,128)(2,1)S(1)}, u32[]{:S(2)}, u32[]{:S(2)}) collective-permute-start(bf16[2,128,512]{2,1,0:T(8,128)(2,1)S(1)} %slice_bitcast_fusion), channel_id=1, source_target_pairs={{0,1},{1,0},{2,3},{3,2},{4,5},{5,4},{6,7},{7,6},{8,9},{9,8},{10,11... | collective-permute-start | bytes 786440 | tf_op jit(solution)/shard_map/ppermute | solution.py:323
  50.3 6.5 %collective-permute-start.5 = (bf16[2,128,512]{2,1,0:T(8,128)(2,1)S(1)}, bf16[2,128,512]{2,1,0:T(8,128)(2,1)S(1)}, u32[]{:S(2)}, u32[]{:S(2)}) collective-permute-start(bf16[2,128,512]{2,1,0:T(8,128)(2,1)S(1)} %slice_bitcast_fusion.2), channel_id=1, source_target_pairs={{0,1},{1,0},{2,3},{3,2},{4,5},{5,4},{6,7},{7,6},{8,9},{9,8},{10,11... | collective-permute-start | bytes 786440 | tf_op jit(solution)/shard_map/ppermute | solution.py:323
  51.4 10.3 %collective-permute-start.12 = (bf16[2,128,512]{2,1,0:T(8,128)(2,1)S(1)}, bf16[2,128,512]{2,1,0:T(8,128)(2,1)S(1)}, u32[]{:S(2)}, u32[]{:S(2)}) collective-permute-start(bf16[2,128,512]{2,1,0:T(8,128)(2,1)S(1)} %fusion), channel_id=1, source_target_pairs={{0,16},{1,24},{4,20},{5,28},{8,17},{9,25},{12,21},{13,29},{18,2},{... | collective-permute-start | bytes 786440 | tf_op jit(solution)/shard_map/ppermute | solution.py:323
  56.2 5.5 %collective-permute-start.11 = (bf16[2,128,512]{2,1,0:T(8,128)(2,1)S(1)}, bf16[2,128,512]{2,1,0:T(8,128)(2,1)S(1)}, u32[]{:S(2)}, u32[]{:S(2)}) collective-permute-start(bf16[2,128,512]{2,1,0:T(8,128)(2,1)S(1)} %fusion), channel_id=1, source_target_pairs={{2,16},{3,24},{6,20},{7,28},{10,17},{11,25},{14,21},{15,29},{16,2}... | collective-permute-start | bytes 786440 | tf_op jit(solution)/shard_map/ppermute | solution.py:323
  57.0 12.6 %collective-permute-start.7 = (bf16[2,128,512]{2,1,0:T(8,128)(2,1)S(1)}, bf16[2,128,512]{2,1,0:T(8,128)(2,1)S(1)}, u32[]{:S(2)}, u32[]{:S(2)}) collective-permute-start(bf16[2,128,512]{2,1,0:T(8,128)(2,1)S(1)} %fusion.1), channel_id=1, source_target_pairs={{0,0},{1,8},{4,4},{5,12},{8,1},{9,9},{12,5},{13,13},{18,18},{19,26... | collective-permute-start | bytes 786440 | tf_op jit(solution)/shard_map/ppermute | solution.py:323
  58.9 10.7 %collective-permute-start.6 = (bf16[2,128,512]{2,1,0:T(8,128)(2,1)S(1)}, bf16[2,128,512]{2,1,0:T(8,128)(2,1)S(1)}, u32[]{:S(2)}, u32[]{:S(2)}) collective-permute-start(bf16[2,128,512]{2,1,0:T(8,128)(2,1)S(1)} %fusion.1), channel_id=1, source_target_pairs={{2,0},{3,8},{6,4},{7,12},{10,1},{11,9},{14,5},{15,13},{16,18},{17,... | collective-permute-start | bytes 786440 | tf_op jit(solution)/shard_map/ppermute | solution.py:323

commit v3 on v2

--- a/solution.py
+++ b/solution.py
@@ -20,23 +20,22 @@
 
 
 def params(**kw):
-    return pltpu.CompilerParams(vmem_limit_bytes=40 * 1024 * 1024, **kw)
+    return pltpu.CompilerParams(vmem_limit_bytes=16 * 1024 * 1024, **kw)
 
 
 def local_kernel(
-    q_ref, k_ref, v_ref, taps_ref, rates_ref, residues_ref, skip_ref,
-    out_ref, message_ref, table_ref,
-    signal_s, conv_s, gate_s, message_s,
+    skip_ref, q_ref, k_ref, v_ref, taps_ref, rates_ref, residues_ref,
+    out_ref, gate_ref, message_ref, table_ref,
+    signal_s, conv_s, message_s,
 ):
     tokens, channels = q_ref.shape
-    poles = rates_ref.shape[0]
-    taps = taps_ref.shape[1]
+    poles, taps = rates_ref.shape[0], taps_ref.shape[1]
     fold = channels // LANES
     edge = taps - 1
-    tap_base = 2 * poles * fold
-    skip_base = tap_base + 3 * taps * fold
+    tap_row = 2 * poles
+    skip_row = tap_row + 3 * taps
+    table_ref[skip_row * fold : (skip_row + 1) * fold, :] = skip_ref[...]
     later = lax.broadcasted_iota(jnp.int32, (tokens, LANES), 0) >= edge
-    table_ref[skip_base : skip_base + fold, :] = skip_ref[...]
     for j in range(fold):
         lanes = slice(j * LANES, (j + 1) * LANES)
         table_ref[pl.ds(j, poles, stride=fold), :] = rates_ref[:, lanes]
@@ -46,8 +45,8 @@
             value = ref[:, lanes].astype(F32)
             total = None
             for shift in range(taps):
+                row = (tap_row + group * taps + shift) * fold + j
                 tap = taps_ref[group, shift : shift + 1, lanes].astype(F32)
-                row = tap_base + (group * taps + shift) * fold + j
                 table_ref[row : row + 1, :] = tap
                 moved = value if shift == 0 else pltpu.roll(value, shift, axis=0)
                 total = tap * moved if total is None else total + tap * moved
@@ -56,12 +55,12 @@
                 source = place if place < edge else tokens - 2 * edge + place
                 row = (poles + group * 2 * edge + place) * fold + j
                 message_s[row : row + 1, :] = value[source : source + 1, :]
-        gate_s[:, lanes] = mixed[0]
+        gate_ref[:, lanes] = mixed[0]
         signal = jnp.where(later, mixed[1] * mixed[2], 0.0)
         signal_s[pl.ds(j, tokens, stride=fold), :] = signal
     decay = [jnp.exp(-table_ref[r * fold : (r + 1) * fold, :]) for r in range(poles)]
     residue = [table_ref[(poles + r) * fold : (poles + r + 1) * fold, :] for r in range(poles)]
-    skip = skip_ref[...]
+    skip = table_ref[skip_row * fold : (skip_row + 1) * fold, :]
 
     def step(t, modes):
         rows = pl.ds(pl.multiple_of(t * fold, fold), fold)
@@ -77,7 +76,7 @@
     for j in range(fold):
         lanes = slice(j * LANES, (j + 1) * LANES)
         conv = conv_s[pl.ds(j, tokens, stride=fold), :]
-        out_ref[:, lanes] = (gate_s[:, lanes] * conv).astype(BF16)
+        out_ref[:, lanes] = (gate_ref[:, lanes] * conv).astype(BF16)
 
 
 def tree_sum(values):
@@ -89,8 +88,8 @@
     return values[0]
 
 
-def local_part(features, short_taps, rates, residues, skip):
-    tokens, _, channels = features.shape
+def local_part(q, k, v, short_taps, rates, residues, skip):
+    tokens, channels = q.shape
     poles, taps = rates.shape[1], short_taps.shape[1]
     fold = channels // LANES
     message_rows = (poles + 6 * (taps - 1)) * fold
@@ -99,28 +98,25 @@
         local_kernel,
         out_shape=(
             jax.ShapeDtypeStruct((tokens, channels), BF16),
+            jax.ShapeDtypeStruct((tokens, channels), F32),
             jax.ShapeDtypeStruct((message_rows, LANES), BF16),
             jax.ShapeDtypeStruct((table_rows, LANES), F32),
         ),
         in_specs=[VMEM] * 7,
-        out_specs=(VMEM,) * 3,
+        out_specs=(VMEM,) * 4,
         scratch_shapes=[
             pltpu.VMEM((tokens * fold, LANES), F32),
             pltpu.VMEM((tokens * fold, LANES), F32),
-            pltpu.VMEM((tokens, channels), F32),
             pltpu.VMEM((message_rows, LANES), F32),
         ],
         compiler_params=params(),
         cost_estimate=cost(4 * tokens * channels * poles, 3 << 20),
         name="local_filter",
-    )(
-        features[:, 0], features[:, 1], features[:, 2],
-        short_taps, rates.T, residues.T, skip.reshape(fold, LANES),
-    )
+    )(skip.reshape(fold, LANES), q, k, v, short_taps, rates.T, residues.T)
 
 
 class Table:
-    def __init__(self, ref, poles, taps, fold, tokens):
+    def __init__(self, ref, poles, taps, fold, tokens, weights=None):
         self.ref, self.poles, self.taps, self.fold, self.edge = ref, poles, taps, fold, taps - 1
         self.rates = ref[0 : poles * fold, :].reshape(poles, fold, LANES)
         self.residues = ref[poles * fold : 2 * poles * fold, :].reshape(poles, fold, LANES)
@@ -128,8 +124,11 @@
         skip_base = self.tap_base + 3 * taps * fold
         self.skip = ref[skip_base : skip_base + fold, :]
         self.tokens = tokens
+        self.weights = weights
 
     def span(self, shards):
+        if self.weights is not None:
+            return self.weights[shards.bit_length() - 1, 0]
         return jnp.exp(-self.rates * float(shards * self.tokens))
 
     def tap(self, group, shift):
@@ -159,6 +158,8 @@
         return [k * v for k, v in pairs]
 
     def lead(self, shards):
+        if self.weights is not None:
+            return [self.weights[shards.bit_length() - 1, 1 + i] for i in range(self.edge)]
         last = shards * self.tokens - 1
         return [jnp.exp(-self.rates * float(last - i)) * self.residues for i in range(self.edge)]
 
@@ -223,11 +224,31 @@
     )(place.reshape(1).astype(jnp.int32), own, other, table)
 
 
-def far_kernel(poles, taps, count, enter, place_ref, near_ref, q_ref, table_ref, *refs):
-    message_refs, (out_ref, conv_s) = refs[:count], refs[count:]
+def weights_kernel(poles, taps, tokens, table_ref, out_ref):
+    fold = out_ref.shape[3]
+    table = Table(table_ref, poles, taps, fold, tokens)
+    for i in range(out_ref.shape[0]):
+        for j, weight in enumerate([table.span(1 << i)] + table.lead(1 << i)):
+            out_ref[i, j] = weight
+
+
+def weights_part(table, tokens, poles, taps, fold):
+    return pl.pallas_call(
+        functools.partial(weights_kernel, poles, taps, tokens),
+        out_shape=jax.ShapeDtypeStruct((3, taps, poles, fold, LANES), F32),
+        in_specs=[VMEM],
+        out_specs=VMEM,
+        compiler_params=params(),
+        cost_estimate=cost(1 << 20, 1 << 20),
+        name="state_weights",
+    )(table)
+
+
+def far_kernel(poles, taps, count, enter, place_ref, near_ref, gate_ref, table_ref, *refs):
+    message_refs, weights_refs, (out_ref, conv_s) = refs[:count], refs[count:-2], refs[-2:]
     tokens, channels = near_ref.shape
     fold = channels // LANES
-    table = Table(table_ref, poles, taps, fold, tokens)
+    table = Table(table_ref, poles, taps, fold, tokens, *weights_refs)
     edge = table.edge
     state, before, current = enter(table, place_ref, *message_refs)
     decay = [jnp.exp(-table.rates[r]) for r in range(poles)]
@@ -243,55 +264,53 @@
 
     lax.fori_loop(edge, tokens, step, modes, unroll=6)
     row_id = lax.broadcasted_iota(jnp.int32, (tokens, LANES), 0)
-    halo = table.last(before, 0)
+    first = table.mixed(before, current, 0)
     for j in range(fold):
         lanes = slice(j * LANES, (j + 1) * LANES)
-        value = q_ref[:, lanes].astype(F32)
-        gate = None
-        for shift in range(taps):
-            moved = value if shift == 0 else pltpu.roll(value, shift, axis=0)
-            for t in range(shift):
-                moved = jnp.where(row_id == t, halo[edge - shift + t][j : j + 1, :], moved)
-            row = table.tap_base + shift * fold + j
-            term = table_ref[row : row + 1, :] * moved
-            gate = term if gate is None else gate + term
+        gate = gate_ref[:, lanes]
+        for t in range(edge):
+            gate = jnp.where(row_id == t, first[t][j : j + 1, :], gate)
         conv = conv_s[pl.ds(j, tokens, stride=fold), :]
         out_ref[:, lanes] = (near_ref[:, lanes].astype(F32) + gate * conv).astype(BF16)
 
 
-def far_part(enter, place, near, q, table, messages, poles, taps):
+def far_part(enter, place, near, gate, table, messages, poles, taps, weights=()):
     tokens, channels = near.shape
     fold = channels // LANES
     count = len(messages)
     return pl.pallas_call(
         functools.partial(far_kernel, poles, taps, count, enter),
         out_shape=jax.ShapeDtypeStruct((tokens, channels), BF16),
-        in_specs=[SMEM] + [VMEM] * (3 + count),
+        in_specs=[SMEM] + [VMEM] * (3 + count + len(weights)),
         out_specs=VMEM,
         scratch_shapes=[pltpu.VMEM((tokens * fold, LANES), F32)],
         compiler_params=params(),
         cost_estimate=cost(4 * tokens * channels * poles, 3 << 20),
         name="far_filter",
-    )(place.reshape(1).astype(jnp.int32), near, q, table, *messages)
-
-
-def project_kernel(count, place_ref, *refs):
-    rows_refs, (own_ref, other_ref, out_ref) = refs[:count], refs[count:]
+    )(place.reshape(1).astype(jnp.int32), near, gate, table, *messages, *weights)
+
+
+def project_kernel(given, place_ref, *refs):
+    *rows_refs, own_ref, other_ref, out_ref = refs
     y, first = place_ref[0], place_ref[1]
     for i, rows_ref in enumerate(rows_refs):
+        place = (first ^ i) if len(rows_refs) > 1 else 0
+        if given and i == 0:
+            out_ref[place] = rows_ref[0]
+            continue
         for half, ref in ((y, own_ref), (1 - y, other_ref)):
             part = lax.dot_general(
                 rows_ref[...], ref[...], (((1,), (1,)), ((), ())), preferred_element_type=F32
             )
-            out_ref[(first ^ i) if count > 1 else 0, half] = part.astype(BF16)
-
-
-def project_part(place, rows, own, other):
-    tokens, channels = rows[0].shape
+            out_ref[place, half] = part.astype(BF16)
+
+
+def project_part(place, rows, own, other, given=False):
+    tokens, channels = rows[-1].shape
     width = own.shape[0]
     count = len(rows)
     return pl.pallas_call(
-        functools.partial(project_kernel, count),
+        functools.partial(project_kernel, given),
         out_shape=jax.ShapeDtypeStruct((count, 2, tokens, width), BF16),
         in_specs=[SMEM] + [VMEM] * (2 + count),
         out_specs=VMEM,
@@ -313,14 +332,15 @@
                 out_ref[:, h * width : (h + 1) * width] = total.astype(BF16)
 
 
-def permute(x, move, keep=None):
+def permute(name, x, move, keep=None):
     pairs = []
     for index in range(32):
         place = (index // 8, index // 4 % 2, index // 2 % 2, index % 2)
         if keep is None or keep(*place):
             z, y, x_, c = move(*place)
             pairs.append((index, ((z * 2 + y) * 2 + x_) * 2 + c))
-    return lax.ppermute(x, AXES, pairs)
+    with jax.named_scope(name):
+        return lax.ppermute(x, AXES, pairs)
 
 
 def over_y(z, y, x, c):
@@ -345,24 +365,25 @@
 
 def per_device_32(features, short_taps, rates, residues, skip, out_weight):
     tokens, _, channels = features.shape
+    q, k, v = (features[:, group] for group in range(3))
     poles, taps = rates.shape[1], short_taps.shape[1]
     seq, tp = lax.axis_index("seq"), lax.axis_index("tp")
-    z, y = seq // 2, seq % 2
-    near, message, table = local_part(features, short_taps, rates, residues, skip)
-    message_y = permute(message, over_y)
-    w_y = permute(after(out_weight, message_y), over_y)
+    z, y = seq >> 1, seq & 1
+    near, gate, message, table = local_part(q, k, v, short_taps, rates, residues, skip)
+    message_y = permute("state_y", message, over_y)
     pair = join_part(y, message, message_y, table, tokens, poles, taps)
-    pair_z = permute(pair, lambda z, y, x, c: (z + 1, y, x, c), lambda z, y, x, c: z + 1 < 4)
+    weights = weights_part(after(table, pair), tokens, poles, taps, channels // LANES)
+    w_y = permute("weights", after(out_weight, weights), over_y)
+    pair_z = permute("state_z1", pair, lambda z, y, x, c: (z + 1, y, x, c), lambda z, y, x, c: z + 1 < 4)
     four = join_part(jnp.ones((), jnp.int32), pair, pair_z, table, 2 * tokens, poles, taps)
-    four_z = permute(four, lambda z, y, x, c: (z + 2, y, x, c), lambda z, y, x, c: z + 2 < 4)
+    four_z = permute("state_z2", four, lambda z, y, x, c: (z + 2, y, x, c), lambda z, y, x, c: z + 2 < 4)
     enter = functools.partial(enter_joined, (2, 4))
-    gated = far_part(
-        enter, y, near, features[:, 0], table, [message, message_y, pair_z, four_z], poles, taps
-    )
-    two = permute(gated, over_z1)
-    one = permute(gated, over_z0)
-    three = permute(two, over_z0)
-    odd = (z ^ tp) % 2
+    messages = [message, message_y, pair_z, four_z]
+    gated = far_part(enter, y, near, gate, table, messages, poles, taps, [weights])
+    two = permute("gated_two", gated, over_z1)
+    one = permute("gated_one", gated, over_z0)
+    three = permute("gated_three", two, over_z0)
+    odd = (z ^ tp) & 1
     place = jnp.stack([y, odd]).astype(jnp.int32)
 
     def odd_of(z, y, x, c):
@@ -373,16 +394,22 @@
             return z ^ far ^ odd_of(z, y, x, c), y, z // 2, z % 2
 
         return [
-            permute(summed, move, lambda z, y, x, c: x != z // 2),
-            permute(summed, move, lambda z, y, x, c: x == z // 2),
+            permute(f"across_{far}", summed, move, lambda z, y, x, c: x != z // 2),
+            permute(f"straight_{far}", summed, move, lambda z, y, x, c: x == z // 2),
         ]
 
-    parts = []
-    for far, rows in ((0, [gated, one]), (2, [two, three])):
-        kept, sent = project_part(place, rows, out_weight, w_y)
-        from_core = permute(sent, over_core)
-        parts += home((kept.astype(F32) + from_core.astype(F32)).astype(BF16), far)
-    kind = (z ^ tp) // 2
+    def add_cores(name, kept, sent):
+        from_core = permute(name, sent, over_core)
+        return (kept.astype(F32) + from_core.astype(F32)).astype(BF16)
+
+    part_two = project_part(place, [two], out_weight, w_y)
+    near = project_part(place, [after(gated, part_two), one], out_weight, w_y)
+    far = project_part(place, [part_two, after(three, near)], out_weight, w_y, given=True)
+    far_sum = add_cores("core_far", far[0], far[1])
+    near = after(near, far_sum)
+    near_sum = add_cores("core_near", near[0], near[1])
+    parts = home(far_sum, 2) + home(near_sum, 0)
+    kind = 1 - ((z ^ tp) >> 1)
     return pl.pallas_call(
         finish_kernel,
         out_shape=jax.ShapeDtypeStruct((tokens, 2 * out_weight.shape[0]), BF16),
@@ -395,11 +422,12 @@
 
 
 def per_device(features, short_taps, rates, residues, skip, out_weight):
+    q, k, v = (features[:, group] for group in range(3))
     poles, taps = rates.shape[1], short_taps.shape[1]
-    near, message, table = local_part(features, short_taps, rates, residues, skip)
+    near, gate, message, table = local_part(q, k, v, short_taps, rates, residues, skip)
     messages = lax.all_gather(message, "seq")
-    place, q = lax.axis_index("seq"), features[:, 0]
-    gated = far_part(enter_any, place, near, q, table, [messages], poles, taps)
+    place = lax.axis_index("seq")
+    gated = far_part(enter_any, place, near, gate, table, [messages], poles, taps)
     partial = lax.dot_general(
         gated,
         lax.all_gather(out_weight, "seq", axis=0, tiled=True),

time: 70.6 us -> 65.3 us (0.925)
  waiting for transfers between devices: 28.5 us -> 23.1 us
  local copies, waits for them, and re-layouts: 1.97 us -> 1.25 us
    ppermute x13, waiting for transfers between devices: 28.5 us -> 23.1 us  [permute(): return lax.ppermute(x, AXES, pairs)]
    pallas_call x2 -> x4, Pallas kernels: 4.1 us -> 4.86 us  [the longest x3 4.77 us: project_part(): pl.pallas_call(functools.partial(project_kernel, given), out_shape=jax.Sh...]
  transfers between devices with their start and end apart: 13 -> 13, of which waited for: 7 -> 9; matrix products, arithmetic and copies ran while one was open for 0% -> 0% of each run, Pallas kernels for 7% -> 7%
where the time goes in v3:
time: 65.3 us; the launch traced here: 65.1 us
  starting transfers between devices  31.5 us (48%)
  waiting for transfers between devices  23.1 us (35%)
  Pallas kernels  8.82 us (14%)
  local copies, waits for them, and re-layouts  1.25 us (2%)
    ppermute x13, starting transfers between devices, permute(): return lax.ppermute(x, AXES, pairs)  31.5 us
    ppermute x13, waiting for transfers between devices, permute(): return lax.ppermute(x, AXES, pairs)  23.1 us
    pallas_call x3, Pallas kernels, project_part(): pl.pallas_call(functools.partial(project_kernel, given), out_shape=jax.Sh...  4.77 us
    pallas_call x1, Pallas kernels, local_part(): pl.pallas_call(local_kernel, out_shape=(jax.ShapeDtypeStruct((tokens, cha...  2.21 us
  transfers between devices with their start and end apart: 13, of which 9 were waited for; matrix products, arithmetic and copies ran while one was open for 0% of the time, Pallas kernels for 7%

profile of v3, /device:TPU:1, one launch (start us, length us, event | category | flops | bytes accessed | tf_op | source)
XLA Modules:
  0.0 65.1 jit_solution(809661351012952602)
XLA Ops:
  0.0 0.0 copy-start.1
  0.0 0.0 copy-start.3
  0.0 0.0 copy-start.4
  0.0 1.2 %slice_bitcast_fusion.3 = (bf16[128,1024]{1,0:T(8,128)(2,1)S(1)}, bf16[128,1024]{1,0:T(8,128)(2,1)S(1)}, bf16[128,1024]{1,0:T(8,128)(2,1)S(1)}) fusion(bf16[128,3,1024]{2,0,1:T(8,128)(2,1)} %param.6), kind=kLoop, calls=%fused_computation.7 | loop fusion | bytes 1572864 | tf_op jit(solution)/shard_map/squeeze | solution.py:368
  1.2 0.0 copy-start
  1.2 0.0 copy-done.2
  1.2 0.0 copy-done.1
  1.2 0.0 copy-done.3
  1.3 0.0 copy-done.4
  1.3 2.2 %local_filter.1 = (bf16[128,1024]{1,0:T(8,128)(2,1)S(1)}, f32[128,1024]{1,0:T(8,128)S(1)}, bf16[224,128]{1,0:T(8,128)(2,1)S(1)}, f32[336,128]{1,0:T(8,128)S(1)}) custom-call(f32[8,128]{1,0:T(8,128)S(1)} %bitcast.26, bf16[128,1024]{1,0:T(8,128)(2,1)S(1)} %get-tuple-element.24.q_ref, bf16[128,1024]{1,0:T(8,128)(2,1)S(1)} %get-tuple-element.25.k_ref, ...), custom_call_target="tpu_custom_call" | custom-call | flops 8388608 | bytes 3145728 | tf_op jit(solution)/shard_map/local_filter/pallas_call | solution.py:97
  3.5 2.1 %collective-permute-start = (bf16[224,128]{1,0:T(8,128)(2,1)S(1)}, bf16[224,128]{1,0:T(8,128)(2,1)S(1)}, u32[]{:S(2)}, u32[]{:S(2)}) collective-permute-start(bf16[224,128]{1,0:T(8,128)(2,1)S(1)} %get-tuple-element.17.own_ref.refs_0_), channel_id=1, source_target_pairs={{0,4},{1,5},{2,6},{3,7},{4,0},{5,1},{6,2},{7,3},{8,12},{9,13},{10,... | collective-permute-start | bytes 172040 | tf_op jit(solution)/shard_map/state_y/ppermute | solution.py:343
  5.6 1.6 %collective-permute-done.other_ref.refs_1_ = bf16[224,128]{1,0:T(8,128)(2,1)S(1)} collective-permute-done((bf16[224,128]{1,0:T(8,128)(2,1)S(1)}, bf16[224,128]{1,0:T(8,128)(2,1)S(1)}, u32[]{:S(2)}, u32[]{:S(2)}) %collective-permute-start) | collective-permute-done | bytes 57376 | tf_op jit(solution)/shard_map/state_y/ppermute | solution.py:343
  7.2 0.1 join_state.2.own_ref
  7.3 0.1 state_weights.1.refs_4_
  7.3 0.0 copy-done
  7.4 1.5 %collective-permute-start.4 = (bf16[512,1024]{1,0:T(8,128)(2,1)S(1)}, bf16[512,1024]{1,0:T(8,128)(2,1)S(1)}, u32[]{:S(2)}, u32[]{:S(2)}) collective-permute-start(bf16[512,1024]{1,0:T(8,128)(2,1)S(1)} %copy-done), channel_id=1, source_target_pairs={{0,4},{1,5},{2,6},{3,7},{4,0},{5,1},{6,2},{7,3},{8,12},{9,13},{10,... | collective-permute-start | bytes 3145736 | tf_op jit(solution)/shard_map/weights/ppermute | solution.py:343
  8.9 3.2 %collective-permute-start.1 = (bf16[224,128]{1,0:T(8,128)(2,1)S(1)}, bf16[224,128]{1,0:T(8,128)(2,1)S(1)}, u32[]{:S(2)}, u32[]{:S(2)}) collective-permute-start(bf16[224,128]{1,0:T(8,128)(2,1)S(1)} %join_state.2.own_ref), channel_id=1, source_target_pairs={{0,8},{1,9},{2,10},{3,11},{4,12},{5,13},{6,14},{7,15},{8,16},{9,17... | collective-permute-start | bytes 172040 | tf_op jit(solution)/shard_map/state_z1/ppermute | solution.py:343
  12.1 1.2 %collective-permute-done.1.other_ref.refs_2_ = bf16[224,128]{1,0:T(8,128)(2,1)S(1)} collective-permute-done((bf16[224,128]{1,0:T(8,128)(2,1)S(1)}, bf16[224,128]{1,0:T(8,128)(2,1)S(1)}, u32[]{:S(2)}, u32[]{:S(2)}) %collective-permute-start.1) | collective-permute-done | bytes 57376 | tf_op jit(solution)/shard_map/state_z1/ppermute | solution.py:343
  13.3 0.1 join_state.3
  13.4 5.0 %collective-permute-start.2 = (bf16[224,128]{1,0:T(8,128)(2,1)S(1)}, bf16[224,128]{1,0:T(8,128)(2,1)S(1)}, u32[]{:S(2)}, u32[]{:S(2)}) collective-permute-start(bf16[224,128]{1,0:T(8,128)(2,1)S(1)} %join_state.3), channel_id=1, source_target_pairs={{0,16},{1,17},{2,18},{3,19},{4,20},{5,21},{6,22},{7,23},{8,24},{9,... | collective-permute-start | bytes 172040 | tf_op jit(solution)/shard_map/state_z2/ppermute | solution.py:343
  18.4 1.2 %collective-permute-done.2.refs_3_ = bf16[224,128]{1,0:T(8,128)(2,1)S(1)} collective-permute-done((bf16[224,128]{1,0:T(8,128)(2,1)S(1)}, bf16[224,128]{1,0:T(8,128)(2,1)S(1)}, u32[]{:S(2)}, u32[]{:S(2)}) %collective-permute-start.2) | collective-permute-done | bytes 57376 | tf_op jit(solution)/shard_map/state_z2/ppermute | solution.py:343
  19.6 0.9 %far_filter.1.refs_0_ = bf16[128,1024]{1,0:T(8,128)(2,1)S(1)} custom-call(s32[1]{0:T(128)} %bitcast.1.place_ref, bf16[128,1024]{1,0:T(8,128)(2,1)S(1)} %get-tuple-element.14.near_ref, f32[128,1024]{1,0:T(8,128)S(1)} %get-tuple-element.15.gate_ref, f32[336,128]{1,0:T(8,128)S(1)} %get-tuple-element.18.table_ref, ...), custom_call_target="tpu_custom_call" | custom-call | flops 8388608 | bytes 3145728 | tf_op jit(solution)/shard_map/far_filter/pallas_call | solution.py:281
  20.5 2.8 %collective-permute-start.3 = (bf16[128,1024]{1,0:T(8,128)(2,1)S(1)}, bf16[128,1024]{1,0:T(8,128)(2,1)S(1)}, u32[]{:S(2)}, u32[]{:S(2)}) collective-permute-start(bf16[128,1024]{1,0:T(8,128)(2,1)S(1)} %far_filter.1.refs_0_), channel_id=1, source_target_pairs={{0,16},{1,17},{2,18},{3,19},{4,20},{5,21},{6,22},{7,23},{8,24},{9,... | collective-permute-start | bytes 786440 | tf_op jit(solution)/shard_map/gated_two/ppermute | solution.py:343
  23.3 1.7 %collective-permute-start.6 = (bf16[128,1024]{1,0:T(8,128)(2,1)S(1)}, bf16[128,1024]{1,0:T(8,128)(2,1)S(1)}, u32[]{:S(2)}, u32[]{:S(2)}) collective-permute-start(bf16[128,1024]{1,0:T(8,128)(2,1)S(1)} %far_filter.1.refs_0_), channel_id=1, source_target_pairs={{0,8},{1,9},{2,10},{3,11},{4,12},{5,13},{6,14},{7,15},{8,0},{9,1},... | collective-permute-start | bytes 786440 | tf_op jit(solution)/shard_map/gated_one/ppermute | solution.py:343
  25.0 7.4 %collective-permute-done.3.refs_0_ = bf16[128,1024]{1,0:T(8,128)(2,1)S(1)} collective-permute-done((bf16[128,1024]{1,0:T(8,128)(2,1)S(1)}, bf16[128,1024]{1,0:T(8,128)(2,1)S(1)}, u32[]{:S(2)}, u32[]{:S(2)}) %collective-permute-start.3) | collective-permute-done | bytes 262176 | tf_op jit(solution)/shard_map/gated_two/ppermute | solution.py:343
  32.4 1.5 %collective-permute-start.5 = (bf16[128,1024]{1,0:T(8,128)(2,1)S(1)}, bf16[128,1024]{1,0:T(8,128)(2,1)S(1)}, u32[]{:S(2)}, u32[]{:S(2)}) collective-permute-start(bf16[128,1024]{1,0:T(8,128)(2,1)S(1)} %collective-permute-done.3.refs_0_), channel_id=1, source_target_pairs={{0,8},{1,9},{2,10},{3,11},{4,12},{5,13},{6,14},{7,15},{8,0},{9,1},... | collective-permute-start | bytes 786440 | tf_op jit(solution)/shard_map/gated_three/ppermute | solution.py:343
  33.9 0.1 pad_add_fusion.place_ref
  34.0 0.0 collective-permute-done.4.refs_2_.refs_3_
  34.0 1.4 %project.3.refs_0_ = bf16[1,2,128,512]{3,2,1,0:T(8,128)(2,1)S(1)} custom-call(s32[2]{0:T(128)S(1)} %pad_add_fusion.place_ref, bf16[128,1024]{1,0:T(8,128)(2,1)S(1)} %collective-permute-done.3.refs_0_, bf16[512,1024]{1,0:T(8,128)(2,1)S(1)} %copy-done, bf16[512,1024]{1,0:T(8,128)(2,1)S(1)} %collective-permute-done.4.refs_2_.refs_3_), custom_call_target="tpu_custom_call" | custom-call | flops 268435456 | bytes 3145728 | tf_op jit(solution)/shard_map/project/pallas_call | solution.py:312
  35.4 0.0 collective-permute-done.6.refs_1_
  35.4 2.0 %project.4 = bf16[2,2,128,512]{3,2,1,0:T(8,128)(2,1)S(1)} custom-call(s32[2]{0:T(128)S(1)} %pad_add_fusion.place_ref, bf16[128,1024]{1,0:T(8,128)(2,1)S(1)} %far_filter.1.refs_0_, bf16[128,1024]{1,0:T(8,128)(2,1)S(1)} %collective-permute-done.6.refs_1_, bf16[512,1024]{1,0:T(8,128)(2,1)S(1)} %copy-done, ...), custom_call_target="tpu_custom_call" | custom-call | flops 536870912 | bytes 3145728 | tf_op jit(solution)/shard_map/project/pallas_call | solution.py:312
  37.4 1.1 %collective-permute-done.5.refs_1_ = bf16[128,1024]{1,0:T(8,128)(2,1)S(1)} collective-permute-done((bf16[128,1024]{1,0:T(8,128)(2,1)S(1)}, bf16[128,1024]{1,0:T(8,128)(2,1)S(1)}, u32[]{:S(2)}, u32[]{:S(2)}) %collective-permute-start.5) | collective-permute-done | bytes 262176 | tf_op jit(solution)/shard_map/gated_three/ppermute | solution.py:343
  38.6 1.4 %project.5 = bf16[2,2,128,512]{3,2,1,0:T(8,128)(2,1)S(1)} custom-call(s32[2]{0:T(128)S(1)} %pad_add_fusion.place_ref, bf16[1,2,128,512]{3,2,1,0:T(8,128)(2,1)S(1)} %project.3.refs_0_, bf16[128,1024]{1,0:T(8,128)(2,1)S(1)} %collective-permute-done.5.refs_1_, bf16[512,1024]{1,0:T(8,128)(2,1)S(1)} %copy-done, ...), custom_call_target="tpu_custom_call" | custom-call | flops 536870912 | bytes 3145728 | tf_op jit(solution)/shard_map/project/pallas_call | solution.py:312
  40.0 4.2 %collective-permute-start.7 = (bf16[2,128,512]{2,1,0:T(8,128)(2,1)S(1)}, bf16[2,128,512]{2,1,0:T(8,128)(2,1)S(1)}, u32[]{:S(2)}, u32[]{:S(2)}) collective-permute-start(bf16[2,128,512]{2,1,0:T(8,128)(2,1)S(1)} %slice_bitcast_fusion), channel_id=1, source_target_pairs={{0,1},{1,0},{2,3},{3,2},{4,5},{5,4},{6,7},{7,6},{8,9},{9,8},{10,11... | collective-permute-start | bytes 786440 | tf_op jit(solution)/shard_map/core_far/ppermute | solution.py:343
  44.1 1.2 %collective-permute-done.7 = bf16[2,128,512]{2,1,0:T(8,128)(2,1)S(1)} collective-permute-done((bf16[2,128,512]{2,1,0:T(8,128)(2,1)S(1)}, bf16[2,128,512]{2,1,0:T(8,128)(2,1)S(1)}, u32[]{:S(2)}, u32[]{:S(2)}) %collective-permute-start.7) | collective-permute-done | bytes 262176 | tf_op jit(solution)/shard_map/core_far/ppermute | solution.py:343
  45.3 0.1 fusion.1
  45.4 0.4 collective-permute-start.10
  45.8 5.0 %collective-permute-start.9 = (bf16[2,128,512]{2,1,0:T(8,128)(2,1)S(1)}, bf16[2,128,512]{2,1,0:T(8,128)(2,1)S(1)}, u32[]{:S(2)}, u32[]{:S(2)}) collective-permute-start(bf16[2,128,512]{2,1,0:T(8,128)(2,1)S(1)} %fusion.1), channel_id=1, source_target_pairs={{0,16},{1,24},{4,20},{5,28},{8,17},{9,25},{12,21},{13,29},{18,2},{... | collective-permute-start | bytes 786440 | tf_op jit(solution)/shard_map/straight_2/ppermute | solution.py:343
  50.9 0.7 %collective-permute-start.8 = (bf16[2,128,512]{2,1,0:T(8,128)(2,1)S(1)}, bf16[2,128,512]{2,1,0:T(8,128)(2,1)S(1)}, u32[]{:S(2)}, u32[]{:S(2)}) collective-permute-start(bf16[2,128,512]{2,1,0:T(8,128)(2,1)S(1)} %fusion.1), channel_id=1, source_target_pairs={{2,16},{3,24},{6,20},{7,28},{10,17},{11,25},{14,21},{15,29},{16,2}... | collective-permute-start | bytes 786440 | tf_op jit(solution)/shard_map/across_2/ppermute | solution.py:343
  51.6 0.0 collective-permute-done.10
  51.6 0.1 fusion
  51.7 1.9 %collective-permute-start.12 = (bf16[2,128,512]{2,1,0:T(8,128)(2,1)S(1)}, bf16[2,128,512]{2,1,0:T(8,128)(2,1)S(1)}, u32[]{:S(2)}, u32[]{:S(2)}) collective-permute-start(bf16[2,128,512]{2,1,0:T(8,128)(2,1)S(1)} %fusion), channel_id=1, source_target_pairs={{0,0},{1,8},{4,4},{5,12},{8,1},{9,9},{12,5},{13,13},{18,18},{19,26... | collective-permute-start | bytes 786440 | tf_op jit(solution)/shard_map/straight_0/ppermute | solution.py:343
  53.6 1.3 %collective-permute-start.11 = (bf16[2,128,512]{2,1,0:T(8,128)(2,1)S(1)}, bf16[2,128,512]{2,1,0:T(8,128)(2,1)S(1)}, u32[]{:S(2)}, u32[]{:S(2)}) collective-permute-start(bf16[2,128,512]{2,1,0:T(8,128)(2,1)S(1)} %fusion), channel_id=1, source_target_pairs={{2,0},{3,8},{6,4},{7,12},{10,1},{11,9},{14,5},{15,13},{16,18},{17,... | collective-permute-start | bytes 786440 | tf_op jit(solution)/shard_map/across_0/ppermute | solution.py:343
  54.9 1.3 %collective-permute-done.9.refs_1_ = bf16[2,128,512]{2,1,0:T(8,128)(2,1)S(1)} collective-permute-done((bf16[2,128,512]{2,1,0:T(8,128)(2,1)S(1)}, bf16[2,128,512]{2,1,0:T(8,128)(2,1)S(1)}, u32[]{:S(2)}, u32[]{:S(2)}) %collective-permute-start.9) | collective-permute-done | bytes 262176 | tf_op jit(solution)/shard_map/straight_2/ppermute | solution.py:343
  56.2 0.0 collective-permute-done.8.refs_0_
  56.2 7.9 %collective-permute-done.12.refs_3_ = bf16[2,128,512]{2,1,0:T(8,128)(2,1)S(1)} collective-permute-done((bf16[2,128,512]{2,1,0:T(8,128)(2,1)S(1)}, bf16[2,128,512]{2,1,0:T(8,128)(2,1)S(1)}, u32[]{:S(2)}, u32[]{:S(2)}) %collective-permute-start.12) | collective-permute-done | bytes 262176 | tf_op jit(solution)/shard_map/straight_0/ppermute | solution.py:343
  64.1 0.2 collective-permute-done.11.refs_2_
  64.3 0.8 %finish.1 = bf16[128,1024]{1,0:T(8,128)(2,1)} custom-call(s32[1]{0:T(128)} %bitcast.place_ref, bf16[2,128,512]{2,1,0:T(8,128)(2,1)S(1)} %collective-permute-done.8.refs_0_, bf16[2,128,512]{2,1,0:T(8,128)(2,1)S(1)} %collective-permute-done.9.refs_1_, bf16[2,128,512]{2,1,0:T(8,128)(2,1)S(1)} %collective-permute-done.11.refs_2_, ...), custom_call_target="tpu_custom_call" | custom-call | flops 262144 | bytes 2097152 | tf_op jit(solution)/shard_map/finish/pallas_call | solution.py:413
  (3 shorter events, 0.0 us)
Async XLA Ops:
  0.0 1.2 %copy-start.2 = (f32[1024,16]{0,1:T(8,128)S(1)}, f32[1024,16]{0,1:T(8,128)}, u32[]{:S(2)}) copy-start(f32[1024,16]{0,1:T(8,128)} %param.9) | copy-start | bytes 196612
  0.0 1.2 %copy-start.1 = (f32[1024,16]{0,1:T(8,128)S(1)}, f32[1024,16]{0,1:T(8,128)}, u32[]{:S(2)}) copy-start(f32[1024,16]{0,1:T(8,128)} %param.8) | copy-start | bytes 196612
  0.0 1.2 %copy-start.3 = (bf16[3,3,1024]{2,1,0:T(4,128)(2,1)S(1)}, bf16[3,3,1024]{2,1,0:T(4,128)(2,1)}, u32[]{:S(2)}) copy-start(bf16[3,3,1024]{2,1,0:T(4,128)(2,1)} %taps_ref.1) | copy-start | bytes 55300
  0.0 1.3 %copy-start.4 = (f32[1024]{0:T(1024)S(1)}, f32[1024]{0:T(1024)}, u32[]{:S(2)}) copy-start(f32[1024]{0:T(1024)} %param.10) | copy-start | bytes 12292
  1.2 6.1 %copy-start = (bf16[512,1024]{1,0:T(8,128)(2,1)S(1)}, bf16[512,1024]{1,0:T(8,128)(2,1)}, u32[]{:S(2)}) copy-start(bf16[512,1024]{1,0:T(8,128)(2,1)} %refs_2_.3) | copy-start | bytes 3145732
  3.5 3.7 %collective-permute-start = (bf16[224,128]{1,0:T(8,128)(2,1)S(1)}, bf16[224,128]{1,0:T(8,128)(2,1)S(1)}, u32[]{:S(2)}, u32[]{:S(2)}) collective-permute-start(bf16[224,128]{1,0:T(8,128)(2,1)S(1)} %get-tuple-element.17.own_ref.refs_0_), channel_id=1, source_target_pairs={{0,4},{1,5},{2,6},{3,7},{4,0},{5,1},{6,2},{7,3},{8,12},{9,13},{10,... | collective-permute-start | bytes 172040 | tf_op jit(solution)/shard_map/state_y/ppermute | solution.py:343
  7.4 26.6 %collective-permute-start.4 = (bf16[512,1024]{1,0:T(8,128)(2,1)S(1)}, bf16[512,1024]{1,0:T(8,128)(2,1)S(1)}, u32[]{:S(2)}, u32[]{:S(2)}) collective-permute-start(bf16[512,1024]{1,0:T(8,128)(2,1)S(1)} %copy-done), channel_id=1, source_target_pairs={{0,4},{1,5},{2,6},{3,7},{4,0},{5,1},{6,2},{7,3},{8,12},{9,13},{10,... | collective-permute-start | bytes 3145736 | tf_op jit(solution)/shard_map/weights/ppermute | solution.py:343
  8.9 4.4 %collective-permute-start.1 = (bf16[224,128]{1,0:T(8,128)(2,1)S(1)}, bf16[224,128]{1,0:T(8,128)(2,1)S(1)}, u32[]{:S(2)}, u32[]{:S(2)}) collective-permute-start(bf16[224,128]{1,0:T(8,128)(2,1)S(1)} %join_state.2.own_ref), channel_id=1, source_target_pairs={{0,8},{1,9},{2,10},{3,11},{4,12},{5,13},{6,14},{7,15},{8,16},{9,17... | collective-permute-start | bytes 172040 | tf_op jit(solution)/shard_map/state_z1/ppermute | solution.py:343
  13.4 6.2 %collective-permute-start.2 = (bf16[224,128]{1,0:T(8,128)(2,1)S(1)}, bf16[224,128]{1,0:T(8,128)(2,1)S(1)}, u32[]{:S(2)}, u32[]{:S(2)}) collective-permute-start(bf16[224,128]{1,0:T(8,128)(2,1)S(1)} %join_state.3), channel_id=1, source_target_pairs={{0,16},{1,17},{2,18},{3,19},{4,20},{5,21},{6,22},{7,23},{8,24},{9,... | collective-permute-start | bytes 172040 | tf_op jit(solution)/shard_map/state_z2/ppermute | solution.py:343
  20.5 11.9 %collective-permute-start.3 = (bf16[128,1024]{1,0:T(8,128)(2,1)S(1)}, bf16[128,1024]{1,0:T(8,128)(2,1)S(1)}, u32[]{:S(2)}, u32[]{:S(2)}) collective-permute-start(bf16[128,1024]{1,0:T(8,128)(2,1)S(1)} %far_filter.1.refs_0_), channel_id=1, source_target_pairs={{0,16},{1,17},{2,18},{3,19},{4,20},{5,21},{6,22},{7,23},{8,24},{9,... | collective-permute-start | bytes 786440 | tf_op jit(solution)/shard_map/gated_two/ppermute | solution.py:343
  23.3 12.1 %collective-permute-start.6 = (bf16[128,1024]{1,0:T(8,128)(2,1)S(1)}, bf16[128,1024]{1,0:T(8,128)(2,1)S(1)}, u32[]{:S(2)}, u32[]{:S(2)}) collective-permute-start(bf16[128,1024]{1,0:T(8,128)(2,1)S(1)} %far_filter.1.refs_0_), channel_id=1, source_target_pairs={{0,8},{1,9},{2,10},{3,11},{4,12},{5,13},{6,14},{7,15},{8,0},{9,1},... | collective-permute-start | bytes 786440 | tf_op jit(solution)/shard_map/gated_one/ppermute | solution.py:343
  32.4 6.2 %collective-permute-start.5 = (bf16[128,1024]{1,0:T(8,128)(2,1)S(1)}, bf16[128,1024]{1,0:T(8,128)(2,1)S(1)}, u32[]{:S(2)}, u32[]{:S(2)}) collective-permute-start(bf16[128,1024]{1,0:T(8,128)(2,1)S(1)} %collective-permute-done.3.refs_0_), channel_id=1, source_target_pairs={{0,8},{1,9},{2,10},{3,11},{4,12},{5,13},{6,14},{7,15},{8,0},{9,1},... | collective-permute-start | bytes 786440 | tf_op jit(solution)/shard_map/gated_three/ppermute | solution.py:343
  40.0 5.3 %collective-permute-start.7 = (bf16[2,128,512]{2,1,0:T(8,128)(2,1)S(1)}, bf16[2,128,512]{2,1,0:T(8,128)(2,1)S(1)}, u32[]{:S(2)}, u32[]{:S(2)}) collective-permute-start(bf16[2,128,512]{2,1,0:T(8,128)(2,1)S(1)} %slice_bitcast_fusion), channel_id=1, source_target_pairs={{0,1},{1,0},{2,3},{3,2},{4,5},{5,4},{6,7},{7,6},{8,9},{9,8},{10,11... | collective-permute-start | bytes 786440 | tf_op jit(solution)/shard_map/core_far/ppermute | solution.py:343
  45.4 6.2 %collective-permute-start.10 = (bf16[2,128,512]{2,1,0:T(8,128)(2,1)S(1)}, bf16[2,128,512]{2,1,0:T(8,128)(2,1)S(1)}, u32[]{:S(2)}, u32[]{:S(2)}) collective-permute-start(bf16[2,128,512]{2,1,0:T(8,128)(2,1)S(1)} %slice_bitcast_fusion.2), channel_id=1, source_target_pairs={{0,1},{1,0},{2,3},{3,2},{4,5},{5,4},{6,7},{7,6},{8,9},{9,8},{10,11... | collective-permute-start | bytes 786440 | tf_op jit(solution)/shard_map/core_near/ppermute | solution.py:343
  45.8 10.4 %collective-permute-start.9 = (bf16[2,128,512]{2,1,0:T(8,128)(2,1)S(1)}, bf16[2,128,512]{2,1,0:T(8,128)(2,1)S(1)}, u32[]{:S(2)}, u32[]{:S(2)}) collective-permute-start(bf16[2,128,512]{2,1,0:T(8,128)(2,1)S(1)} %fusion.1), channel_id=1, source_target_pairs={{0,16},{1,24},{4,20},{5,28},{8,17},{9,25},{12,21},{13,29},{18,2},{... | collective-permute-start | bytes 786440 | tf_op jit(solution)/shard_map/straight_2/ppermute | solution.py:343
  50.9 5.3 %collective-permute-start.8 = (bf16[2,128,512]{2,1,0:T(8,128)(2,1)S(1)}, bf16[2,128,512]{2,1,0:T(8,128)(2,1)S(1)}, u32[]{:S(2)}, u32[]{:S(2)}) collective-permute-start(bf16[2,128,512]{2,1,0:T(8,128)(2,1)S(1)} %fusion.1), channel_id=1, source_target_pairs={{2,16},{3,24},{6,20},{7,28},{10,17},{11,25},{14,21},{15,29},{16,2}... | collective-permute-start | bytes 786440 | tf_op jit(solution)/shard_map/across_2/ppermute | solution.py:343
  51.7 12.4 %collective-permute-start.12 = (bf16[2,128,512]{2,1,0:T(8,128)(2,1)S(1)}, bf16[2,128,512]{2,1,0:T(8,128)(2,1)S(1)}, u32[]{:S(2)}, u32[]{:S(2)}) collective-permute-start(bf16[2,128,512]{2,1,0:T(8,128)(2,1)S(1)} %fusion), channel_id=1, source_target_pairs={{0,0},{1,8},{4,4},{5,12},{8,1},{9,9},{12,5},{13,13},{18,18},{19,26... | collective-permute-start | bytes 786440 | tf_op jit(solution)/shard_map/straight_0/ppermute | solution.py:343
  53.6 10.7 %collective-permute-start.11 = (bf16[2,128,512]{2,1,0:T(8,128)(2,1)S(1)}, bf16[2,128,512]{2,1,0:T(8,128)(2,1)S(1)}, u32[]{:S(2)}, u32[]{:S(2)}) collective-permute-start(bf16[2,128,512]{2,1,0:T(8,128)(2,1)S(1)} %fusion), channel_id=1, source_target_pairs={{2,0},{3,8},{6,4},{7,12},{10,1},{11,9},{14,5},{15,13},{16,18},{17,... | collective-permute-start | bytes 786440 | tf_op jit(solution)/shard_map/across_0/ppermute | solution.py:343

commit v4 on v3

--- a/solution.py
+++ b/solution.py
@@ -128,7 +128,7 @@
 
     def span(self, shards):
         if self.weights is not None:
-            return self.weights[shards.bit_length() - 1, 0]
+            return self.weights[shards // 4, 0]
         return jnp.exp(-self.rates * float(shards * self.tokens))
 
     def tap(self, group, shift):
@@ -159,7 +159,7 @@
 
     def lead(self, shards):
         if self.weights is not None:
-            return [self.weights[shards.bit_length() - 1, 1 + i] for i in range(self.edge)]
+            return [self.weights[shards // 4, 1 + i] for i in range(self.edge)]
         last = shards * self.tokens - 1
         return [jnp.exp(-self.rates * float(last - i)) * self.residues for i in range(self.edge)]
 
@@ -186,56 +186,68 @@
     return (state,) + pick(place_ref[0])
 
 
-def enter_joined(spans, table, place_ref, own_ref, other_ref, *refs):
-    joined = [table.message(ref[...]) for ref in refs]
-    own, other = table.message(own_ref[...]), table.message(other_ref[...])
-    before = jnp.zeros_like(own)
-    state = before[: table.poles]
-    for shards, current in zip(spans[::-1], joined[::-1]):
-        state = table.enter(state, table.span(shards), table.lead(shards), before, current)
-        before = current
-    second = place_ref[0] == 1
-    behind = table.enter(state, table.span(1), table.lead(1), before, other)
-    return jnp.where(second, behind, state), jnp.where(second, other, before), own
-
-
-def join_kernel(poles, taps, tokens, place_ref, own_ref, other_ref, table_ref, out_ref):
-    fold = own_ref.shape[0] // (poles + 6 * (taps - 1))
+def in_order(place, values):
+    out = []
+    for p in range(4):
+        value = values[p]
+        for g in range(1, 4):
+            value = jnp.where(place == g, values[p ^ g], value)
+        out.append(value)
+    return out
+
+
+def enter_group(table, place_ref, *refs):
+    messages = [table.message(ref[...]) for ref in refs]
+    place, group = place_ref[0], in_order(place_ref[0], messages[:4])
+    before = jnp.zeros_like(messages[4])
+    state = table.enter(before[: table.poles], table.span(4), table.lead(4), before, messages[4])
+    before = messages[4]
+    for p in range(3):
+        behind = table.enter(state, table.span(1), table.lead(1), before, group[p])
+        state = jnp.where(p < place, behind, state)
+        before = jnp.where(p < place, group[p], before)
+    return state, before, messages[0]
+
+
+def join_kernel(poles, taps, tokens, place_ref, *refs):
+    *message_refs, table_ref, out_ref = refs
+    fold = out_ref.shape[0] // (poles + 6 * (taps - 1))
     table = Table(table_ref, poles, taps, fold, tokens)
-    own, other = table.message(own_ref[...]), table.message(other_ref[...])
-    second = place_ref[0] == 1
-    before, current = jnp.where(second, other, own), jnp.where(second, own, other)
-    state = table.enter(before[:poles], table.span(1), table.lead(1), before, current)
+    group = in_order(place_ref[0], [table.message(ref[...]) for ref in message_refs])
+    span, lead = table.span(1), table.lead(1)
+    state = group[0][:poles]
+    for before, current in zip(group[:-1], group[1:]):
+        state = table.enter(state, span, lead, before, current)
     out = [state[r] for r in range(poles)]
-    for group in range(3):
-        out += table.first(before, group) + table.last(current, group)
+    for kind in range(3):
+        out += table.first(group[0], kind) + table.last(group[3], kind)
     out_ref[...] = jnp.concatenate(out, axis=0).astype(BF16)
 
 
-def join_part(place, own, other, table, tokens, poles, taps):
+def join_part(place, messages, table, tokens, poles, taps):
     return pl.pallas_call(
         functools.partial(join_kernel, poles, taps, tokens),
-        out_shape=jax.ShapeDtypeStruct(own.shape, BF16),
-        in_specs=[SMEM] + [VMEM] * 3,
+        out_shape=jax.ShapeDtypeStruct(messages[0].shape, BF16),
+        in_specs=[SMEM] + [VMEM] * 5,
         out_specs=VMEM,
         compiler_params=params(),
         cost_estimate=cost(1 << 20, 1 << 18),
         name="join_state",
-    )(place.reshape(1).astype(jnp.int32), own, other, table)
+    )(place.reshape(1).astype(jnp.int32), *messages, table)
 
 
 def weights_kernel(poles, taps, tokens, table_ref, out_ref):
     fold = out_ref.shape[3]
     table = Table(table_ref, poles, taps, fold, tokens)
-    for i in range(out_ref.shape[0]):
-        for j, weight in enumerate([table.span(1 << i)] + table.lead(1 << i)):
+    for i, shards in enumerate((1, 4)):
+        for j, weight in enumerate([table.span(shards)] + table.lead(shards)):
             out_ref[i, j] = weight
 
 
 def weights_part(table, tokens, poles, taps, fold):
     return pl.pallas_call(
         functools.partial(weights_kernel, poles, taps, tokens),
-        out_shape=jax.ShapeDtypeStruct((3, taps, poles, fold, LANES), F32),
+        out_shape=jax.ShapeDtypeStruct((2, taps, poles, fold, LANES), F32),
         in_specs=[VMEM],
         out_specs=VMEM,
         compiler_params=params(),
@@ -370,16 +382,20 @@
     seq, tp = lax.axis_index("seq"), lax.axis_index("tp")
     z, y = seq >> 1, seq & 1
     near, gate, message, table = local_part(q, k, v, short_taps, rates, residues, skip)
-    message_y = permute("state_y", message, over_y)
-    pair = join_part(y, message, message_y, table, tokens, poles, taps)
-    weights = weights_part(after(table, pair), tokens, poles, taps, channels // LANES)
+    messages = [
+        message,
+        permute("state_y", message, over_y),
+        permute("state_z", message, over_z0),
+        permute("state_zy", message, lambda z, y, x, c: (z ^ 1, 1 - y, x, c)),
+    ]
+    place = seq & 3
+    joined = join_part(place, messages, table, tokens, poles, taps)
+    weights = weights_part(after(table, joined), tokens, poles, taps, channels // LANES)
     w_y = permute("weights", after(out_weight, weights), over_y)
-    pair_z = permute("state_z1", pair, lambda z, y, x, c: (z + 1, y, x, c), lambda z, y, x, c: z + 1 < 4)
-    four = join_part(jnp.ones((), jnp.int32), pair, pair_z, table, 2 * tokens, poles, taps)
-    four_z = permute("state_z2", four, lambda z, y, x, c: (z + 2, y, x, c), lambda z, y, x, c: z + 2 < 4)
-    enter = functools.partial(enter_joined, (2, 4))
-    messages = [message, message_y, pair_z, four_z]
-    gated = far_part(enter, y, near, gate, table, messages, poles, taps, [weights])
+    joined = permute("state_half", joined, over_z1, lambda z, y, x, c: z < 2)
+    gated = far_part(
+        enter_group, place, near, gate, table, messages + [joined], poles, taps, [weights]
+    )
     two = permute("gated_two", gated, over_z1)
     one = permute("gated_one", gated, over_z0)
     three = permute("gated_three", two, over_z0)

time: 65.3 us -> 62.5 us (0.957)
  starting transfers between devices: 31.5 us -> 27.8 us
  waiting for transfers between devices: 23.1 us -> 23.9 us
    ppermute x13 -> x14, starting transfers between devices: 31.5 us -> 27.8 us  [permute(): return lax.ppermute(x, AXES, pairs)]
    ppermute x13 -> x14, waiting for transfers between devices: 23.1 us -> 23.9 us  [permute(): return lax.ppermute(x, AXES, pairs)]
  transfers between devices with their start and end apart: 13 -> 14, of which waited for: 9 -> 9; matrix products, arithmetic and copies ran while one was open for 0% -> 0% of each run, Pallas kernels for 7% -> 7%
where the time goes in v4:
time: 62.5 us; the launch traced here: 62.3 us
  starting transfers between devices  27.8 us (44%)
  waiting for transfers between devices  23.9 us (38%)
  Pallas kernels  8.9 us (14%)
  local copies, waits for them, and re-layouts  1.25 us (2%)
    ppermute x14, starting transfers between devices, permute(): return lax.ppermute(x, AXES, pairs)  27.8 us
    ppermute x14, waiting for transfers between devices, permute(): return lax.ppermute(x, AXES, pairs)  23.9 us
    pallas_call x3, Pallas kernels, project_part(): pl.pallas_call(functools.partial(project_kernel, given), out_shape=jax.Sh...  4.77 us
    pallas_call x1, Pallas kernels, local_part(): pl.pallas_call(local_kernel, out_shape=(jax.ShapeDtypeStruct((tokens, cha...  2.21 us
  transfers between devices with their start and end apart: 14, of which 9 were waited for; matrix products, arithmetic and copies ran while one was open for 0% of the time, Pallas kernels for 7%

profile of v4, /device:TPU:1, one launch (start us, length us, event | category | flops | bytes accessed | tf_op | source)
XLA Modules:
  0.0 62.3 jit_solution(10600377682739573927)
XLA Ops:
  0.0 0.0 copy-start.2
  0.0 0.0 copy-start.4
  0.0 1.2 %slice_bitcast_fusion.3 = (bf16[128,1024]{1,0:T(8,128)(2,1)S(1)}, bf16[128,1024]{1,0:T(8,128)(2,1)S(1)}, bf16[128,1024]{1,0:T(8,128)(2,1)S(1)}) fusion(bf16[128,3,1024]{2,0,1:T(8,128)(2,1)} %param.6), kind=kLoop, calls=%fused_computation.7 | loop fusion | bytes 1572864 | tf_op jit(solution)/shard_map/squeeze | solution.py:380
  1.2 0.0 copy-start
  1.2 0.0 copy-done.2
  1.2 0.0 copy-done.1
  1.2 0.0 copy-done.3
  1.3 0.0 copy-done.4
  1.3 2.2 %local_filter.1 = (bf16[128,1024]{1,0:T(8,128)(2,1)S(1)}, f32[128,1024]{1,0:T(8,128)S(1)}, bf16[224,128]{1,0:T(8,128)(2,1)S(1)}, f32[336,128]{1,0:T(8,128)S(1)}) custom-call(f32[8,128]{1,0:T(8,128)S(1)} %bitcast.27, bf16[128,1024]{1,0:T(8,128)(2,1)S(1)} %get-tuple-element.24.q_ref, bf16[128,1024]{1,0:T(8,128)(2,1)S(1)} %get-tuple-element.25.k_ref, ...), custom_call_target="tpu_custom_call" | custom-call | flops 8388608 | bytes 3145728 | tf_op jit(solution)/shard_map/local_filter/pallas_call | solution.py:97
  3.5 3.1 %collective-permute-start.2 = (bf16[224,128]{1,0:T(8,128)(2,1)S(1)}, bf16[224,128]{1,0:T(8,128)(2,1)S(1)}, u32[]{:S(2)}, u32[]{:S(2)}) collective-permute-start(bf16[224,128]{1,0:T(8,128)(2,1)S(1)} %get-tuple-element.17.refs_0_), channel_id=1, source_target_pairs={{0,12},{1,13},{2,14},{3,15},{4,8},{5,9},{6,10},{7,11},{8,4},{9,5},... | collective-permute-start | bytes 172040 | tf_op jit(solution)/shard_map/state_zy/ppermute | solution.py:355
  6.6 0.2 collective-permute-start.1
  6.8 0.2 collective-permute-start
  7.0 1.2 %collective-permute-done.2.refs_3_ = bf16[224,128]{1,0:T(8,128)(2,1)S(1)} collective-permute-done((bf16[224,128]{1,0:T(8,128)(2,1)S(1)}, bf16[224,128]{1,0:T(8,128)(2,1)S(1)}, u32[]{:S(2)}, u32[]{:S(2)}) %collective-permute-start.2) | collective-permute-done | bytes 57376 | tf_op jit(solution)/shard_map/state_zy/ppermute | solution.py:355
  8.2 1.9 %collective-permute-done.1.refs_2_ = bf16[224,128]{1,0:T(8,128)(2,1)S(1)} collective-permute-done((bf16[224,128]{1,0:T(8,128)(2,1)S(1)}, bf16[224,128]{1,0:T(8,128)(2,1)S(1)}, u32[]{:S(2)}, u32[]{:S(2)}) %collective-permute-start.1) | collective-permute-done | bytes 57376 | tf_op jit(solution)/shard_map/state_z/ppermute | solution.py:355
  10.1 0.0 collective-permute-done.refs_1_
  10.1 0.1 join_state.1
  10.3 0.1 state_weights.1.refs_5_
  10.3 0.0 copy-done
  10.3 0.4 collective-permute-start.5
  10.8 4.4 %collective-permute-start.3 = (bf16[224,128]{1,0:T(8,128)(2,1)S(1)}, bf16[224,128]{1,0:T(8,128)(2,1)S(1)}, u32[]{:S(2)}, u32[]{:S(2)}) collective-permute-start(bf16[224,128]{1,0:T(8,128)(2,1)S(1)} %join_state.1), channel_id=1, source_target_pairs={{0,16},{1,17},{2,18},{3,19},{4,20},{5,21},{6,22},{7,23},{8,24},{9,... | collective-permute-start | bytes 172040 | tf_op jit(solution)/shard_map/state_half/ppermute | solution.py:355
  15.1 1.2 %collective-permute-done.3.refs_4_ = bf16[224,128]{1,0:T(8,128)(2,1)S(1)} collective-permute-done((bf16[224,128]{1,0:T(8,128)(2,1)S(1)}, bf16[224,128]{1,0:T(8,128)(2,1)S(1)}, u32[]{:S(2)}, u32[]{:S(2)}) %collective-permute-start.3) | collective-permute-done | bytes 57376 | tf_op jit(solution)/shard_map/state_half/ppermute | solution.py:355
  16.4 1.0 %far_filter.1.refs_0_ = bf16[128,1024]{1,0:T(8,128)(2,1)S(1)} custom-call(s32[1]{0:T(128)} %bitcast.3.place_ref, bf16[128,1024]{1,0:T(8,128)(2,1)S(1)} %get-tuple-element.14.near_ref, f32[128,1024]{1,0:T(8,128)S(1)} %get-tuple-element.15.gate_ref, f32[336,128]{1,0:T(8,128)S(1)} %get-tuple-element.18.refs_4_.table_ref, ...), custom_call_target="tpu_custom_call" | custom-call | flops 8388608 | bytes 3145728 | tf_op jit(solution)/shard_map/far_filter/pallas_call | solution.py:293
  17.3 2.8 %collective-permute-start.4 = (bf16[128,1024]{1,0:T(8,128)(2,1)S(1)}, bf16[128,1024]{1,0:T(8,128)(2,1)S(1)}, u32[]{:S(2)}, u32[]{:S(2)}) collective-permute-start(bf16[128,1024]{1,0:T(8,128)(2,1)S(1)} %far_filter.1.refs_0_), channel_id=1, source_target_pairs={{0,16},{1,17},{2,18},{3,19},{4,20},{5,21},{6,22},{7,23},{8,24},{9,... | collective-permute-start | bytes 786440 | tf_op jit(solution)/shard_map/gated_two/ppermute | solution.py:355
  20.1 1.7 %collective-permute-start.7 = (bf16[128,1024]{1,0:T(8,128)(2,1)S(1)}, bf16[128,1024]{1,0:T(8,128)(2,1)S(1)}, u32[]{:S(2)}, u32[]{:S(2)}) collective-permute-start(bf16[128,1024]{1,0:T(8,128)(2,1)S(1)} %far_filter.1.refs_0_), channel_id=1, source_target_pairs={{0,8},{1,9},{2,10},{3,11},{4,12},{5,13},{6,14},{7,15},{8,0},{9,1},... | collective-permute-start | bytes 786440 | tf_op jit(solution)/shard_map/gated_one/ppermute | solution.py:355
  21.9 8.2 %collective-permute-done.4.refs_0_ = bf16[128,1024]{1,0:T(8,128)(2,1)S(1)} collective-permute-done((bf16[128,1024]{1,0:T(8,128)(2,1)S(1)}, bf16[128,1024]{1,0:T(8,128)(2,1)S(1)}, u32[]{:S(2)}, u32[]{:S(2)}) %collective-permute-start.4) | collective-permute-done | bytes 262176 | tf_op jit(solution)/shard_map/gated_two/ppermute | solution.py:355
  30.1 1.7 %collective-permute-start.6 = (bf16[128,1024]{1,0:T(8,128)(2,1)S(1)}, bf16[128,1024]{1,0:T(8,128)(2,1)S(1)}, u32[]{:S(2)}, u32[]{:S(2)}) collective-permute-start(bf16[128,1024]{1,0:T(8,128)(2,1)S(1)} %collective-permute-done.4.refs_0_), channel_id=1, source_target_pairs={{0,8},{1,9},{2,10},{3,11},{4,12},{5,13},{6,14},{7,15},{8,0},{9,1},... | collective-permute-start | bytes 786440 | tf_op jit(solution)/shard_map/gated_three/ppermute | solution.py:355
  31.8 0.1 pad_add_fusion.place_ref
  31.9 1.1 %collective-permute-done.5.refs_2_.refs_3_ = bf16[512,1024]{1,0:T(8,128)(2,1)S(1)} collective-permute-done((bf16[512,1024]{1,0:T(8,128)(2,1)S(1)}, bf16[512,1024]{1,0:T(8,128)(2,1)S(1)}, u32[]{:S(2)}, u32[]{:S(2)}) %collective-permute-start.5) | collective-permute-done | bytes 1048608 | tf_op jit(solution)/shard_map/weights/ppermute | solution.py:355
  33.0 1.4 %project.3.refs_0_ = bf16[1,2,128,512]{3,2,1,0:T(8,128)(2,1)S(1)} custom-call(s32[2]{0:T(128)S(1)} %pad_add_fusion.place_ref, bf16[128,1024]{1,0:T(8,128)(2,1)S(1)} %collective-permute-done.4.refs_0_, bf16[512,1024]{1,0:T(8,128)(2,1)S(1)} %copy-done, bf16[512,1024]{1,0:T(8,128)(2,1)S(1)} %collective-permute-done.5.refs_2_.refs_3_), custom_call_target="tpu_custom_call" | custom-call | flops 268435456 | bytes 3145728 | tf_op jit(solution)/shard_map/project/pallas_call | solution.py:324
  34.3 0.0 collective-permute-done.7.refs_1_
  34.3 2.0 %project.4 = bf16[2,2,128,512]{3,2,1,0:T(8,128)(2,1)S(1)} custom-call(s32[2]{0:T(128)S(1)} %pad_add_fusion.place_ref, bf16[128,1024]{1,0:T(8,128)(2,1)S(1)} %far_filter.1.refs_0_, bf16[128,1024]{1,0:T(8,128)(2,1)S(1)} %collective-permute-done.7.refs_1_, bf16[512,1024]{1,0:T(8,128)(2,1)S(1)} %copy-done, ...), custom_call_target="tpu_custom_call" | custom-call | flops 536870912 | bytes 3145728 | tf_op jit(solution)/shard_map/project/pallas_call | solution.py:324
  36.4 0.0 collective-permute-done.6.refs_1_
  36.4 1.4 %project.5 = bf16[2,2,128,512]{3,2,1,0:T(8,128)(2,1)S(1)} custom-call(s32[2]{0:T(128)S(1)} %pad_add_fusion.place_ref, bf16[1,2,128,512]{3,2,1,0:T(8,128)(2,1)S(1)} %project.3.refs_0_, bf16[128,1024]{1,0:T(8,128)(2,1)S(1)} %collective-permute-done.6.refs_1_, bf16[512,1024]{1,0:T(8,128)(2,1)S(1)} %copy-done, ...), custom_call_target="tpu_custom_call" | custom-call | flops 536870912 | bytes 3145728 | tf_op jit(solution)/shard_map/project/pallas_call | solution.py:324
  37.8 3.2 %collective-permute-start.8 = (bf16[2,128,512]{2,1,0:T(8,128)(2,1)S(1)}, bf16[2,128,512]{2,1,0:T(8,128)(2,1)S(1)}, u32[]{:S(2)}, u32[]{:S(2)}) collective-permute-start(bf16[2,128,512]{2,1,0:T(8,128)(2,1)S(1)} %slice_bitcast_fusion), channel_id=1, source_target_pairs={{0,1},{1,0},{2,3},{3,2},{4,5},{5,4},{6,7},{7,6},{8,9},{9,8},{10,11... | collective-permute-start | bytes 786440 | tf_op jit(solution)/shard_map/core_far/ppermute | solution.py:355
  41.0 1.2 %collective-permute-done.8 = bf16[2,128,512]{2,1,0:T(8,128)(2,1)S(1)} collective-permute-done((bf16[2,128,512]{2,1,0:T(8,128)(2,1)S(1)}, bf16[2,128,512]{2,1,0:T(8,128)(2,1)S(1)}, u32[]{:S(2)}, u32[]{:S(2)}) %collective-permute-start.8) | collective-permute-done | bytes 262176 | tf_op jit(solution)/shard_map/core_far/ppermute | solution.py:355
  42.1 0.1 fusion.1
  42.2 0.4 collective-permute-start.11
  42.7 5.8 %collective-permute-start.10 = (bf16[2,128,512]{2,1,0:T(8,128)(2,1)S(1)}, bf16[2,128,512]{2,1,0:T(8,128)(2,1)S(1)}, u32[]{:S(2)}, u32[]{:S(2)}) collective-permute-start(bf16[2,128,512]{2,1,0:T(8,128)(2,1)S(1)} %fusion.1), channel_id=1, source_target_pairs={{0,16},{1,24},{4,20},{5,28},{8,17},{9,25},{12,21},{13,29},{18,2},{... | collective-permute-start | bytes 786440 | tf_op jit(solution)/shard_map/straight_2/ppermute | solution.py:355
  48.4 0.7 %collective-permute-start.9 = (bf16[2,128,512]{2,1,0:T(8,128)(2,1)S(1)}, bf16[2,128,512]{2,1,0:T(8,128)(2,1)S(1)}, u32[]{:S(2)}, u32[]{:S(2)}) collective-permute-start(bf16[2,128,512]{2,1,0:T(8,128)(2,1)S(1)} %fusion.1), channel_id=1, source_target_pairs={{2,16},{3,24},{6,20},{7,28},{10,17},{11,25},{14,21},{15,29},{16,2}... | collective-permute-start | bytes 786440 | tf_op jit(solution)/shard_map/across_2/ppermute | solution.py:355
  49.1 0.0 collective-permute-done.11
  49.1 0.1 fusion
  49.2 1.9 %collective-permute-start.13 = (bf16[2,128,512]{2,1,0:T(8,128)(2,1)S(1)}, bf16[2,128,512]{2,1,0:T(8,128)(2,1)S(1)}, u32[]{:S(2)}, u32[]{:S(2)}) collective-permute-start(bf16[2,128,512]{2,1,0:T(8,128)(2,1)S(1)} %fusion), channel_id=1, source_target_pairs={{0,0},{1,8},{4,4},{5,12},{8,1},{9,9},{12,5},{13,13},{18,18},{19,26... | collective-permute-start | bytes 786440 | tf_op jit(solution)/shard_map/straight_0/ppermute | solution.py:355
  51.1 1.3 %collective-permute-start.12 = (bf16[2,128,512]{2,1,0:T(8,128)(2,1)S(1)}, bf16[2,128,512]{2,1,0:T(8,128)(2,1)S(1)}, u32[]{:S(2)}, u32[]{:S(2)}) collective-permute-start(bf16[2,128,512]{2,1,0:T(8,128)(2,1)S(1)} %fusion), channel_id=1, source_target_pairs={{2,0},{3,8},{6,4},{7,12},{10,1},{11,9},{14,5},{15,13},{16,18},{17,... | collective-permute-start | bytes 786440 | tf_op jit(solution)/shard_map/across_0/ppermute | solution.py:355
  52.4 1.5 %collective-permute-done.10.refs_1_ = bf16[2,128,512]{2,1,0:T(8,128)(2,1)S(1)} collective-permute-done((bf16[2,128,512]{2,1,0:T(8,128)(2,1)S(1)}, bf16[2,128,512]{2,1,0:T(8,128)(2,1)S(1)}, u32[]{:S(2)}, u32[]{:S(2)}) %collective-permute-start.10) | collective-permute-done | bytes 262176 | tf_op jit(solution)/shard_map/straight_2/ppermute | solution.py:355
  54.0 0.0 collective-permute-done.9.refs_0_
  54.0 5.9 %collective-permute-done.13.refs_3_ = bf16[2,128,512]{2,1,0:T(8,128)(2,1)S(1)} collective-permute-done((bf16[2,128,512]{2,1,0:T(8,128)(2,1)S(1)}, bf16[2,128,512]{2,1,0:T(8,128)(2,1)S(1)}, u32[]{:S(2)}, u32[]{:S(2)}) %collective-permute-start.13) | collective-permute-done | bytes 262176 | tf_op jit(solution)/shard_map/straight_0/ppermute | solution.py:355
  59.9 1.7 %collective-permute-done.12.refs_2_ = bf16[2,128,512]{2,1,0:T(8,128)(2,1)S(1)} collective-permute-done((bf16[2,128,512]{2,1,0:T(8,128)(2,1)S(1)}, bf16[2,128,512]{2,1,0:T(8,128)(2,1)S(1)}, u32[]{:S(2)}, u32[]{:S(2)}) %collective-permute-start.12) | collective-permute-done | bytes 262176 | tf_op jit(solution)/shard_map/across_0/ppermute | solution.py:355
  61.6 0.8 %finish.1 = bf16[128,1024]{1,0:T(8,128)(2,1)} custom-call(s32[1]{0:T(128)} %bitcast.place_ref, bf16[2,128,512]{2,1,0:T(8,128)(2,1)S(1)} %collective-permute-done.9.refs_0_, bf16[2,128,512]{2,1,0:T(8,128)(2,1)S(1)} %collective-permute-done.10.refs_1_, bf16[2,128,512]{2,1,0:T(8,128)(2,1)S(1)} %collective-permute-done.12.refs_2_, ...), custom_call_target="tpu_custom_call" | custom-call | flops 262144 | bytes 2097152 | tf_op jit(solution)/shard_map/finish/pallas_call | solution.py:429
  (4 shorter events, 0.0 us)
Async XLA Ops:
  0.0 1.2 %copy-start.2 = (f32[1024,16]{0,1:T(8,128)S(1)}, f32[1024,16]{0,1:T(8,128)}, u32[]{:S(2)}) copy-start(f32[1024,16]{0,1:T(8,128)} %param.9) | copy-start | bytes 196612
  0.0 1.2 %copy-start.1 = (f32[1024,16]{0,1:T(8,128)S(1)}, f32[1024,16]{0,1:T(8,128)}, u32[]{:S(2)}) copy-start(f32[1024,16]{0,1:T(8,128)} %param.8) | copy-start | bytes 196612
  0.0 1.2 %copy-start.3 = (bf16[3,3,1024]{2,1,0:T(4,128)(2,1)S(1)}, bf16[3,3,1024]{2,1,0:T(4,128)(2,1)}, u32[]{:S(2)}) copy-start(bf16[3,3,1024]{2,1,0:T(4,128)(2,1)} %taps_ref.1) | copy-start | bytes 55300
  0.0 1.3 %copy-start.4 = (f32[1024]{0:T(1024)S(1)}, f32[1024]{0:T(1024)}, u32[]{:S(2)}) copy-start(f32[1024]{0:T(1024)} %param.10) | copy-start | bytes 12292
  1.2 9.1 %copy-start = (bf16[512,1024]{1,0:T(8,128)(2,1)S(1)}, bf16[512,1024]{1,0:T(8,128)(2,1)}, u32[]{:S(2)}) copy-start(bf16[512,1024]{1,0:T(8,128)(2,1)} %refs_2_.3) | copy-start | bytes 3145732
  3.5 4.7 %collective-permute-start.2 = (bf16[224,128]{1,0:T(8,128)(2,1)S(1)}, bf16[224,128]{1,0:T(8,128)(2,1)S(1)}, u32[]{:S(2)}, u32[]{:S(2)}) collective-permute-start(bf16[224,128]{1,0:T(8,128)(2,1)S(1)} %get-tuple-element.17.refs_0_), channel_id=1, source_target_pairs={{0,12},{1,13},{2,14},{3,15},{4,8},{5,9},{6,10},{7,11},{8,4},{9,5},... | collective-permute-start | bytes 172040 | tf_op jit(solution)/shard_map/state_zy/ppermute | solution.py:355
  6.6 3.5 %collective-permute-start.1 = (bf16[224,128]{1,0:T(8,128)(2,1)S(1)}, bf16[224,128]{1,0:T(8,128)(2,1)S(1)}, u32[]{:S(2)}, u32[]{:S(2)}) collective-permute-start(bf16[224,128]{1,0:T(8,128)(2,1)S(1)} %get-tuple-element.17.refs_0_), channel_id=1, source_target_pairs={{0,8},{1,9},{2,10},{3,11},{4,12},{5,13},{6,14},{7,15},{8,0},{9,1},... | collective-permute-start | bytes 172040 | tf_op jit(solution)/shard_map/state_z/ppermute | solution.py:355
  6.8 3.3 %collective-permute-start = (bf16[224,128]{1,0:T(8,128)(2,1)S(1)}, bf16[224,128]{1,0:T(8,128)(2,1)S(1)}, u32[]{:S(2)}, u32[]{:S(2)}) collective-permute-start(bf16[224,128]{1,0:T(8,128)(2,1)S(1)} %get-tuple-element.17.refs_0_), channel_id=1, source_target_pairs={{0,4},{1,5},{2,6},{3,7},{4,0},{5,1},{6,2},{7,3},{8,12},{9,13},{10,... | collective-permute-start | bytes 172040 | tf_op jit(solution)/shard_map/state_y/ppermute | solution.py:355
  10.3 22.6 %collective-permute-start.5 = (bf16[512,1024]{1,0:T(8,128)(2,1)S(1)}, bf16[512,1024]{1,0:T(8,128)(2,1)S(1)}, u32[]{:S(2)}, u32[]{:S(2)}) collective-permute-start(bf16[512,1024]{1,0:T(8,128)(2,1)S(1)} %copy-done), channel_id=1, source_target_pairs={{0,4},{1,5},{2,6},{3,7},{4,0},{5,1},{6,2},{7,3},{8,12},{9,13},{10,... | collective-permute-start | bytes 3145736 | tf_op jit(solution)/shard_map/weights/ppermute | solution.py:355
  10.8 5.6 %collective-permute-start.3 = (bf16[224,128]{1,0:T(8,128)(2,1)S(1)}, bf16[224,128]{1,0:T(8,128)(2,1)S(1)}, u32[]{:S(2)}, u32[]{:S(2)}) collective-permute-start(bf16[224,128]{1,0:T(8,128)(2,1)S(1)} %join_state.1), channel_id=1, source_target_pairs={{0,16},{1,17},{2,18},{3,19},{4,20},{5,21},{6,22},{7,23},{8,24},{9,... | collective-permute-start | bytes 172040 | tf_op jit(solution)/shard_map/state_half/ppermute | solution.py:355
  17.3 12.7 %collective-permute-start.4 = (bf16[128,1024]{1,0:T(8,128)(2,1)S(1)}, bf16[128,1024]{1,0:T(8,128)(2,1)S(1)}, u32[]{:S(2)}, u32[]{:S(2)}) collective-permute-start(bf16[128,1024]{1,0:T(8,128)(2,1)S(1)} %far_filter.1.refs_0_), channel_id=1, source_target_pairs={{0,16},{1,17},{2,18},{3,19},{4,20},{5,21},{6,22},{7,23},{8,24},{9,... | collective-permute-start | bytes 786440 | tf_op jit(solution)/shard_map/gated_two/ppermute | solution.py:355
  20.1 14.2 %collective-permute-start.7 = (bf16[128,1024]{1,0:T(8,128)(2,1)S(1)}, bf16[128,1024]{1,0:T(8,128)(2,1)S(1)}, u32[]{:S(2)}, u32[]{:S(2)}) collective-permute-start(bf16[128,1024]{1,0:T(8,128)(2,1)S(1)} %far_filter.1.refs_0_), channel_id=1, source_target_pairs={{0,8},{1,9},{2,10},{3,11},{4,12},{5,13},{6,14},{7,15},{8,0},{9,1},... | collective-permute-start | bytes 786440 | tf_op jit(solution)/shard_map/gated_one/ppermute | solution.py:355
  30.1 6.3 %collective-permute-start.6 = (bf16[128,1024]{1,0:T(8,128)(2,1)S(1)}, bf16[128,1024]{1,0:T(8,128)(2,1)S(1)}, u32[]{:S(2)}, u32[]{:S(2)}) collective-permute-start(bf16[128,1024]{1,0:T(8,128)(2,1)S(1)} %collective-permute-done.4.refs_0_), channel_id=1, source_target_pairs={{0,8},{1,9},{2,10},{3,11},{4,12},{5,13},{6,14},{7,15},{8,0},{9,1},... | collective-permute-start | bytes 786440 | tf_op jit(solution)/shard_map/gated_three/ppermute | solution.py:355
  37.8 4.3 %collective-permute-start.8 = (bf16[2,128,512]{2,1,0:T(8,128)(2,1)S(1)}, bf16[2,128,512]{2,1,0:T(8,128)(2,1)S(1)}, u32[]{:S(2)}, u32[]{:S(2)}) collective-permute-start(bf16[2,128,512]{2,1,0:T(8,128)(2,1)S(1)} %slice_bitcast_fusion), channel_id=1, source_target_pairs={{0,1},{1,0},{2,3},{3,2},{4,5},{5,4},{6,7},{7,6},{8,9},{9,8},{10,11... | collective-permute-start | bytes 786440 | tf_op jit(solution)/shard_map/core_far/ppermute | solution.py:355
  42.2 6.9 %collective-permute-start.11 = (bf16[2,128,512]{2,1,0:T(8,128)(2,1)S(1)}, bf16[2,128,512]{2,1,0:T(8,128)(2,1)S(1)}, u32[]{:S(2)}, u32[]{:S(2)}) collective-permute-start(bf16[2,128,512]{2,1,0:T(8,128)(2,1)S(1)} %slice_bitcast_fusion.2), channel_id=1, source_target_pairs={{0,1},{1,0},{2,3},{3,2},{4,5},{5,4},{6,7},{7,6},{8,9},{9,8},{10,11... | collective-permute-start | bytes 786440 | tf_op jit(solution)/shard_map/core_near/ppermute | solution.py:355
  42.7 11.3 %collective-permute-start.10 = (bf16[2,128,512]{2,1,0:T(8,128)(2,1)S(1)}, bf16[2,128,512]{2,1,0:T(8,128)(2,1)S(1)}, u32[]{:S(2)}, u32[]{:S(2)}) collective-permute-start(bf16[2,128,512]{2,1,0:T(8,128)(2,1)S(1)} %fusion.1), channel_id=1, source_target_pairs={{0,16},{1,24},{4,20},{5,28},{8,17},{9,25},{12,21},{13,29},{18,2},{... | collective-permute-start | bytes 786440 | tf_op jit(solution)/shard_map/straight_2/ppermute | solution.py:355
  48.4 5.5 %collective-permute-start.9 = (bf16[2,128,512]{2,1,0:T(8,128)(2,1)S(1)}, bf16[2,128,512]{2,1,0:T(8,128)(2,1)S(1)}, u32[]{:S(2)}, u32[]{:S(2)}) collective-permute-start(bf16[2,128,512]{2,1,0:T(8,128)(2,1)S(1)} %fusion.1), channel_id=1, source_target_pairs={{2,16},{3,24},{6,20},{7,28},{10,17},{11,25},{14,21},{15,29},{16,2}... | collective-permute-start | bytes 786440 | tf_op jit(solution)/shard_map/across_2/ppermute | solution.py:355
  49.2 10.7 %collective-permute-start.13 = (bf16[2,128,512]{2,1,0:T(8,128)(2,1)S(1)}, bf16[2,128,512]{2,1,0:T(8,128)(2,1)S(1)}, u32[]{:S(2)}, u32[]{:S(2)}) collective-permute-start(bf16[2,128,512]{2,1,0:T(8,128)(2,1)S(1)} %fusion), channel_id=1, source_target_pairs={{0,0},{1,8},{4,4},{5,12},{8,1},{9,9},{12,5},{13,13},{18,18},{19,26... | collective-permute-start | bytes 786440 | tf_op jit(solution)/shard_map/straight_0/ppermute | solution.py:355
  51.1 10.4 %collective-permute-start.12 = (bf16[2,128,512]{2,1,0:T(8,128)(2,1)S(1)}, bf16[2,128,512]{2,1,0:T(8,128)(2,1)S(1)}, u32[]{:S(2)}, u32[]{:S(2)}) collective-permute-start(bf16[2,128,512]{2,1,0:T(8,128)(2,1)S(1)} %fusion), channel_id=1, source_target_pairs={{2,0},{3,8},{6,4},{7,12},{10,1},{11,9},{14,5},{15,13},{16,18},{17,... | collective-permute-start | bytes 786440 | tf_op jit(solution)/shard_map/across_0/ppermute | solution.py:355

commit v5 on v4

--- a/solution.py
+++ b/solution.py
@@ -8,6 +8,7 @@
 from jax.sharding import PartitionSpec as P
 
 LANES = 128
+SUBLANES = 16
 F32 = jnp.float32
 BF16 = jnp.bfloat16
 VMEM = pl.BlockSpec(memory_space=pltpu.VMEM)
@@ -23,10 +24,10 @@
     return pltpu.CompilerParams(vmem_limit_bytes=16 * 1024 * 1024, **kw)
 
 
-def local_kernel(
+def signal_kernel(
     skip_ref, q_ref, k_ref, v_ref, taps_ref, rates_ref, residues_ref,
-    out_ref, gate_ref, message_ref, table_ref,
-    signal_s, conv_s, message_s,
+    signal_ref, message_ref, table_ref,
+    message_s,
 ):
     tokens, channels = q_ref.shape
     poles, taps = rates_ref.shape[0], taps_ref.shape[1]
@@ -42,41 +43,66 @@
         table_ref[pl.ds(poles * fold + j, poles, stride=fold), :] = residues_ref[:, lanes]
         mixed = []
         for group, ref in enumerate((q_ref, k_ref, v_ref)):
-            value = ref[:, lanes].astype(F32)
             total = None
+            value = ref[:, lanes].astype(F32) if group else None
             for shift in range(taps):
                 row = (tap_row + group * taps + shift) * fold + j
                 tap = taps_ref[group, shift : shift + 1, lanes].astype(F32)
                 table_ref[row : row + 1, :] = tap
-                moved = value if shift == 0 else pltpu.roll(value, shift, axis=0)
-                total = tap * moved if total is None else total + tap * moved
+                if group:
+                    moved = value if shift == 0 else pltpu.roll(value, shift, axis=0)
+                    total = tap * moved if total is None else total + tap * moved
             mixed.append(total)
+            first, last = ref[:SUBLANES, lanes].astype(F32), ref[-SUBLANES:, lanes].astype(F32)
             for place in range(2 * edge):
-                source = place if place < edge else tokens - 2 * edge + place
                 row = (poles + group * 2 * edge + place) * fold + j
-                message_s[row : row + 1, :] = value[source : source + 1, :]
-        gate_ref[:, lanes] = mixed[0]
+                source = place if place < edge else SUBLANES - 2 * edge + place
+                source_rows = first if place < edge else last
+                message_s[row : row + 1, :] = source_rows[source : source + 1, :]
         signal = jnp.where(later, mixed[1] * mixed[2], 0.0)
-        signal_s[pl.ds(j, tokens, stride=fold), :] = signal
+        signal_ref[pl.ds(j, tokens, stride=fold), :] = signal
+    decay = [jnp.exp(-table_ref[r * fold : (r + 1) * fold, :]) for r in range(poles)]
+
+    def step(t, modes):
+        value = signal_ref[pl.ds(pl.multiple_of(t * fold, fold), fold), :]
+        return tuple(d * m + value for d, m in zip(decay, modes))
+
+    modes = lax.fori_loop(0, tokens, step, (jnp.zeros((fold, LANES), F32),) * poles, unroll=8)
+    for r in range(poles):
+        residue = table_ref[(poles + r) * fold : (poles + r + 1) * fold, :]
+        message_s[r * fold : (r + 1) * fold, :] = residue * modes[r]
+    message_ref[...] = message_s[...].astype(BF16)
+
+
+def near_kernel(poles, taps, q_ref, signal_ref, table_ref, out_ref, gate_ref, conv_s):
+    tokens, channels = q_ref.shape
+    fold = channels // LANES
+    tap_row = 2 * poles
+    skip_row = tap_row + 3 * taps
     decay = [jnp.exp(-table_ref[r * fold : (r + 1) * fold, :]) for r in range(poles)]
     residue = [table_ref[(poles + r) * fold : (poles + r + 1) * fold, :] for r in range(poles)]
     skip = table_ref[skip_row * fold : (skip_row + 1) * fold, :]
 
     def step(t, modes):
         rows = pl.ds(pl.multiple_of(t * fold, fold), fold)
-        value = signal_s[rows, :]
+        value = signal_ref[rows, :]
         modes = tuple(d * m + c * value for d, c, m in zip(decay, residue, modes))
         conv_s[rows, :] = tree_sum(modes + (skip * value,))
         return modes
 
-    modes = lax.fori_loop(0, tokens, step, (jnp.zeros((fold, LANES), F32),) * poles, unroll=4)
-    for r in range(poles):
-        message_s[r * fold : (r + 1) * fold, :] = modes[r]
-    message_ref[...] = message_s[...].astype(BF16)
+    lax.fori_loop(0, tokens, step, (jnp.zeros((fold, LANES), F32),) * poles, unroll=4)
     for j in range(fold):
         lanes = slice(j * LANES, (j + 1) * LANES)
+        value = q_ref[:, lanes].astype(F32)
+        gate = None
+        for shift in range(taps):
+            row = (tap_row + shift) * fold + j
+            moved = value if shift == 0 else pltpu.roll(value, shift, axis=0)
+            term = table_ref[row : row + 1, :] * moved
+            gate = term if gate is None else gate + term
+        gate_ref[:, lanes] = gate
         conv = conv_s[pl.ds(j, tokens, stride=fold), :]
-        out_ref[:, lanes] = (gate_ref[:, lanes] * conv).astype(BF16)
+        out_ref[:, lanes] = (gate * conv).astype(BF16)
 
 
 def tree_sum(values):
@@ -88,31 +114,43 @@
     return values[0]
 
 
-def local_part(q, k, v, short_taps, rates, residues, skip):
+def signal_part(q, k, v, short_taps, rates, residues, skip):
     tokens, channels = q.shape
     poles, taps = rates.shape[1], short_taps.shape[1]
     fold = channels // LANES
     message_rows = (poles + 6 * (taps - 1)) * fold
     table_rows = (2 * poles + 3 * taps + 1) * fold
     return pl.pallas_call(
-        local_kernel,
+        signal_kernel,
         out_shape=(
-            jax.ShapeDtypeStruct((tokens, channels), BF16),
-            jax.ShapeDtypeStruct((tokens, channels), F32),
+            jax.ShapeDtypeStruct((tokens * fold, LANES), F32),
             jax.ShapeDtypeStruct((message_rows, LANES), BF16),
             jax.ShapeDtypeStruct((table_rows, LANES), F32),
         ),
         in_specs=[VMEM] * 7,
-        out_specs=(VMEM,) * 4,
-        scratch_shapes=[
-            pltpu.VMEM((tokens * fold, LANES), F32),
-            pltpu.VMEM((tokens * fold, LANES), F32),
-            pltpu.VMEM((message_rows, LANES), F32),
-        ],
-        compiler_params=params(),
-        cost_estimate=cost(4 * tokens * channels * poles, 3 << 20),
-        name="local_filter",
+        out_specs=(VMEM,) * 3,
+        scratch_shapes=[pltpu.VMEM((message_rows, LANES), F32)],
+        compiler_params=params(),
+        cost_estimate=cost(2 * tokens * channels * poles, 2 << 20),
+        name="signal",
     )(skip.reshape(fold, LANES), q, k, v, short_taps, rates.T, residues.T)
+
+
+def near_part(q, signal, table, poles, taps):
+    tokens, channels = q.shape
+    return pl.pallas_call(
+        functools.partial(near_kernel, poles, taps),
+        out_shape=(
+            jax.ShapeDtypeStruct((tokens, channels), BF16),
+            jax.ShapeDtypeStruct((tokens, channels), F32),
+        ),
+        in_specs=[VMEM] * 3,
+        out_specs=(VMEM,) * 2,
+        scratch_shapes=[pltpu.VMEM(signal.shape, F32)],
+        compiler_params=params(),
+        cost_estimate=cost(4 * tokens * channels * poles, 2 << 20),
+        name="near_filter",
+    )(q, signal, table)
 
 
 class Table:
@@ -381,7 +419,8 @@
     poles, taps = rates.shape[1], short_taps.shape[1]
     seq, tp = lax.axis_index("seq"), lax.axis_index("tp")
     z, y = seq >> 1, seq & 1
-    near, gate, message, table = local_part(q, k, v, short_taps, rates, residues, skip)
+    signal, message, table = signal_part(q, k, v, short_taps, rates, residues, skip)
+    near, gate = near_part(q, signal, table, poles, taps)
     messages = [
         message,
         permute("state_y", message, over_y),
@@ -440,7 +479,8 @@
 def per_device(features, short_taps, rates, residues, skip, out_weight):
     q, k, v = (features[:, group] for group in range(3))
     poles, taps = rates.shape[1], short_taps.shape[1]
-    near, gate, message, table = local_part(q, k, v, short_taps, rates, residues, skip)
+    signal, message, table = signal_part(q, k, v, short_taps, rates, residues, skip)
+    near, gate = near_part(q, signal, table, poles, taps)
     messages = lax.all_gather(message, "seq")
     place = lax.axis_index("seq")
     gated = far_part(enter_any, place, near, gate, table, [messages], poles, taps)

time: 62.5 us -> 61.4 us (0.982)
  waiting for transfers between devices: 23.9 us -> 22.7 us
    ppermute x14, waiting for transfers between devices: 23.9 us -> 22.7 us  [permute(): return lax.ppermute(x, AXES, pairs)]
    pallas_call x1 -> x2, Pallas kernels: 2.21 us -> 2.66 us  [the longest x1 1.55 us: near_part(): pl.pallas_call(functools.partial(near_kernel, poles, taps), out_shape=(ja...]
  transfers between devices with their start and end apart: 14 -> 14, of which waited for: 9 -> 8; matrix products, arithmetic and copies ran while one was open for 0% -> 0% of each run, Pallas kernels for 7% -> 10%
where the time goes in v5:
time: 61.4 us; the launch traced here: 61.2 us
  starting transfers between devices  27.5 us (45%)
  waiting for transfers between devices  22.7 us (37%)
  Pallas kernels  9.35 us (15%)
  local copies, waits for them, and re-layouts  1.25 us (2%)
    ppermute x14, starting transfers between devices, permute(): return lax.ppermute(x, AXES, pairs)  27.5 us
    ppermute x14, waiting for transfers between devices, permute(): return lax.ppermute(x, AXES, pairs)  22.7 us
    pallas_call x3, Pallas kernels, project_part(): pl.pallas_call(functools.partial(project_kernel, given), out_shape=jax.Sh...  4.77 us
    pallas_call x1, Pallas kernels, near_part(): pl.pallas_call(functools.partial(near_kernel, poles, taps), out_shape=(ja...  1.55 us
  transfers between devices with their start and end apart: 14, of which 8 were waited for; matrix products, arithmetic and copies ran while one was open for 0% of the time, Pallas kernels for 10%

profile of v5, /device:TPU:1, one launch (start us, length us, event | category | flops | bytes accessed | tf_op | source)
XLA Modules:
  0.0 61.2 jit_solution(17611363935934986527)
XLA Ops:
  0.0 0.0 copy-start.4
  0.0 1.2 %slice_bitcast_fusion.3 = (bf16[128,1024]{1,0:T(8,128)(2,1)S(1)}, bf16[128,1024]{1,0:T(8,128)(2,1)S(1)}, bf16[128,1024]{1,0:T(8,128)(2,1)S(1)}) fusion(bf16[128,3,1024]{2,0,1:T(8,128)(2,1)} %param.6), kind=kLoop, calls=%fused_computation.7 | loop fusion | bytes 1572864 | tf_op jit(solution)/shard_map/squeeze | solution.py:418
  1.2 0.0 copy-start
  1.2 0.0 copy-done.2
  1.2 0.0 copy-done.1
  1.2 0.0 copy-done.3
  1.3 0.0 copy-done.4
  1.3 1.1 %signal.1 = (f32[1024,128]{1,0:T(8,128)S(1)}, bf16[224,128]{1,0:T(8,128)(2,1)S(1)}, f32[336,128]{1,0:T(8,128)S(1)}) custom-call(f32[8,128]{1,0:T(8,128)S(1)} %bitcast.27, bf16[128,1024]{1,0:T(8,128)(2,1)S(1)} %get-tuple-element.26.q_ref, bf16[128,1024]{1,0:T(8,128)(2,1)S(1)} %get-tuple-element.27.k_ref, bf16[128,1024]{1,0:T(8,128)(2,1)S(1)} %get-tuple-element.25.v_ref, ...), custom_call_target="tpu_custom_call" | custom-call | flops 4194304 | bytes 2097152 | tf_op jit(solution)/shard_map/signal/pallas_call | solution.py:123
  2.4 3.1 %collective-permute-start.2 = (bf16[224,128]{1,0:T(8,128)(2,1)S(1)}, bf16[224,128]{1,0:T(8,128)(2,1)S(1)}, u32[]{:S(2)}, u32[]{:S(2)}) collective-permute-start(bf16[224,128]{1,0:T(8,128)(2,1)S(1)} %get-tuple-element.19.refs_0_), channel_id=1, source_target_pairs={{0,12},{1,13},{2,14},{3,15},{4,8},{5,9},{6,10},{7,11},{8,4},{9,5},... | collective-permute-start | bytes 172040 | tf_op jit(solution)/shard_map/state_zy/ppermute | solution.py:393
  5.5 0.2 collective-permute-start.1
  5.7 0.2 collective-permute-start
  5.9 1.2 %collective-permute-done.2.refs_3_ = bf16[224,128]{1,0:T(8,128)(2,1)S(1)} collective-permute-done((bf16[224,128]{1,0:T(8,128)(2,1)S(1)}, bf16[224,128]{1,0:T(8,128)(2,1)S(1)}, u32[]{:S(2)}, u32[]{:S(2)}) %collective-permute-start.2) | collective-permute-done | bytes 57376 | tf_op jit(solution)/shard_map/state_zy/ppermute | solution.py:393
  7.1 1.9 %collective-permute-done.1.refs_2_ = bf16[224,128]{1,0:T(8,128)(2,1)S(1)} collective-permute-done((bf16[224,128]{1,0:T(8,128)(2,1)S(1)}, bf16[224,128]{1,0:T(8,128)(2,1)S(1)}, u32[]{:S(2)}, u32[]{:S(2)}) %collective-permute-start.1) | collective-permute-done | bytes 57376 | tf_op jit(solution)/shard_map/state_z/ppermute | solution.py:393
  9.0 0.0 collective-permute-done.refs_1_
  9.0 0.1 join_state.1
  9.2 0.1 state_weights.1.refs_5_
  9.2 0.0 copy-done
  9.2 0.4 collective-permute-start.5
  9.7 4.4 %collective-permute-start.3 = (bf16[224,128]{1,0:T(8,128)(2,1)S(1)}, bf16[224,128]{1,0:T(8,128)(2,1)S(1)}, u32[]{:S(2)}, u32[]{:S(2)}) collective-permute-start(bf16[224,128]{1,0:T(8,128)(2,1)S(1)} %join_state.1), channel_id=1, source_target_pairs={{0,16},{1,17},{2,18},{3,19},{4,20},{5,21},{6,22},{7,23},{8,24},{9,... | collective-permute-start | bytes 172040 | tf_op jit(solution)/shard_map/state_half/ppermute | solution.py:393
  14.0 1.5 %near_filter.1 = (bf16[128,1024]{1,0:T(8,128)(2,1)S(1)}, f32[128,1024]{1,0:T(8,128)S(1)}) custom-call(bf16[128,1024]{1,0:T(8,128)(2,1)S(1)} %get-tuple-element.26.q_ref, f32[1024,128]{1,0:T(8,128)S(1)} %get-tuple-element.15.signal_ref, f32[336,128]{1,0:T(8,128)S(1)} %get-tuple-element.20.table_ref.refs_4_), custom_call_target="tpu_custom_call" | custom-call | flops 8388608 | bytes 2097152 | tf_op jit(solution)/shard_map/near_filter/pallas_call | solution.py:141
  15.6 0.0 collective-permute-done.3.refs_4_
  15.6 1.0 %far_filter.1.refs_0_ = bf16[128,1024]{1,0:T(8,128)(2,1)S(1)} custom-call(s32[1]{0:T(128)} %bitcast.3.place_ref, bf16[128,1024]{1,0:T(8,128)(2,1)S(1)} %get-tuple-element.17.near_ref, f32[128,1024]{1,0:T(8,128)S(1)} %get-tuple-element.18.gate_ref, f32[336,128]{1,0:T(8,128)S(1)} %get-tuple-element.20.table_ref.refs_4_, ...), custom_call_target="tpu_custom_call" | custom-call | flops 8388608 | bytes 3145728 | tf_op jit(solution)/shard_map/far_filter/pallas_call | solution.py:331
  16.6 2.5 %collective-permute-start.4 = (bf16[128,1024]{1,0:T(8,128)(2,1)S(1)}, bf16[128,1024]{1,0:T(8,128)(2,1)S(1)}, u32[]{:S(2)}, u32[]{:S(2)}) collective-permute-start(bf16[128,1024]{1,0:T(8,128)(2,1)S(1)} %far_filter.1.refs_0_), channel_id=1, source_target_pairs={{0,16},{1,17},{2,18},{3,19},{4,20},{5,21},{6,22},{7,23},{8,24},{9,... | collective-permute-start | bytes 786440 | tf_op jit(solution)/shard_map/gated_two/ppermute | solution.py:393
  19.0 1.7 %collective-permute-start.7 = (bf16[128,1024]{1,0:T(8,128)(2,1)S(1)}, bf16[128,1024]{1,0:T(8,128)(2,1)S(1)}, u32[]{:S(2)}, u32[]{:S(2)}) collective-permute-start(bf16[128,1024]{1,0:T(8,128)(2,1)S(1)} %far_filter.1.refs_0_), channel_id=1, source_target_pairs={{0,8},{1,9},{2,10},{3,11},{4,12},{5,13},{6,14},{7,15},{8,0},{9,1},... | collective-permute-start | bytes 786440 | tf_op jit(solution)/shard_map/gated_one/ppermute | solution.py:393
  20.8 8.2 %collective-permute-done.4.refs_0_ = bf16[128,1024]{1,0:T(8,128)(2,1)S(1)} collective-permute-done((bf16[128,1024]{1,0:T(8,128)(2,1)S(1)}, bf16[128,1024]{1,0:T(8,128)(2,1)S(1)}, u32[]{:S(2)}, u32[]{:S(2)}) %collective-permute-start.4) | collective-permute-done | bytes 262176 | tf_op jit(solution)/shard_map/gated_two/ppermute | solution.py:393
  29.0 1.7 %collective-permute-start.6 = (bf16[128,1024]{1,0:T(8,128)(2,1)S(1)}, bf16[128,1024]{1,0:T(8,128)(2,1)S(1)}, u32[]{:S(2)}, u32[]{:S(2)}) collective-permute-start(bf16[128,1024]{1,0:T(8,128)(2,1)S(1)} %collective-permute-done.4.refs_0_), channel_id=1, source_target_pairs={{0,8},{1,9},{2,10},{3,11},{4,12},{5,13},{6,14},{7,15},{8,0},{9,1},... | collective-permute-start | bytes 786440 | tf_op jit(solution)/shard_map/gated_three/ppermute | solution.py:393
  30.7 0.1 pad_add_fusion.place_ref
  30.8 1.1 %collective-permute-done.5.refs_2_.refs_3_ = bf16[512,1024]{1,0:T(8,128)(2,1)S(1)} collective-permute-done((bf16[512,1024]{1,0:T(8,128)(2,1)S(1)}, bf16[512,1024]{1,0:T(8,128)(2,1)S(1)}, u32[]{:S(2)}, u32[]{:S(2)}) %collective-permute-start.5) | collective-permute-done | bytes 1048608 | tf_op jit(solution)/shard_map/weights/ppermute | solution.py:393
  31.9 1.4 %project.3.refs_0_ = bf16[1,2,128,512]{3,2,1,0:T(8,128)(2,1)S(1)} custom-call(s32[2]{0:T(128)S(1)} %pad_add_fusion.place_ref, bf16[128,1024]{1,0:T(8,128)(2,1)S(1)} %collective-permute-done.4.refs_0_, bf16[512,1024]{1,0:T(8,128)(2,1)S(1)} %copy-done, bf16[512,1024]{1,0:T(8,128)(2,1)S(1)} %collective-permute-done.5.refs_2_.refs_3_), custom_call_target="tpu_custom_call" | custom-call | flops 268435456 | bytes 3145728 | tf_op jit(solution)/shard_map/project/pallas_call | solution.py:362
  33.2 0.0 collective-permute-done.7.refs_1_
  33.2 2.0 %project.4 = bf16[2,2,128,512]{3,2,1,0:T(8,128)(2,1)S(1)} custom-call(s32[2]{0:T(128)S(1)} %pad_add_fusion.place_ref, bf16[128,1024]{1,0:T(8,128)(2,1)S(1)} %far_filter.1.refs_0_, bf16[128,1024]{1,0:T(8,128)(2,1)S(1)} %collective-permute-done.7.refs_1_, bf16[512,1024]{1,0:T(8,128)(2,1)S(1)} %copy-done, ...), custom_call_target="tpu_custom_call" | custom-call | flops 536870912 | bytes 3145728 | tf_op jit(solution)/shard_map/project/pallas_call | solution.py:362
  35.3 0.0 collective-permute-done.6.refs_1_
  35.3 1.4 %project.5 = bf16[2,2,128,512]{3,2,1,0:T(8,128)(2,1)S(1)} custom-call(s32[2]{0:T(128)S(1)} %pad_add_fusion.place_ref, bf16[1,2,128,512]{3,2,1,0:T(8,128)(2,1)S(1)} %project.3.refs_0_, bf16[128,1024]{1,0:T(8,128)(2,1)S(1)} %collective-permute-done.6.refs_1_, bf16[512,1024]{1,0:T(8,128)(2,1)S(1)} %copy-done, ...), custom_call_target="tpu_custom_call" | custom-call | flops 536870912 | bytes 3145728 | tf_op jit(solution)/shard_map/project/pallas_call | solution.py:362
  36.7 3.2 %collective-permute-start.8 = (bf16[2,128,512]{2,1,0:T(8,128)(2,1)S(1)}, bf16[2,128,512]{2,1,0:T(8,128)(2,1)S(1)}, u32[]{:S(2)}, u32[]{:S(2)}) collective-permute-start(bf16[2,128,512]{2,1,0:T(8,128)(2,1)S(1)} %slice_bitcast_fusion), channel_id=1, source_target_pairs={{0,1},{1,0},{2,3},{3,2},{4,5},{5,4},{6,7},{7,6},{8,9},{9,8},{10,11... | collective-permute-start | bytes 786440 | tf_op jit(solution)/shard_map/core_far/ppermute | solution.py:393
  39.9 1.2 %collective-permute-done.8 = bf16[2,128,512]{2,1,0:T(8,128)(2,1)S(1)} collective-permute-done((bf16[2,128,512]{2,1,0:T(8,128)(2,1)S(1)}, bf16[2,128,512]{2,1,0:T(8,128)(2,1)S(1)}, u32[]{:S(2)}, u32[]{:S(2)}) %collective-permute-start.8) | collective-permute-done | bytes 262176 | tf_op jit(solution)/shard_map/core_far/ppermute | solution.py:393
  41.0 0.1 fusion.1
  41.1 0.4 collective-permute-start.11
  41.6 5.8 %collective-permute-start.10 = (bf16[2,128,512]{2,1,0:T(8,128)(2,1)S(1)}, bf16[2,128,512]{2,1,0:T(8,128)(2,1)S(1)}, u32[]{:S(2)}, u32[]{:S(2)}) collective-permute-start(bf16[2,128,512]{2,1,0:T(8,128)(2,1)S(1)} %fusion.1), channel_id=1, source_target_pairs={{0,16},{1,24},{4,20},{5,28},{8,17},{9,25},{12,21},{13,29},{18,2},{... | collective-permute-start | bytes 786440 | tf_op jit(solution)/shard_map/straight_2/ppermute | solution.py:393
  47.3 0.7 %collective-permute-start.9 = (bf16[2,128,512]{2,1,0:T(8,128)(2,1)S(1)}, bf16[2,128,512]{2,1,0:T(8,128)(2,1)S(1)}, u32[]{:S(2)}, u32[]{:S(2)}) collective-permute-start(bf16[2,128,512]{2,1,0:T(8,128)(2,1)S(1)} %fusion.1), channel_id=1, source_target_pairs={{2,16},{3,24},{6,20},{7,28},{10,17},{11,25},{14,21},{15,29},{16,2}... | collective-permute-start | bytes 786440 | tf_op jit(solution)/shard_map/across_2/ppermute | solution.py:393
  48.0 0.0 collective-permute-done.11
  48.0 0.1 fusion
  48.1 1.9 %collective-permute-start.13 = (bf16[2,128,512]{2,1,0:T(8,128)(2,1)S(1)}, bf16[2,128,512]{2,1,0:T(8,128)(2,1)S(1)}, u32[]{:S(2)}, u32[]{:S(2)}) collective-permute-start(bf16[2,128,512]{2,1,0:T(8,128)(2,1)S(1)} %fusion), channel_id=1, source_target_pairs={{0,0},{1,8},{4,4},{5,12},{8,1},{9,9},{12,5},{13,13},{18,18},{19,26... | collective-permute-start | bytes 786440 | tf_op jit(solution)/shard_map/straight_0/ppermute | solution.py:393
  50.0 1.3 %collective-permute-start.12 = (bf16[2,128,512]{2,1,0:T(8,128)(2,1)S(1)}, bf16[2,128,512]{2,1,0:T(8,128)(2,1)S(1)}, u32[]{:S(2)}, u32[]{:S(2)}) collective-permute-start(bf16[2,128,512]{2,1,0:T(8,128)(2,1)S(1)} %fusion), channel_id=1, source_target_pairs={{2,0},{3,8},{6,4},{7,12},{10,1},{11,9},{14,5},{15,13},{16,18},{17,... | collective-permute-start | bytes 786440 | tf_op jit(solution)/shard_map/across_0/ppermute | solution.py:393
  51.3 1.5 %collective-permute-done.10.refs_1_ = bf16[2,128,512]{2,1,0:T(8,128)(2,1)S(1)} collective-permute-done((bf16[2,128,512]{2,1,0:T(8,128)(2,1)S(1)}, bf16[2,128,512]{2,1,0:T(8,128)(2,1)S(1)}, u32[]{:S(2)}, u32[]{:S(2)}) %collective-permute-start.10) | collective-permute-done | bytes 262176 | tf_op jit(solution)/shard_map/straight_2/ppermute | solution.py:393
  52.9 0.0 collective-permute-done.9.refs_0_
  52.9 5.9 %collective-permute-done.13.refs_3_ = bf16[2,128,512]{2,1,0:T(8,128)(2,1)S(1)} collective-permute-done((bf16[2,128,512]{2,1,0:T(8,128)(2,1)S(1)}, bf16[2,128,512]{2,1,0:T(8,128)(2,1)S(1)}, u32[]{:S(2)}, u32[]{:S(2)}) %collective-permute-start.13) | collective-permute-done | bytes 262176 | tf_op jit(solution)/shard_map/straight_0/ppermute | solution.py:393
  58.8 1.7 %collective-permute-done.12.refs_2_ = bf16[2,128,512]{2,1,0:T(8,128)(2,1)S(1)} collective-permute-done((bf16[2,128,512]{2,1,0:T(8,128)(2,1)S(1)}, bf16[2,128,512]{2,1,0:T(8,128)(2,1)S(1)}, u32[]{:S(2)}, u32[]{:S(2)}) %collective-permute-start.12) | collective-permute-done | bytes 262176 | tf_op jit(solution)/shard_map/across_0/ppermute | solution.py:393
  60.5 0.8 %finish.1 = bf16[128,1024]{1,0:T(8,128)(2,1)} custom-call(s32[1]{0:T(128)} %bitcast.place_ref, bf16[2,128,512]{2,1,0:T(8,128)(2,1)S(1)} %collective-permute-done.9.refs_0_, bf16[2,128,512]{2,1,0:T(8,128)(2,1)S(1)} %collective-permute-done.10.refs_1_, bf16[2,128,512]{2,1,0:T(8,128)(2,1)S(1)} %collective-permute-done.12.refs_2_, ...), custom_call_target="tpu_custom_call" | custom-call | flops 262144 | bytes 2097152 | tf_op jit(solution)/shard_map/finish/pallas_call | solution.py:468
  (5 shorter events, 0.0 us)
Async XLA Ops:
  0.0 1.2 %copy-start.2 = (f32[1024,16]{0,1:T(8,128)S(1)}, f32[1024,16]{0,1:T(8,128)}, u32[]{:S(2)}) copy-start(f32[1024,16]{0,1:T(8,128)} %param.9) | copy-start | bytes 196612
  0.0 1.2 %copy-start.1 = (f32[1024,16]{0,1:T(8,128)S(1)}, f32[1024,16]{0,1:T(8,128)}, u32[]{:S(2)}) copy-start(f32[1024,16]{0,1:T(8,128)} %param.8) | copy-start | bytes 196612
  0.0 1.2 %copy-start.3 = (bf16[3,3,1024]{2,1,0:T(4,128)(2,1)S(1)}, bf16[3,3,1024]{2,1,0:T(4,128)(2,1)}, u32[]{:S(2)}) copy-start(bf16[3,3,1024]{2,1,0:T(4,128)(2,1)} %taps_ref.1) | copy-start | bytes 55300
  0.0 1.3 %copy-start.4 = (f32[1024]{0:T(1024)S(1)}, f32[1024]{0:T(1024)}, u32[]{:S(2)}) copy-start(f32[1024]{0:T(1024)} %param.10) | copy-start | bytes 12292
  1.2 8.0 %copy-start = (bf16[512,1024]{1,0:T(8,128)(2,1)S(1)}, bf16[512,1024]{1,0:T(8,128)(2,1)}, u32[]{:S(2)}) copy-start(bf16[512,1024]{1,0:T(8,128)(2,1)} %refs_2_.3) | copy-start | bytes 3145732
  2.4 4.7 %collective-permute-start.2 = (bf16[224,128]{1,0:T(8,128)(2,1)S(1)}, bf16[224,128]{1,0:T(8,128)(2,1)S(1)}, u32[]{:S(2)}, u32[]{:S(2)}) collective-permute-start(bf16[224,128]{1,0:T(8,128)(2,1)S(1)} %get-tuple-element.19.refs_0_), channel_id=1, source_target_pairs={{0,12},{1,13},{2,14},{3,15},{4,8},{5,9},{6,10},{7,11},{8,4},{9,5},... | collective-permute-start | bytes 172040 | tf_op jit(solution)/shard_map/state_zy/ppermute | solution.py:393
  5.5 3.5 %collective-permute-start.1 = (bf16[224,128]{1,0:T(8,128)(2,1)S(1)}, bf16[224,128]{1,0:T(8,128)(2,1)S(1)}, u32[]{:S(2)}, u32[]{:S(2)}) collective-permute-start(bf16[224,128]{1,0:T(8,128)(2,1)S(1)} %get-tuple-element.19.refs_0_), channel_id=1, source_target_pairs={{0,8},{1,9},{2,10},{3,11},{4,12},{5,13},{6,14},{7,15},{8,0},{9,1},... | collective-permute-start | bytes 172040 | tf_op jit(solution)/shard_map/state_z/ppermute | solution.py:393
  5.7 3.3 %collective-permute-start = (bf16[224,128]{1,0:T(8,128)(2,1)S(1)}, bf16[224,128]{1,0:T(8,128)(2,1)S(1)}, u32[]{:S(2)}, u32[]{:S(2)}) collective-permute-start(bf16[224,128]{1,0:T(8,128)(2,1)S(1)} %get-tuple-element.19.refs_0_), channel_id=1, source_target_pairs={{0,4},{1,5},{2,6},{3,7},{4,0},{5,1},{6,2},{7,3},{8,12},{9,13},{10,... | collective-permute-start | bytes 172040 | tf_op jit(solution)/shard_map/state_y/ppermute | solution.py:393
  9.2 22.6 %collective-permute-start.5 = (bf16[512,1024]{1,0:T(8,128)(2,1)S(1)}, bf16[512,1024]{1,0:T(8,128)(2,1)S(1)}, u32[]{:S(2)}, u32[]{:S(2)}) collective-permute-start(bf16[512,1024]{1,0:T(8,128)(2,1)S(1)} %copy-done), channel_id=1, source_target_pairs={{0,4},{1,5},{2,6},{3,7},{4,0},{5,1},{6,2},{7,3},{8,12},{9,13},{10,... | collective-permute-start | bytes 3145736 | tf_op jit(solution)/shard_map/weights/ppermute | solution.py:393
  9.7 5.9 %collective-permute-start.3 = (bf16[224,128]{1,0:T(8,128)(2,1)S(1)}, bf16[224,128]{1,0:T(8,128)(2,1)S(1)}, u32[]{:S(2)}, u32[]{:S(2)}) collective-permute-start(bf16[224,128]{1,0:T(8,128)(2,1)S(1)} %join_state.1), channel_id=1, source_target_pairs={{0,16},{1,17},{2,18},{3,19},{4,20},{5,21},{6,22},{7,23},{8,24},{9,... | collective-permute-start | bytes 172040 | tf_op jit(solution)/shard_map/state_half/ppermute | solution.py:393
  16.6 12.4 %collective-permute-start.4 = (bf16[128,1024]{1,0:T(8,128)(2,1)S(1)}, bf16[128,1024]{1,0:T(8,128)(2,1)S(1)}, u32[]{:S(2)}, u32[]{:S(2)}) collective-permute-start(bf16[128,1024]{1,0:T(8,128)(2,1)S(1)} %far_filter.1.refs_0_), channel_id=1, source_target_pairs={{0,16},{1,17},{2,18},{3,19},{4,20},{5,21},{6,22},{7,23},{8,24},{9,... | collective-permute-start | bytes 786440 | tf_op jit(solution)/shard_map/gated_two/ppermute | solution.py:393
  19.0 14.2 %collective-permute-start.7 = (bf16[128,1024]{1,0:T(8,128)(2,1)S(1)}, bf16[128,1024]{1,0:T(8,128)(2,1)S(1)}, u32[]{:S(2)}, u32[]{:S(2)}) collective-permute-start(bf16[128,1024]{1,0:T(8,128)(2,1)S(1)} %far_filter.1.refs_0_), channel_id=1, source_target_pairs={{0,8},{1,9},{2,10},{3,11},{4,12},{5,13},{6,14},{7,15},{8,0},{9,1},... | collective-permute-start | bytes 786440 | tf_op jit(solution)/shard_map/gated_one/ppermute | solution.py:393
  29.0 6.3 %collective-permute-start.6 = (bf16[128,1024]{1,0:T(8,128)(2,1)S(1)}, bf16[128,1024]{1,0:T(8,128)(2,1)S(1)}, u32[]{:S(2)}, u32[]{:S(2)}) collective-permute-start(bf16[128,1024]{1,0:T(8,128)(2,1)S(1)} %collective-permute-done.4.refs_0_), channel_id=1, source_target_pairs={{0,8},{1,9},{2,10},{3,11},{4,12},{5,13},{6,14},{7,15},{8,0},{9,1},... | collective-permute-start | bytes 786440 | tf_op jit(solution)/shard_map/gated_three/ppermute | solution.py:393
  36.7 4.3 %collective-permute-start.8 = (bf16[2,128,512]{2,1,0:T(8,128)(2,1)S(1)}, bf16[2,128,512]{2,1,0:T(8,128)(2,1)S(1)}, u32[]{:S(2)}, u32[]{:S(2)}) collective-permute-start(bf16[2,128,512]{2,1,0:T(8,128)(2,1)S(1)} %slice_bitcast_fusion), channel_id=1, source_target_pairs={{0,1},{1,0},{2,3},{3,2},{4,5},{5,4},{6,7},{7,6},{8,9},{9,8},{10,11... | collective-permute-start | bytes 786440 | tf_op jit(solution)/shard_map/core_far/ppermute | solution.py:393
  41.1 6.9 %collective-permute-start.11 = (bf16[2,128,512]{2,1,0:T(8,128)(2,1)S(1)}, bf16[2,128,512]{2,1,0:T(8,128)(2,1)S(1)}, u32[]{:S(2)}, u32[]{:S(2)}) collective-permute-start(bf16[2,128,512]{2,1,0:T(8,128)(2,1)S(1)} %slice_bitcast_fusion.2), channel_id=1, source_target_pairs={{0,1},{1,0},{2,3},{3,2},{4,5},{5,4},{6,7},{7,6},{8,9},{9,8},{10,11... | collective-permute-start | bytes 786440 | tf_op jit(solution)/shard_map/core_near/ppermute | solution.py:393
  41.6 11.3 %collective-permute-start.10 = (bf16[2,128,512]{2,1,0:T(8,128)(2,1)S(1)}, bf16[2,128,512]{2,1,0:T(8,128)(2,1)S(1)}, u32[]{:S(2)}, u32[]{:S(2)}) collective-permute-start(bf16[2,128,512]{2,1,0:T(8,128)(2,1)S(1)} %fusion.1), channel_id=1, source_target_pairs={{0,16},{1,24},{4,20},{5,28},{8,17},{9,25},{12,21},{13,29},{18,2},{... | collective-permute-start | bytes 786440 | tf_op jit(solution)/shard_map/straight_2/ppermute | solution.py:393
  47.3 5.5 %collective-permute-start.9 = (bf16[2,128,512]{2,1,0:T(8,128)(2,1)S(1)}, bf16[2,128,512]{2,1,0:T(8,128)(2,1)S(1)}, u32[]{:S(2)}, u32[]{:S(2)}) collective-permute-start(bf16[2,128,512]{2,1,0:T(8,128)(2,1)S(1)} %fusion.1), channel_id=1, source_target_pairs={{2,16},{3,24},{6,20},{7,28},{10,17},{11,25},{14,21},{15,29},{16,2}... | collective-permute-start | bytes 786440 | tf_op jit(solution)/shard_map/across_2/ppermute | solution.py:393
  48.1 10.7 %collective-permute-start.13 = (bf16[2,128,512]{2,1,0:T(8,128)(2,1)S(1)}, bf16[2,128,512]{2,1,0:T(8,128)(2,1)S(1)}, u32[]{:S(2)}, u32[]{:S(2)}) collective-permute-start(bf16[2,128,512]{2,1,0:T(8,128)(2,1)S(1)} %fusion), channel_id=1, source_target_pairs={{0,0},{1,8},{4,4},{5,12},{8,1},{9,9},{12,5},{13,13},{18,18},{19,26... | collective-permute-start | bytes 786440 | tf_op jit(solution)/shard_map/straight_0/ppermute | solution.py:393
  50.0 10.4 %collective-permute-start.12 = (bf16[2,128,512]{2,1,0:T(8,128)(2,1)S(1)}, bf16[2,128,512]{2,1,0:T(8,128)(2,1)S(1)}, u32[]{:S(2)}, u32[]{:S(2)}) collective-permute-start(bf16[2,128,512]{2,1,0:T(8,128)(2,1)S(1)} %fusion), channel_id=1, source_target_pairs={{2,0},{3,8},{6,4},{7,12},{10,1},{11,9},{14,5},{15,13},{16,18},{17,... | collective-permute-start | bytes 786440 | tf_op jit(solution)/shard_map/across_0/ppermute | solution.py:393

commit v6 on v5

--- a/solution.py
+++ b/solution.py
@@ -235,7 +235,7 @@
 
 
 def enter_group(table, place_ref, *refs):
-    messages = [table.message(ref[...]) for ref in refs]
+    messages = [table.message(ref[...]) for ref in refs[3::-1] + refs[4:]]
     place, group = place_ref[0], in_order(place_ref[0], messages[:4])
     before = jnp.zeros_like(messages[4])
     state = table.enter(before[: table.poles], table.span(4), table.lead(4), before, messages[4])
@@ -248,7 +248,7 @@
 
 
 def join_kernel(poles, taps, tokens, place_ref, *refs):
-    *message_refs, table_ref, out_ref = refs
+    message_refs, (table_ref, out_ref) = refs[3::-1], refs[4:]
     fold = out_ref.shape[0] // (poles + 6 * (taps - 1))
     table = Table(table_ref, poles, taps, fold, tokens)
     group = in_order(place_ref[0], [table.message(ref[...]) for ref in message_refs])
@@ -271,7 +271,7 @@
         compiler_params=params(),
         cost_estimate=cost(1 << 20, 1 << 18),
         name="join_state",
-    )(place.reshape(1).astype(jnp.int32), *messages, table)
+    )(place.reshape(1).astype(jnp.int32), *messages[::-1], table)
 
 
 def weights_kernel(poles, taps, tokens, table_ref, out_ref):
@@ -340,34 +340,51 @@
     )(place.reshape(1).astype(jnp.int32), near, gate, table, *messages, *weights)
 
 
-def project_kernel(given, place_ref, *refs):
-    *rows_refs, own_ref, other_ref, out_ref = refs
-    y, first = place_ref[0], place_ref[1]
-    for i, rows_ref in enumerate(rows_refs):
-        place = (first ^ i) if len(rows_refs) > 1 else 0
-        if given and i == 0:
-            out_ref[place] = rows_ref[0]
-            continue
-        for half, ref in ((y, own_ref), (1 - y, other_ref)):
-            part = lax.dot_general(
-                rows_ref[...], ref[...], (((1,), (1,)), ((), ())), preferred_element_type=F32
-            )
-            out_ref[place, half] = part.astype(BF16)
-
-
-def project_part(place, rows, own, other, given=False):
-    tokens, channels = rows[-1].shape
-    width = own.shape[0]
-    count = len(rows)
-    return pl.pallas_call(
-        functools.partial(project_kernel, given),
-        out_shape=jax.ShapeDtypeStruct((count, 2, tokens, width), BF16),
-        in_specs=[SMEM] + [VMEM] * (2 + count),
-        out_specs=VMEM,
-        compiler_params=params(),
-        cost_estimate=cost(4 * count * tokens * channels * width, 3 << 20),
-        name="project",
-    )(place, *rows, own, other)
+def project(rows, weight_ref):
+    stacked = jnp.concatenate([r[...] for r in rows], axis=0) if len(rows) > 1 else rows[0][...]
+    product = lax.dot_general(
+        stacked, weight_ref[...], (((1,), (1,)), ((), ())), preferred_element_type=F32
+    ).astype(BF16)
+    tokens = rows[0].shape[0]
+    return [product[i * tokens : (i + 1) * tokens] for i in range(len(rows))]
+
+
+def own_kernel(*refs):
+    *rows_refs, weight_ref, out_ref = refs
+    for i, product in enumerate(project(rows_refs, weight_ref)):
+        out_ref[i] = product
+
+
+def other_kernel(
+    place_ref, zero_ref, one_ref, two_ref, near_own_ref, two_own_ref, weight_ref, near_ref, out_ref
+):
+    y, odd = place_ref[0], place_ref[1]
+    zero, one, two = project([zero_ref, one_ref, two_ref], weight_ref)
+    for i, product in enumerate((zero, one)):
+        near_ref[odd ^ i, y] = near_own_ref[i]
+        near_ref[odd ^ i, 1 - y] = product
+    out_ref[y] = two_own_ref[0]
+    out_ref[1 - y] = two
+
+
+def far_project_kernel(place_ref, two_ref, three_ref, own_ref, other_ref, out_ref):
+    y, odd = place_ref[0], place_ref[1]
+    out_ref[odd] = two_ref[...]
+    for half, ref in ((y, own_ref), (1 - y, other_ref)):
+        out_ref[1 - odd, half] = project([three_ref], ref)[0]
+
+
+def project_part(kernel, name, operands, shapes, flops):
+    out_shape = tuple(jax.ShapeDtypeStruct(shape, BF16) for shape in shapes)
+    return pl.pallas_call(
+        kernel,
+        out_shape=out_shape,
+        in_specs=[SMEM if x.dtype == jnp.int32 else VMEM for x in operands],
+        out_specs=(VMEM,) * len(shapes),
+        compiler_params=params(),
+        cost_estimate=cost(flops, 3 << 20),
+        name=name,
+    )(*operands)
 
 
 def finish_kernel(place_ref, *refs):
@@ -433,7 +450,7 @@
     w_y = permute("weights", after(out_weight, weights), over_y)
     joined = permute("state_half", joined, over_z1, lambda z, y, x, c: z < 2)
     gated = far_part(
-        enter_group, place, near, gate, table, messages + [joined], poles, taps, [weights]
+        enter_group, place, near, gate, table, messages[::-1] + [joined], poles, taps, [weights]
     )
     two = permute("gated_two", gated, over_z1)
     one = permute("gated_one", gated, over_z0)
@@ -449,22 +466,39 @@
             return z ^ far ^ odd_of(z, y, x, c), y, z // 2, z % 2
 
         return [
+            permute(f"straight_{far}", summed, move, lambda z, y, x, c: x == z // 2),
             permute(f"across_{far}", summed, move, lambda z, y, x, c: x != z // 2),
-            permute(f"straight_{far}", summed, move, lambda z, y, x, c: x == z // 2),
         ]
 
     def add_cores(name, kept, sent):
         from_core = permute(name, sent, over_core)
         return (kept.astype(F32) + from_core.astype(F32)).astype(BF16)
 
-    part_two = project_part(place, [two], out_weight, w_y)
-    near = project_part(place, [after(gated, part_two), one], out_weight, w_y)
-    far = project_part(place, [part_two, after(three, near)], out_weight, w_y, given=True)
+    width = out_weight.shape[0]
+    whole, flops = (2, tokens, width), 2 * tokens * channels * width
+    (two_own,) = project_part(own_kernel, "project_two", [two, out_weight], [(1, tokens, width)], flops)
+    (near_own,) = project_part(
+        own_kernel, "project_near", [gated, one, out_weight], [whole], 2 * flops
+    )
+    near, part_two = project_part(
+        other_kernel,
+        "project_other",
+        [place, gated, one, two, near_own, two_own, w_y],
+        [(2,) + whole, whole],
+        3 * flops,
+    )
+    (far,) = project_part(
+        far_project_kernel,
+        "project_far",
+        [place, part_two, three, out_weight, w_y],
+        [(2,) + whole],
+        2 * flops,
+    )
     far_sum = add_cores("core_far", far[0], far[1])
     near = after(near, far_sum)
     near_sum = add_cores("core_near", near[0], near[1])
-    parts = home(far_sum, 2) + home(near_sum, 0)
-    kind = 1 - ((z ^ tp) >> 1)
+    parts = home(near_sum, 0) + home(far_sum, 2)
+    kind = (z ^ tp) >> 1
     return pl.pallas_call(
         finish_kernel,
         out_shape=jax.ShapeDtypeStruct((tokens, 2 * out_weight.shape[0]), BF16),

time: 61.4 us -> 61.4 us (level)
  Pallas kernels: 9.35 us -> 8.06 us
  waiting for transfers between devices: 22.7 us -> 23.4 us
    pallas_call x3 -> x4, Pallas kernels: 4.77 us -> 3.46 us  [project_part(): pl.pallas_call(kernel, out_shape=out_shape, in_specs=[SMEM if x.dtype ==...]
    ppermute x14, waiting for transfers between devices: 22.7 us -> 23.4 us  [permute(): return lax.ppermute(x, AXES, pairs)]
    ppermute x14, starting transfers between devices: 27.5 us -> 28.1 us  [permute(): return lax.ppermute(x, AXES, pairs)]
  transfers between devices with their start and end apart: 14 -> 14, of which waited for: 8 -> 9; matrix products, arithmetic and copies ran while one was open for 0% -> 0% of each run, Pallas kernels for 10% -> 8%
where the time goes in v6:
time: 61.4 us; the launch traced here: 61.2 us
  starting transfers between devices  28.1 us (46%)
  waiting for transfers between devices  23.4 us (38%)
  Pallas kernels  8.06 us (13%)
  local copies, waits for them, and re-layouts  1.25 us (2%)
    ppermute x14, starting transfers between devices, permute(): return lax.ppermute(x, AXES, pairs)  28.1 us
    ppermute x14, waiting for transfers between devices, permute(): return lax.ppermute(x, AXES, pairs)  23.4 us
    pallas_call x4, Pallas kernels, project_part(): pl.pallas_call(kernel, out_shape=out_shape, in_specs=[SMEM if x.dtype ==...  3.46 us
    pallas_call x1, Pallas kernels, near_part(): pl.pallas_call(functools.partial(near_kernel, poles, taps), out_shape=(ja...  1.55 us
  transfers between devices with their start and end apart: 14, of which 9 were waited for; matrix products, arithmetic and copies ran while one was open for 0% of the time, Pallas kernels for 8%

profile of v6, /device:TPU:1, one launch (start us, length us, event | category | flops | bytes accessed | tf_op | source)
XLA Modules:
  0.0 61.2 jit_solution(17367748789677269275)
XLA Ops:
  0.0 0.0 copy-start.4
  0.0 1.2 %slice_bitcast_fusion.3 = (bf16[128,1024]{1,0:T(8,128)(2,1)S(1)}, bf16[128,1024]{1,0:T(8,128)(2,1)S(1)}, bf16[128,1024]{1,0:T(8,128)(2,1)S(1)}) fusion(bf16[128,3,1024]{2,0,1:T(8,128)(2,1)} %param.6), kind=kLoop, calls=%fused_computation.7 | loop fusion | bytes 1572864 | tf_op jit(solution)/shard_map/squeeze | solution.py:435
  1.2 0.0 copy-start
  1.2 0.0 copy-done.1
  1.2 0.0 copy-done.2
  1.2 0.0 copy-done.3
  1.3 0.0 copy-done.4
  1.3 1.1 %signal.1 = (f32[1024,128]{1,0:T(8,128)S(1)}, bf16[224,128]{1,0:T(8,128)(2,1)S(1)}, f32[336,128]{1,0:T(8,128)S(1)}) custom-call(f32[8,128]{1,0:T(8,128)S(1)} %bitcast.27, bf16[128,1024]{1,0:T(8,128)(2,1)S(1)} %get-tuple-element.26.q_ref, bf16[128,1024]{1,0:T(8,128)(2,1)S(1)} %get-tuple-element.27.k_ref, bf16[128,1024]{1,0:T(8,128)(2,1)S(1)} %get-tuple-element.25.v_ref, ...), custom_call_target="tpu_custom_call" | custom-call | flops 4194304 | bytes 2097152 | tf_op jit(solution)/shard_map/signal/pallas_call | solution.py:123
  2.4 3.1 %collective-permute-start = (bf16[224,128]{1,0:T(8,128)(2,1)S(1)}, bf16[224,128]{1,0:T(8,128)(2,1)S(1)}, u32[]{:S(2)}, u32[]{:S(2)}) collective-permute-start(bf16[224,128]{1,0:T(8,128)(2,1)S(1)} %get-tuple-element.19.refs_3_), channel_id=1, source_target_pairs={{0,12},{1,13},{2,14},{3,15},{4,8},{5,9},{6,10},{7,11},{8,4},{9,5},... | collective-permute-start | bytes 172040 | tf_op jit(solution)/shard_map/state_zy/ppermute | solution.py:410
  5.5 0.2 collective-permute-start.1
  5.7 0.2 collective-permute-start.2
  5.9 1.2 %collective-permute-done.refs_0_ = bf16[224,128]{1,0:T(8,128)(2,1)S(1)} collective-permute-done((bf16[224,128]{1,0:T(8,128)(2,1)S(1)}, bf16[224,128]{1,0:T(8,128)(2,1)S(1)}, u32[]{:S(2)}, u32[]{:S(2)}) %collective-permute-start) | collective-permute-done | bytes 57376 | tf_op jit(solution)/shard_map/state_zy/ppermute | solution.py:410
  7.1 1.9 %collective-permute-done.1.refs_1_ = bf16[224,128]{1,0:T(8,128)(2,1)S(1)} collective-permute-done((bf16[224,128]{1,0:T(8,128)(2,1)S(1)}, bf16[224,128]{1,0:T(8,128)(2,1)S(1)}, u32[]{:S(2)}, u32[]{:S(2)}) %collective-permute-start.1) | collective-permute-done | bytes 57376 | tf_op jit(solution)/shard_map/state_z/ppermute | solution.py:410
  9.0 0.0 collective-permute-done.2.refs_2_
  9.0 0.1 join_state.1
  9.2 0.1 state_weights.1.refs_5_
  9.2 0.4 collective-permute-start.6
  9.7 4.4 %collective-permute-start.3 = (bf16[224,128]{1,0:T(8,128)(2,1)S(1)}, bf16[224,128]{1,0:T(8,128)(2,1)S(1)}, u32[]{:S(2)}, u32[]{:S(2)}) collective-permute-start(bf16[224,128]{1,0:T(8,128)(2,1)S(1)} %join_state.1), channel_id=1, source_target_pairs={{0,16},{1,17},{2,18},{3,19},{4,20},{5,21},{6,22},{7,23},{8,24},{9,... | collective-permute-start | bytes 172040 | tf_op jit(solution)/shard_map/state_half/ppermute | solution.py:410
  14.0 1.5 %near_filter.1 = (bf16[128,1024]{1,0:T(8,128)(2,1)S(1)}, f32[128,1024]{1,0:T(8,128)S(1)}) custom-call(bf16[128,1024]{1,0:T(8,128)(2,1)S(1)} %get-tuple-element.26.q_ref, f32[1024,128]{1,0:T(8,128)S(1)} %get-tuple-element.15.signal_ref, f32[336,128]{1,0:T(8,128)S(1)} %get-tuple-element.20.table_ref.refs_4_), custom_call_target="tpu_custom_call" | custom-call | flops 8388608 | bytes 2097152 | tf_op jit(solution)/shard_map/near_filter/pallas_call | solution.py:141
  15.6 0.0 collective-permute-done.3.refs_4_
  15.6 1.0 %far_filter.1.refs_0_.zero_ref = bf16[128,1024]{1,0:T(8,128)(2,1)S(1)} custom-call(s32[1]{0:T(128)} %bitcast.3.place_ref, bf16[128,1024]{1,0:T(8,128)(2,1)S(1)} %get-tuple-element.17.near_ref, f32[128,1024]{1,0:T(8,128)S(1)} %get-tuple-element.18.gate_ref, f32[336,128]{1,0:T(8,128)S(1)} %get-tuple-element.20.table_ref.refs_4_, ...), custom_call_target="tpu_custom_call" | custom-call | flops 8388608 | bytes 3145728 | tf_op jit(solution)/shard_map/far_filter/pallas_call | solution.py:331
  16.6 2.5 %collective-permute-start.5 = (bf16[128,1024]{1,0:T(8,128)(2,1)S(1)}, bf16[128,1024]{1,0:T(8,128)(2,1)S(1)}, u32[]{:S(2)}, u32[]{:S(2)}) collective-permute-start(bf16[128,1024]{1,0:T(8,128)(2,1)S(1)} %far_filter.1.refs_0_.zero_ref), channel_id=1, source_target_pairs={{0,16},{1,17},{2,18},{3,19},{4,20},{5,21},{6,22},{7,23},{8,24},{9,... | collective-permute-start | bytes 786440 | tf_op jit(solution)/shard_map/gated_two/ppermute | solution.py:410
  19.0 1.7 %collective-permute-start.4 = (bf16[128,1024]{1,0:T(8,128)(2,1)S(1)}, bf16[128,1024]{1,0:T(8,128)(2,1)S(1)}, u32[]{:S(2)}, u32[]{:S(2)}) collective-permute-start(bf16[128,1024]{1,0:T(8,128)(2,1)S(1)} %far_filter.1.refs_0_.zero_ref), channel_id=1, source_target_pairs={{0,8},{1,9},{2,10},{3,11},{4,12},{5,13},{6,14},{7,15},{8,0},{9,1},... | collective-permute-start | bytes 786440 | tf_op jit(solution)/shard_map/gated_one/ppermute | solution.py:410
  20.8 8.2 %collective-permute-done.5.refs_0_.two_ref = bf16[128,1024]{1,0:T(8,128)(2,1)S(1)} collective-permute-done((bf16[128,1024]{1,0:T(8,128)(2,1)S(1)}, bf16[128,1024]{1,0:T(8,128)(2,1)S(1)}, u32[]{:S(2)}, u32[]{:S(2)}) %collective-permute-start.5) | collective-permute-done | bytes 262176 | tf_op jit(solution)/shard_map/gated_two/ppermute | solution.py:410
  29.0 1.7 %collective-permute-start.7 = (bf16[128,1024]{1,0:T(8,128)(2,1)S(1)}, bf16[128,1024]{1,0:T(8,128)(2,1)S(1)}, u32[]{:S(2)}, u32[]{:S(2)}) collective-permute-start(bf16[128,1024]{1,0:T(8,128)(2,1)S(1)} %collective-permute-done.5.refs_0_.two_ref), channel_id=1, source_target_pairs={{0,8},{1,9},{2,10},{3,11},{4,12},{5,13},{6,14},{7,15},{8,0},{9,1},... | collective-permute-start | bytes 786440 | tf_op jit(solution)/shard_map/gated_three/ppermute | solution.py:410
  30.7 0.1 pad_add_fusion.place_ref
  30.8 0.5 project_two.1.two_own_ref
  31.3 0.0 collective-permute-done.4.refs_1_.one_ref
  31.3 0.5 project_near.1.near_own_ref
  31.8 0.1 collective-permute-done.6.weight_ref.other_ref
  31.9 1.1 %project_other.1 = (bf16[2,2,128,512]{3,2,1,0:T(8,128)(2,1)S(1)}, bf16[2,128,512]{2,1,0:T(8,128)(2,1)S(1)}) custom-call(s32[2]{0:T(128)S(1)} %pad_add_fusion.place_ref, bf16[128,1024]{1,0:T(8,128)(2,1)S(1)} %far_filter.1.refs_0_.zero_ref, bf16[128,1024]{1,0:T(8,128)(2,1)S(1)} %collective-permute-done.4.refs_1_.one_ref, ...), custom_call_target="tpu_custom_call" | custom-call | flops 402653184 | bytes 3145728 | tf_op jit(solution)/shard_map/project_other/pallas_call | solution.py:379
  33.0 1.7 %collective-permute-done.7.three_ref = bf16[128,1024]{1,0:T(8,128)(2,1)S(1)} collective-permute-done((bf16[128,1024]{1,0:T(8,128)(2,1)S(1)}, bf16[128,1024]{1,0:T(8,128)(2,1)S(1)}, u32[]{:S(2)}, u32[]{:S(2)}) %collective-permute-start.7) | collective-permute-done | bytes 262176 | tf_op jit(solution)/shard_map/gated_three/ppermute | solution.py:410
  34.7 1.4 %project_far.1 = bf16[2,2,128,512]{3,2,1,0:T(8,128)(2,1)S(1)} custom-call(s32[2]{0:T(128)S(1)} %pad_add_fusion.place_ref, bf16[2,128,512]{2,1,0:T(8,128)(2,1)S(1)} %get-tuple-element.23.two_ref, bf16[128,1024]{1,0:T(8,128)(2,1)S(1)} %collective-permute-done.7.three_ref, bf16[512,1024]{1,0:T(8,128)(2,1)S(1)} %copy-done, ...), custom_call_target="tpu_custom_call" | custom-call | flops 268435456 | bytes 3145728 | tf_op jit(solution)/shard_map/project_far/pallas_call | solution.py:379
  36.1 3.8 %collective-permute-start.8 = (bf16[2,128,512]{2,1,0:T(8,128)(2,1)S(1)}, bf16[2,128,512]{2,1,0:T(8,128)(2,1)S(1)}, u32[]{:S(2)}, u32[]{:S(2)}) collective-permute-start(bf16[2,128,512]{2,1,0:T(8,128)(2,1)S(1)} %slice_bitcast_fusion), channel_id=1, source_target_pairs={{0,1},{1,0},{2,3},{3,2},{4,5},{5,4},{6,7},{7,6},{8,9},{9,8},{10,11... | collective-permute-start | bytes 786440 | tf_op jit(solution)/shard_map/core_far/ppermute | solution.py:410
  39.9 1.2 %collective-permute-done.8 = bf16[2,128,512]{2,1,0:T(8,128)(2,1)S(1)} collective-permute-done((bf16[2,128,512]{2,1,0:T(8,128)(2,1)S(1)}, bf16[2,128,512]{2,1,0:T(8,128)(2,1)S(1)}, u32[]{:S(2)}, u32[]{:S(2)}) %collective-permute-start.8) | collective-permute-done | bytes 262176 | tf_op jit(solution)/shard_map/core_far/ppermute | solution.py:410
  41.0 0.1 fusion.1
  41.1 0.4 collective-permute-start.9
  41.6 5.8 %collective-permute-start.12 = (bf16[2,128,512]{2,1,0:T(8,128)(2,1)S(1)}, bf16[2,128,512]{2,1,0:T(8,128)(2,1)S(1)}, u32[]{:S(2)}, u32[]{:S(2)}) collective-permute-start(bf16[2,128,512]{2,1,0:T(8,128)(2,1)S(1)} %fusion.1), channel_id=1, source_target_pairs={{0,16},{1,24},{4,20},{5,28},{8,17},{9,25},{12,21},{13,29},{18,2},{... | collective-permute-start | bytes 786440 | tf_op jit(solution)/shard_map/straight_2/ppermute | solution.py:410
  47.4 0.7 %collective-permute-start.13 = (bf16[2,128,512]{2,1,0:T(8,128)(2,1)S(1)}, bf16[2,128,512]{2,1,0:T(8,128)(2,1)S(1)}, u32[]{:S(2)}, u32[]{:S(2)}) collective-permute-start(bf16[2,128,512]{2,1,0:T(8,128)(2,1)S(1)} %fusion.1), channel_id=1, source_target_pairs={{2,16},{3,24},{6,20},{7,28},{10,17},{11,25},{14,21},{15,29},{16,2}... | collective-permute-start | bytes 786440 | tf_op jit(solution)/shard_map/across_2/ppermute | solution.py:410
  48.0 0.0 collective-permute-done.9
  48.1 0.1 fusion
  48.1 1.9 %collective-permute-start.10 = (bf16[2,128,512]{2,1,0:T(8,128)(2,1)S(1)}, bf16[2,128,512]{2,1,0:T(8,128)(2,1)S(1)}, u32[]{:S(2)}, u32[]{:S(2)}) collective-permute-start(bf16[2,128,512]{2,1,0:T(8,128)(2,1)S(1)} %fusion), channel_id=1, source_target_pairs={{0,0},{1,8},{4,4},{5,12},{8,1},{9,9},{12,5},{13,13},{18,18},{19,26... | collective-permute-start | bytes 786440 | tf_op jit(solution)/shard_map/straight_0/ppermute | solution.py:410
  50.1 1.3 %collective-permute-start.11 = (bf16[2,128,512]{2,1,0:T(8,128)(2,1)S(1)}, bf16[2,128,512]{2,1,0:T(8,128)(2,1)S(1)}, u32[]{:S(2)}, u32[]{:S(2)}) collective-permute-start(bf16[2,128,512]{2,1,0:T(8,128)(2,1)S(1)} %fusion), channel_id=1, source_target_pairs={{2,0},{3,8},{6,4},{7,12},{10,1},{11,9},{14,5},{15,13},{16,18},{17,... | collective-permute-start | bytes 786440 | tf_op jit(solution)/shard_map/across_0/ppermute | solution.py:410
  51.4 1.5 %collective-permute-done.12.refs_2_ = bf16[2,128,512]{2,1,0:T(8,128)(2,1)S(1)} collective-permute-done((bf16[2,128,512]{2,1,0:T(8,128)(2,1)S(1)}, bf16[2,128,512]{2,1,0:T(8,128)(2,1)S(1)}, u32[]{:S(2)}, u32[]{:S(2)}) %collective-permute-start.12) | collective-permute-done | bytes 262176 | tf_op jit(solution)/shard_map/straight_2/ppermute | solution.py:410
  52.9 0.0 collective-permute-done.13.refs_3_
  52.9 6.4 %collective-permute-done.10.refs_0_ = bf16[2,128,512]{2,1,0:T(8,128)(2,1)S(1)} collective-permute-done((bf16[2,128,512]{2,1,0:T(8,128)(2,1)S(1)}, bf16[2,128,512]{2,1,0:T(8,128)(2,1)S(1)}, u32[]{:S(2)}, u32[]{:S(2)}) %collective-permute-start.10) | collective-permute-done | bytes 262176 | tf_op jit(solution)/shard_map/straight_0/ppermute | solution.py:410
  59.3 1.2 %collective-permute-done.11.refs_1_ = bf16[2,128,512]{2,1,0:T(8,128)(2,1)S(1)} collective-permute-done((bf16[2,128,512]{2,1,0:T(8,128)(2,1)S(1)}, bf16[2,128,512]{2,1,0:T(8,128)(2,1)S(1)}, u32[]{:S(2)}, u32[]{:S(2)}) %collective-permute-start.11) | collective-permute-done | bytes 262176 | tf_op jit(solution)/shard_map/across_0/ppermute | solution.py:410
  60.5 0.8 %finish.1 = bf16[128,1024]{1,0:T(8,128)(2,1)} custom-call(s32[1]{0:T(128)} %bitcast.place_ref, bf16[2,128,512]{2,1,0:T(8,128)(2,1)S(1)} %collective-permute-done.10.refs_0_, bf16[2,128,512]{2,1,0:T(8,128)(2,1)S(1)} %collective-permute-done.11.refs_1_, bf16[2,128,512]{2,1,0:T(8,128)(2,1)S(1)} %collective-permute-done.12.refs_2_, ...), custom_call_target="tpu_custom_call" | custom-call | flops 262144 | bytes 2097152 | tf_op jit(solution)/shard_map/finish/pallas_call | solution.py:502
  (6 shorter events, 0.0 us)
Async XLA Ops:
  0.0 1.2 %copy-start.1 = (f32[1024,16]{0,1:T(8,128)S(1)}, f32[1024,16]{0,1:T(8,128)}, u32[]{:S(2)}) copy-start(f32[1024,16]{0,1:T(8,128)} %param.8) | copy-start | bytes 196612
  0.0 1.2 %copy-start.2 = (f32[1024,16]{0,1:T(8,128)S(1)}, f32[1024,16]{0,1:T(8,128)}, u32[]{:S(2)}) copy-start(f32[1024,16]{0,1:T(8,128)} %param.9) | copy-start | bytes 196612
  0.0 1.2 %copy-start.3 = (bf16[3,3,1024]{2,1,0:T(4,128)(2,1)S(1)}, bf16[3,3,1024]{2,1,0:T(4,128)(2,1)}, u32[]{:S(2)}) copy-start(bf16[3,3,1024]{2,1,0:T(4,128)(2,1)} %taps_ref.1) | copy-start | bytes 55300
  0.0 1.3 %copy-start.4 = (f32[1024]{0:T(1024)S(1)}, f32[1024]{0:T(1024)}, u32[]{:S(2)}) copy-start(f32[1024]{0:T(1024)} %param.10) | copy-start | bytes 12292
  1.2 8.0 %copy-start = (bf16[512,1024]{1,0:T(8,128)(2,1)S(1)}, bf16[512,1024]{1,0:T(8,128)(2,1)}, u32[]{:S(2)}) copy-start(bf16[512,1024]{1,0:T(8,128)(2,1)} %own_ref.1) | copy-start | bytes 3145732
  2.4 4.7 %collective-permute-start = (bf16[224,128]{1,0:T(8,128)(2,1)S(1)}, bf16[224,128]{1,0:T(8,128)(2,1)S(1)}, u32[]{:S(2)}, u32[]{:S(2)}) collective-permute-start(bf16[224,128]{1,0:T(8,128)(2,1)S(1)} %get-tuple-element.19.refs_3_), channel_id=1, source_target_pairs={{0,12},{1,13},{2,14},{3,15},{4,8},{5,9},{6,10},{7,11},{8,4},{9,5},... | collective-permute-start | bytes 172040 | tf_op jit(solution)/shard_map/state_zy/ppermute | solution.py:410
  5.5 3.5 %collective-permute-start.1 = (bf16[224,128]{1,0:T(8,128)(2,1)S(1)}, bf16[224,128]{1,0:T(8,128)(2,1)S(1)}, u32[]{:S(2)}, u32[]{:S(2)}) collective-permute-start(bf16[224,128]{1,0:T(8,128)(2,1)S(1)} %get-tuple-element.19.refs_3_), channel_id=1, source_target_pairs={{0,8},{1,9},{2,10},{3,11},{4,12},{5,13},{6,14},{7,15},{8,0},{9,1},... | collective-permute-start | bytes 172040 | tf_op jit(solution)/shard_map/state_z/ppermute | solution.py:410
  5.7 3.3 %collective-permute-start.2 = (bf16[224,128]{1,0:T(8,128)(2,1)S(1)}, bf16[224,128]{1,0:T(8,128)(2,1)S(1)}, u32[]{:S(2)}, u32[]{:S(2)}) collective-permute-start(bf16[224,128]{1,0:T(8,128)(2,1)S(1)} %get-tuple-element.19.refs_3_), channel_id=1, source_target_pairs={{0,4},{1,5},{2,6},{3,7},{4,0},{5,1},{6,2},{7,3},{8,12},{9,13},{10,... | collective-permute-start | bytes 172040 | tf_op jit(solution)/shard_map/state_y/ppermute | solution.py:410
  9.2 22.6 %collective-permute-start.6 = (bf16[512,1024]{1,0:T(8,128)(2,1)S(1)}, bf16[512,1024]{1,0:T(8,128)(2,1)S(1)}, u32[]{:S(2)}, u32[]{:S(2)}) collective-permute-start(bf16[512,1024]{1,0:T(8,128)(2,1)S(1)} %copy-done), channel_id=1, source_target_pairs={{0,4},{1,5},{2,6},{3,7},{4,0},{5,1},{6,2},{7,3},{8,12},{9,13},{10,... | collective-permute-start | bytes 3145736 | tf_op jit(solution)/shard_map/weights/ppermute | solution.py:410
  9.7 5.9 %collective-permute-start.3 = (bf16[224,128]{1,0:T(8,128)(2,1)S(1)}, bf16[224,128]{1,0:T(8,128)(2,1)S(1)}, u32[]{:S(2)}, u32[]{:S(2)}) collective-permute-start(bf16[224,128]{1,0:T(8,128)(2,1)S(1)} %join_state.1), channel_id=1, source_target_pairs={{0,16},{1,17},{2,18},{3,19},{4,20},{5,21},{6,22},{7,23},{8,24},{9,... | collective-permute-start | bytes 172040 | tf_op jit(solution)/shard_map/state_half/ppermute | solution.py:410
  16.6 12.4 %collective-permute-start.5 = (bf16[128,1024]{1,0:T(8,128)(2,1)S(1)}, bf16[128,1024]{1,0:T(8,128)(2,1)S(1)}, u32[]{:S(2)}, u32[]{:S(2)}) collective-permute-start(bf16[128,1024]{1,0:T(8,128)(2,1)S(1)} %far_filter.1.refs_0_.zero_ref), channel_id=1, source_target_pairs={{0,16},{1,17},{2,18},{3,19},{4,20},{5,21},{6,22},{7,23},{8,24},{9,... | collective-permute-start | bytes 786440 | tf_op jit(solution)/shard_map/gated_two/ppermute | solution.py:410
  19.0 12.2 %collective-permute-start.4 = (bf16[128,1024]{1,0:T(8,128)(2,1)S(1)}, bf16[128,1024]{1,0:T(8,128)(2,1)S(1)}, u32[]{:S(2)}, u32[]{:S(2)}) collective-permute-start(bf16[128,1024]{1,0:T(8,128)(2,1)S(1)} %far_filter.1.refs_0_.zero_ref), channel_id=1, source_target_pairs={{0,8},{1,9},{2,10},{3,11},{4,12},{5,13},{6,14},{7,15},{8,0},{9,1},... | collective-permute-start | bytes 786440 | tf_op jit(solution)/shard_map/gated_one/ppermute | solution.py:410
  29.0 5.7 %collective-permute-start.7 = (bf16[128,1024]{1,0:T(8,128)(2,1)S(1)}, bf16[128,1024]{1,0:T(8,128)(2,1)S(1)}, u32[]{:S(2)}, u32[]{:S(2)}) collective-permute-start(bf16[128,1024]{1,0:T(8,128)(2,1)S(1)} %collective-permute-done.5.refs_0_.two_ref), channel_id=1, source_target_pairs={{0,8},{1,9},{2,10},{3,11},{4,12},{5,13},{6,14},{7,15},{8,0},{9,1},... | collective-permute-start | bytes 786440 | tf_op jit(solution)/shard_map/gated_three/ppermute | solution.py:410
  36.1 5.0 %collective-permute-start.8 = (bf16[2,128,512]{2,1,0:T(8,128)(2,1)S(1)}, bf16[2,128,512]{2,1,0:T(8,128)(2,1)S(1)}, u32[]{:S(2)}, u32[]{:S(2)}) collective-permute-start(bf16[2,128,512]{2,1,0:T(8,128)(2,1)S(1)} %slice_bitcast_fusion), channel_id=1, source_target_pairs={{0,1},{1,0},{2,3},{3,2},{4,5},{5,4},{6,7},{7,6},{8,9},{9,8},{10,11... | collective-permute-start | bytes 786440 | tf_op jit(solution)/shard_map/core_far/ppermute | solution.py:410
  41.1 6.9 %collective-permute-start.9 = (bf16[2,128,512]{2,1,0:T(8,128)(2,1)S(1)}, bf16[2,128,512]{2,1,0:T(8,128)(2,1)S(1)}, u32[]{:S(2)}, u32[]{:S(2)}) collective-permute-start(bf16[2,128,512]{2,1,0:T(8,128)(2,1)S(1)} %slice_bitcast_fusion.2), channel_id=1, source_target_pairs={{0,1},{1,0},{2,3},{3,2},{4,5},{5,4},{6,7},{7,6},{8,9},{9,8},{10,11... | collective-permute-start | bytes 786440 | tf_op jit(solution)/shard_map/core_near/ppermute | solution.py:410
  41.6 11.3 %collective-permute-start.12 = (bf16[2,128,512]{2,1,0:T(8,128)(2,1)S(1)}, bf16[2,128,512]{2,1,0:T(8,128)(2,1)S(1)}, u32[]{:S(2)}, u32[]{:S(2)}) collective-permute-start(bf16[2,128,512]{2,1,0:T(8,128)(2,1)S(1)} %fusion.1), channel_id=1, source_target_pairs={{0,16},{1,24},{4,20},{5,28},{8,17},{9,25},{12,21},{13,29},{18,2},{... | collective-permute-start | bytes 786440 | tf_op jit(solution)/shard_map/straight_2/ppermute | solution.py:410
  47.4 5.5 %collective-permute-start.13 = (bf16[2,128,512]{2,1,0:T(8,128)(2,1)S(1)}, bf16[2,128,512]{2,1,0:T(8,128)(2,1)S(1)}, u32[]{:S(2)}, u32[]{:S(2)}) collective-permute-start(bf16[2,128,512]{2,1,0:T(8,128)(2,1)S(1)} %fusion.1), channel_id=1, source_target_pairs={{2,16},{3,24},{6,20},{7,28},{10,17},{11,25},{14,21},{15,29},{16,2}... | collective-permute-start | bytes 786440 | tf_op jit(solution)/shard_map/across_2/ppermute | solution.py:410
  48.1 11.2 %collective-permute-start.10 = (bf16[2,128,512]{2,1,0:T(8,128)(2,1)S(1)}, bf16[2,128,512]{2,1,0:T(8,128)(2,1)S(1)}, u32[]{:S(2)}, u32[]{:S(2)}) collective-permute-start(bf16[2,128,512]{2,1,0:T(8,128)(2,1)S(1)} %fusion), channel_id=1, source_target_pairs={{0,0},{1,8},{4,4},{5,12},{8,1},{9,9},{12,5},{13,13},{18,18},{19,26... | collective-permute-start | bytes 786440 | tf_op jit(solution)/shard_map/straight_0/ppermute | solution.py:410
  50.1 10.4 %collective-permute-start.11 = (bf16[2,128,512]{2,1,0:T(8,128)(2,1)S(1)}, bf16[2,128,512]{2,1,0:T(8,128)(2,1)S(1)}, u32[]{:S(2)}, u32[]{:S(2)}) collective-permute-start(bf16[2,128,512]{2,1,0:T(8,128)(2,1)S(1)} %fusion), channel_id=1, source_target_pairs={{2,0},{3,8},{6,4},{7,12},{10,1},{11,9},{14,5},{15,13},{16,18},{17,... | collective-permute-start | bytes 786440 | tf_op jit(solution)/shard_map/across_0/ppermute | solution.py:410

commit v7 on v6

--- a/solution.py
+++ b/solution.py
@@ -105,6 +105,10 @@
         out_ref[:, lanes] = (gate * conv).astype(BF16)
 
 
+def folded_shape(tokens, fold):
+    return ((tokens + 1) * fold, LANES)
+
+
 def tree_sum(values):
     values = list(values)
     while len(values) > 1:
@@ -123,7 +127,7 @@
     return pl.pallas_call(
         signal_kernel,
         out_shape=(
-            jax.ShapeDtypeStruct((tokens * fold, LANES), F32),
+            jax.ShapeDtypeStruct(folded_shape(tokens, fold), F32),
             jax.ShapeDtypeStruct((message_rows, LANES), BF16),
             jax.ShapeDtypeStruct((table_rows, LANES), F32),
         ),
@@ -333,7 +337,7 @@
         out_shape=jax.ShapeDtypeStruct((tokens, channels), BF16),
         in_specs=[SMEM] + [VMEM] * (3 + count + len(weights)),
         out_specs=VMEM,
-        scratch_shapes=[pltpu.VMEM((tokens * fold, LANES), F32)],
+        scratch_shapes=[pltpu.VMEM(folded_shape(tokens, fold), F32)],
         compiler_params=params(),
         cost_estimate=cost(4 * tokens * channels * poles, 3 << 20),
         name="far_filter",

time: 61.4 us -> 61.4 us (level)
  transfers between devices with their start and end apart: 14 -> 14, of which waited for: 9 -> 9; matrix products, arithmetic and copies ran while one was open for 0% -> 0% of each run, Pallas kernels for 8% -> 7%
where the time goes in v7:
time: 61.4 us; the launch traced here: 61.2 us
  starting transfers between devices  28.2 us (46%)
  waiting for transfers between devices  23.4 us (38%)
  Pallas kernels  8.01 us (13%)
  local copies, waits for them, and re-layouts  1.25 us (2%)
    ppermute x14, starting transfers between devices, permute(): return lax.ppermute(x, AXES, pairs)  28.2 us
    ppermute x14, waiting for transfers between devices, permute(): return lax.ppermute(x, AXES, pairs)  23.4 us
    pallas_call x4, Pallas kernels, project_part(): pl.pallas_call(kernel, out_shape=out_shape, in_specs=[SMEM if x.dtype ==...  3.46 us
    pallas_call x1, Pallas kernels, near_part(): pl.pallas_call(functools.partial(near_kernel, poles, taps), out_shape=(ja...  1.52 us
  transfers between devices with their start and end apart: 14, of which 9 were waited for; matrix products, arithmetic and copies ran while one was open for 0% of the time, Pallas kernels for 7%

profile of v7, /device:TPU:1, one launch (start us, length us, event | category | flops | bytes accessed | tf_op | source)
XLA Modules:
  0.0 61.2 jit_solution(8396414209864470001)
XLA Ops:
  0.0 1.2 %slice_bitcast_fusion.3 = (bf16[128,1024]{1,0:T(8,128)(2,1)S(1)}, bf16[128,1024]{1,0:T(8,128)(2,1)S(1)}, bf16[128,1024]{1,0:T(8,128)(2,1)S(1)}) fusion(bf16[128,3,1024]{2,0,1:T(8,128)(2,1)} %param.6), kind=kLoop, calls=%fused_computation.7 | loop fusion | bytes 1572864 | tf_op jit(solution)/shard_map/squeeze | solution.py:439
  1.2 0.0 copy-start
  1.2 0.0 copy-done.1
  1.2 0.0 copy-done.2
  1.2 0.0 copy-done.3
  1.3 0.0 copy-done.4
  1.3 1.1 %signal.1 = (f32[1032,128]{1,0:T(8,128)S(1)}, bf16[224,128]{1,0:T(8,128)(2,1)S(1)}, f32[336,128]{1,0:T(8,128)S(1)}) custom-call(f32[8,128]{1,0:T(8,128)S(1)} %bitcast.27, bf16[128,1024]{1,0:T(8,128)(2,1)S(1)} %get-tuple-element.26.q_ref, bf16[128,1024]{1,0:T(8,128)(2,1)S(1)} %get-tuple-element.27.k_ref, bf16[128,1024]{1,0:T(8,128)(2,1)S(1)} %get-tuple-element.25.v_ref, ...), custom_call_target="tpu_custom_call" | custom-call | flops 4194304 | bytes 2097152 | tf_op jit(solution)/shard_map/signal/pallas_call | solution.py:127
  2.4 3.1 %collective-permute-start = (bf16[224,128]{1,0:T(8,128)(2,1)S(1)}, bf16[224,128]{1,0:T(8,128)(2,1)S(1)}, u32[]{:S(2)}, u32[]{:S(2)}) collective-permute-start(bf16[224,128]{1,0:T(8,128)(2,1)S(1)} %get-tuple-element.19.refs_3_), channel_id=1, source_target_pairs={{0,12},{1,13},{2,14},{3,15},{4,8},{5,9},{6,10},{7,11},{8,4},{9,5},... | collective-permute-start | bytes 172040 | tf_op jit(solution)/shard_map/state_zy/ppermute | solution.py:414
  5.5 0.2 collective-permute-start.1
  5.7 0.2 collective-permute-start.2
  5.9 1.2 %collective-permute-done.refs_0_ = bf16[224,128]{1,0:T(8,128)(2,1)S(1)} collective-permute-done((bf16[224,128]{1,0:T(8,128)(2,1)S(1)}, bf16[224,128]{1,0:T(8,128)(2,1)S(1)}, u32[]{:S(2)}, u32[]{:S(2)}) %collective-permute-start) | collective-permute-done | bytes 57376 | tf_op jit(solution)/shard_map/state_zy/ppermute | solution.py:414
  7.1 1.9 %collective-permute-done.1.refs_1_ = bf16[224,128]{1,0:T(8,128)(2,1)S(1)} collective-permute-done((bf16[224,128]{1,0:T(8,128)(2,1)S(1)}, bf16[224,128]{1,0:T(8,128)(2,1)S(1)}, u32[]{:S(2)}, u32[]{:S(2)}) %collective-permute-start.1) | collective-permute-done | bytes 57376 | tf_op jit(solution)/shard_map/state_z/ppermute | solution.py:414
  9.0 0.0 collective-permute-done.2.refs_2_
  9.0 0.1 join_state.1
  9.2 0.1 state_weights.1.refs_5_
  9.2 0.0 copy-done
  9.2 0.4 collective-permute-start.6
  9.7 4.4 %collective-permute-start.3 = (bf16[224,128]{1,0:T(8,128)(2,1)S(1)}, bf16[224,128]{1,0:T(8,128)(2,1)S(1)}, u32[]{:S(2)}, u32[]{:S(2)}) collective-permute-start(bf16[224,128]{1,0:T(8,128)(2,1)S(1)} %join_state.1), channel_id=1, source_target_pairs={{0,16},{1,17},{2,18},{3,19},{4,20},{5,21},{6,22},{7,23},{8,24},{9,... | collective-permute-start | bytes 172040 | tf_op jit(solution)/shard_map/state_half/ppermute | solution.py:414
  14.0 1.5 %near_filter.1 = (bf16[128,1024]{1,0:T(8,128)(2,1)S(1)}, f32[128,1024]{1,0:T(8,128)S(1)}) custom-call(bf16[128,1024]{1,0:T(8,128)(2,1)S(1)} %get-tuple-element.26.q_ref, f32[1032,128]{1,0:T(8,128)S(1)} %get-tuple-element.15.signal_ref, f32[336,128]{1,0:T(8,128)S(1)} %get-tuple-element.20.table_ref.refs_4_), custom_call_target="tpu_custom_call" | custom-call | flops 8388608 | bytes 2097152 | tf_op jit(solution)/shard_map/near_filter/pallas_call | solution.py:145
  15.6 0.0 collective-permute-done.3.refs_4_
  15.6 1.0 %far_filter.1.refs_0_.zero_ref = bf16[128,1024]{1,0:T(8,128)(2,1)S(1)} custom-call(s32[1]{0:T(128)} %bitcast.3.place_ref, bf16[128,1024]{1,0:T(8,128)(2,1)S(1)} %get-tuple-element.17.near_ref, f32[128,1024]{1,0:T(8,128)S(1)} %get-tuple-element.18.gate_ref, f32[336,128]{1,0:T(8,128)S(1)} %get-tuple-element.20.table_ref.refs_4_, ...), custom_call_target="tpu_custom_call" | custom-call | flops 8388608 | bytes 3145728 | tf_op jit(solution)/shard_map/far_filter/pallas_call | solution.py:335
  16.5 2.5 %collective-permute-start.5 = (bf16[128,1024]{1,0:T(8,128)(2,1)S(1)}, bf16[128,1024]{1,0:T(8,128)(2,1)S(1)}, u32[]{:S(2)}, u32[]{:S(2)}) collective-permute-start(bf16[128,1024]{1,0:T(8,128)(2,1)S(1)} %far_filter.1.refs_0_.zero_ref), channel_id=1, source_target_pairs={{0,16},{1,17},{2,18},{3,19},{4,20},{5,21},{6,22},{7,23},{8,24},{9,... | collective-permute-start | bytes 786440 | tf_op jit(solution)/shard_map/gated_two/ppermute | solution.py:414
  19.0 1.7 %collective-permute-start.4 = (bf16[128,1024]{1,0:T(8,128)(2,1)S(1)}, bf16[128,1024]{1,0:T(8,128)(2,1)S(1)}, u32[]{:S(2)}, u32[]{:S(2)}) collective-permute-start(bf16[128,1024]{1,0:T(8,128)(2,1)S(1)} %far_filter.1.refs_0_.zero_ref), channel_id=1, source_target_pairs={{0,8},{1,9},{2,10},{3,11},{4,12},{5,13},{6,14},{7,15},{8,0},{9,1},... | collective-permute-start | bytes 786440 | tf_op jit(solution)/shard_map/gated_one/ppermute | solution.py:414
  20.8 8.2 %collective-permute-done.5.refs_0_.two_ref = bf16[128,1024]{1,0:T(8,128)(2,1)S(1)} collective-permute-done((bf16[128,1024]{1,0:T(8,128)(2,1)S(1)}, bf16[128,1024]{1,0:T(8,128)(2,1)S(1)}, u32[]{:S(2)}, u32[]{:S(2)}) %collective-permute-start.5) | collective-permute-done | bytes 262176 | tf_op jit(solution)/shard_map/gated_two/ppermute | solution.py:414
  29.0 1.7 %collective-permute-start.7 = (bf16[128,1024]{1,0:T(8,128)(2,1)S(1)}, bf16[128,1024]{1,0:T(8,128)(2,1)S(1)}, u32[]{:S(2)}, u32[]{:S(2)}) collective-permute-start(bf16[128,1024]{1,0:T(8,128)(2,1)S(1)} %collective-permute-done.5.refs_0_.two_ref), channel_id=1, source_target_pairs={{0,8},{1,9},{2,10},{3,11},{4,12},{5,13},{6,14},{7,15},{8,0},{9,1},... | collective-permute-start | bytes 786440 | tf_op jit(solution)/shard_map/gated_three/ppermute | solution.py:414
  30.7 0.1 pad_add_fusion.place_ref
  30.8 0.5 project_two.1.two_own_ref
  31.3 0.0 collective-permute-done.4.refs_1_.one_ref
  31.3 0.5 project_near.1.near_own_ref
  31.8 0.1 collective-permute-done.6.weight_ref.other_ref
  31.9 1.1 %project_other.1 = (bf16[2,2,128,512]{3,2,1,0:T(8,128)(2,1)S(1)}, bf16[2,128,512]{2,1,0:T(8,128)(2,1)S(1)}) custom-call(s32[2]{0:T(128)S(1)} %pad_add_fusion.place_ref, bf16[128,1024]{1,0:T(8,128)(2,1)S(1)} %far_filter.1.refs_0_.zero_ref, bf16[128,1024]{1,0:T(8,128)(2,1)S(1)} %collective-permute-done.4.refs_1_.one_ref, ...), custom_call_target="tpu_custom_call" | custom-call | flops 402653184 | bytes 3145728 | tf_op jit(solution)/shard_map/project_other/pallas_call | solution.py:383
  33.0 1.7 %collective-permute-done.7.three_ref = bf16[128,1024]{1,0:T(8,128)(2,1)S(1)} collective-permute-done((bf16[128,1024]{1,0:T(8,128)(2,1)S(1)}, bf16[128,1024]{1,0:T(8,128)(2,1)S(1)}, u32[]{:S(2)}, u32[]{:S(2)}) %collective-permute-start.7) | collective-permute-done | bytes 262176 | tf_op jit(solution)/shard_map/gated_three/ppermute | solution.py:414
  34.7 1.4 %project_far.1 = bf16[2,2,128,512]{3,2,1,0:T(8,128)(2,1)S(1)} custom-call(s32[2]{0:T(128)S(1)} %pad_add_fusion.place_ref, bf16[2,128,512]{2,1,0:T(8,128)(2,1)S(1)} %get-tuple-element.23.two_ref, bf16[128,1024]{1,0:T(8,128)(2,1)S(1)} %collective-permute-done.7.three_ref, bf16[512,1024]{1,0:T(8,128)(2,1)S(1)} %copy-done, ...), custom_call_target="tpu_custom_call" | custom-call | flops 268435456 | bytes 3145728 | tf_op jit(solution)/shard_map/project_far/pallas_call | solution.py:383
  36.1 3.8 %collective-permute-start.8 = (bf16[2,128,512]{2,1,0:T(8,128)(2,1)S(1)}, bf16[2,128,512]{2,1,0:T(8,128)(2,1)S(1)}, u32[]{:S(2)}, u32[]{:S(2)}) collective-permute-start(bf16[2,128,512]{2,1,0:T(8,128)(2,1)S(1)} %slice_bitcast_fusion), channel_id=1, source_target_pairs={{0,1},{1,0},{2,3},{3,2},{4,5},{5,4},{6,7},{7,6},{8,9},{9,8},{10,11... | collective-permute-start | bytes 786440 | tf_op jit(solution)/shard_map/core_far/ppermute | solution.py:414
  39.9 1.2 %collective-permute-done.8 = bf16[2,128,512]{2,1,0:T(8,128)(2,1)S(1)} collective-permute-done((bf16[2,128,512]{2,1,0:T(8,128)(2,1)S(1)}, bf16[2,128,512]{2,1,0:T(8,128)(2,1)S(1)}, u32[]{:S(2)}, u32[]{:S(2)}) %collective-permute-start.8) | collective-permute-done | bytes 262176 | tf_op jit(solution)/shard_map/core_far/ppermute | solution.py:414
  41.0 0.1 fusion.1
  41.1 0.4 collective-permute-start.9
  41.6 5.8 %collective-permute-start.12 = (bf16[2,128,512]{2,1,0:T(8,128)(2,1)S(1)}, bf16[2,128,512]{2,1,0:T(8,128)(2,1)S(1)}, u32[]{:S(2)}, u32[]{:S(2)}) collective-permute-start(bf16[2,128,512]{2,1,0:T(8,128)(2,1)S(1)} %fusion.1), channel_id=1, source_target_pairs={{0,16},{1,24},{4,20},{5,28},{8,17},{9,25},{12,21},{13,29},{18,2},{... | collective-permute-start | bytes 786440 | tf_op jit(solution)/shard_map/straight_2/ppermute | solution.py:414
  47.3 0.7 %collective-permute-start.13 = (bf16[2,128,512]{2,1,0:T(8,128)(2,1)S(1)}, bf16[2,128,512]{2,1,0:T(8,128)(2,1)S(1)}, u32[]{:S(2)}, u32[]{:S(2)}) collective-permute-start(bf16[2,128,512]{2,1,0:T(8,128)(2,1)S(1)} %fusion.1), channel_id=1, source_target_pairs={{2,16},{3,24},{6,20},{7,28},{10,17},{11,25},{14,21},{15,29},{16,2}... | collective-permute-start | bytes 786440 | tf_op jit(solution)/shard_map/across_2/ppermute | solution.py:414
  48.0 0.0 collective-permute-done.9
  48.0 0.1 fusion
  48.1 1.9 %collective-permute-start.10 = (bf16[2,128,512]{2,1,0:T(8,128)(2,1)S(1)}, bf16[2,128,512]{2,1,0:T(8,128)(2,1)S(1)}, u32[]{:S(2)}, u32[]{:S(2)}) collective-permute-start(bf16[2,128,512]{2,1,0:T(8,128)(2,1)S(1)} %fusion), channel_id=1, source_target_pairs={{0,0},{1,8},{4,4},{5,12},{8,1},{9,9},{12,5},{13,13},{18,18},{19,26... | collective-permute-start | bytes 786440 | tf_op jit(solution)/shard_map/straight_0/ppermute | solution.py:414
  50.0 1.3 %collective-permute-start.11 = (bf16[2,128,512]{2,1,0:T(8,128)(2,1)S(1)}, bf16[2,128,512]{2,1,0:T(8,128)(2,1)S(1)}, u32[]{:S(2)}, u32[]{:S(2)}) collective-permute-start(bf16[2,128,512]{2,1,0:T(8,128)(2,1)S(1)} %fusion), channel_id=1, source_target_pairs={{2,0},{3,8},{6,4},{7,12},{10,1},{11,9},{14,5},{15,13},{16,18},{17,... | collective-permute-start | bytes 786440 | tf_op jit(solution)/shard_map/across_0/ppermute | solution.py:414
  51.3 1.5 %collective-permute-done.12.refs_2_ = bf16[2,128,512]{2,1,0:T(8,128)(2,1)S(1)} collective-permute-done((bf16[2,128,512]{2,1,0:T(8,128)(2,1)S(1)}, bf16[2,128,512]{2,1,0:T(8,128)(2,1)S(1)}, u32[]{:S(2)}, u32[]{:S(2)}) %collective-permute-start.12) | collective-permute-done | bytes 262176 | tf_op jit(solution)/shard_map/straight_2/ppermute | solution.py:414
  52.9 0.0 collective-permute-done.13.refs_3_
  52.9 6.4 %collective-permute-done.10.refs_0_ = bf16[2,128,512]{2,1,0:T(8,128)(2,1)S(1)} collective-permute-done((bf16[2,128,512]{2,1,0:T(8,128)(2,1)S(1)}, bf16[2,128,512]{2,1,0:T(8,128)(2,1)S(1)}, u32[]{:S(2)}, u32[]{:S(2)}) %collective-permute-start.10) | collective-permute-done | bytes 262176 | tf_op jit(solution)/shard_map/straight_0/ppermute | solution.py:414
  59.3 1.2 %collective-permute-done.11.refs_1_ = bf16[2,128,512]{2,1,0:T(8,128)(2,1)S(1)} collective-permute-done((bf16[2,128,512]{2,1,0:T(8,128)(2,1)S(1)}, bf16[2,128,512]{2,1,0:T(8,128)(2,1)S(1)}, u32[]{:S(2)}, u32[]{:S(2)}) %collective-permute-start.11) | collective-permute-done | bytes 262176 | tf_op jit(solution)/shard_map/across_0/ppermute | solution.py:414
  60.5 0.8 %finish.1 = bf16[128,1024]{1,0:T(8,128)(2,1)} custom-call(s32[1]{0:T(128)} %bitcast.place_ref, bf16[2,128,512]{2,1,0:T(8,128)(2,1)S(1)} %collective-permute-done.10.refs_0_, bf16[2,128,512]{2,1,0:T(8,128)(2,1)S(1)} %collective-permute-done.11.refs_1_, bf16[2,128,512]{2,1,0:T(8,128)(2,1)S(1)} %collective-permute-done.12.refs_2_, ...), custom_call_target="tpu_custom_call" | custom-call | flops 262144 | bytes 2097152 | tf_op jit(solution)/shard_map/finish/pallas_call | solution.py:506
  (6 shorter events, 0.0 us)
Async XLA Ops:
  0.0 1.2 %copy-start.1 = (f32[1024,16]{0,1:T(8,128)S(1)}, f32[1024,16]{0,1:T(8,128)}, u32[]{:S(2)}) copy-start(f32[1024,16]{0,1:T(8,128)} %param.8) | copy-start | bytes 196612
  0.0 1.2 %copy-start.2 = (f32[1024,16]{0,1:T(8,128)S(1)}, f32[1024,16]{0,1:T(8,128)}, u32[]{:S(2)}) copy-start(f32[1024,16]{0,1:T(8,128)} %param.9) | copy-start | bytes 196612
  0.0 1.2 %copy-start.3 = (bf16[3,3,1024]{2,1,0:T(4,128)(2,1)S(1)}, bf16[3,3,1024]{2,1,0:T(4,128)(2,1)}, u32[]{:S(2)}) copy-start(bf16[3,3,1024]{2,1,0:T(4,128)(2,1)} %taps_ref.1) | copy-start | bytes 55300
  0.0 1.3 %copy-start.4 = (f32[1024]{0:T(1024)S(1)}, f32[1024]{0:T(1024)}, u32[]{:S(2)}) copy-start(f32[1024]{0:T(1024)} %param.10) | copy-start | bytes 12292
  1.2 8.0 %copy-start = (bf16[512,1024]{1,0:T(8,128)(2,1)S(1)}, bf16[512,1024]{1,0:T(8,128)(2,1)}, u32[]{:S(2)}) copy-start(bf16[512,1024]{1,0:T(8,128)(2,1)} %own_ref.1) | copy-start | bytes 3145732
  2.4 4.7 %collective-permute-start = (bf16[224,128]{1,0:T(8,128)(2,1)S(1)}, bf16[224,128]{1,0:T(8,128)(2,1)S(1)}, u32[]{:S(2)}, u32[]{:S(2)}) collective-permute-start(bf16[224,128]{1,0:T(8,128)(2,1)S(1)} %get-tuple-element.19.refs_3_), channel_id=1, source_target_pairs={{0,12},{1,13},{2,14},{3,15},{4,8},{5,9},{6,10},{7,11},{8,4},{9,5},... | collective-permute-start | bytes 172040 | tf_op jit(solution)/shard_map/state_zy/ppermute | solution.py:414
  5.5 3.5 %collective-permute-start.1 = (bf16[224,128]{1,0:T(8,128)(2,1)S(1)}, bf16[224,128]{1,0:T(8,128)(2,1)S(1)}, u32[]{:S(2)}, u32[]{:S(2)}) collective-permute-start(bf16[224,128]{1,0:T(8,128)(2,1)S(1)} %get-tuple-element.19.refs_3_), channel_id=1, source_target_pairs={{0,8},{1,9},{2,10},{3,11},{4,12},{5,13},{6,14},{7,15},{8,0},{9,1},... | collective-permute-start | bytes 172040 | tf_op jit(solution)/shard_map/state_z/ppermute | solution.py:414
  5.7 3.3 %collective-permute-start.2 = (bf16[224,128]{1,0:T(8,128)(2,1)S(1)}, bf16[224,128]{1,0:T(8,128)(2,1)S(1)}, u32[]{:S(2)}, u32[]{:S(2)}) collective-permute-start(bf16[224,128]{1,0:T(8,128)(2,1)S(1)} %get-tuple-element.19.refs_3_), channel_id=1, source_target_pairs={{0,4},{1,5},{2,6},{3,7},{4,0},{5,1},{6,2},{7,3},{8,12},{9,13},{10,... | collective-permute-start | bytes 172040 | tf_op jit(solution)/shard_map/state_y/ppermute | solution.py:414
  9.2 22.6 %collective-permute-start.6 = (bf16[512,1024]{1,0:T(8,128)(2,1)S(1)}, bf16[512,1024]{1,0:T(8,128)(2,1)S(1)}, u32[]{:S(2)}, u32[]{:S(2)}) collective-permute-start(bf16[512,1024]{1,0:T(8,128)(2,1)S(1)} %copy-done), channel_id=1, source_target_pairs={{0,4},{1,5},{2,6},{3,7},{4,0},{5,1},{6,2},{7,3},{8,12},{9,13},{10,... | collective-permute-start | bytes 3145736 | tf_op jit(solution)/shard_map/weights/ppermute | solution.py:414
  9.7 5.9 %collective-permute-start.3 = (bf16[224,128]{1,0:T(8,128)(2,1)S(1)}, bf16[224,128]{1,0:T(8,128)(2,1)S(1)}, u32[]{:S(2)}, u32[]{:S(2)}) collective-permute-start(bf16[224,128]{1,0:T(8,128)(2,1)S(1)} %join_state.1), channel_id=1, source_target_pairs={{0,16},{1,17},{2,18},{3,19},{4,20},{5,21},{6,22},{7,23},{8,24},{9,... | collective-permute-start | bytes 172040 | tf_op jit(solution)/shard_map/state_half/ppermute | solution.py:414
  16.5 12.4 %collective-permute-start.5 = (bf16[128,1024]{1,0:T(8,128)(2,1)S(1)}, bf16[128,1024]{1,0:T(8,128)(2,1)S(1)}, u32[]{:S(2)}, u32[]{:S(2)}) collective-permute-start(bf16[128,1024]{1,0:T(8,128)(2,1)S(1)} %far_filter.1.refs_0_.zero_ref), channel_id=1, source_target_pairs={{0,16},{1,17},{2,18},{3,19},{4,20},{5,21},{6,22},{7,23},{8,24},{9,... | collective-permute-start | bytes 786440 | tf_op jit(solution)/shard_map/gated_two/ppermute | solution.py:414
  19.0 12.2 %collective-permute-start.4 = (bf16[128,1024]{1,0:T(8,128)(2,1)S(1)}, bf16[128,1024]{1,0:T(8,128)(2,1)S(1)}, u32[]{:S(2)}, u32[]{:S(2)}) collective-permute-start(bf16[128,1024]{1,0:T(8,128)(2,1)S(1)} %far_filter.1.refs_0_.zero_ref), channel_id=1, source_target_pairs={{0,8},{1,9},{2,10},{3,11},{4,12},{5,13},{6,14},{7,15},{8,0},{9,1},... | collective-permute-start | bytes 786440 | tf_op jit(solution)/shard_map/gated_one/ppermute | solution.py:414
  29.0 5.7 %collective-permute-start.7 = (bf16[128,1024]{1,0:T(8,128)(2,1)S(1)}, bf16[128,1024]{1,0:T(8,128)(2,1)S(1)}, u32[]{:S(2)}, u32[]{:S(2)}) collective-permute-start(bf16[128,1024]{1,0:T(8,128)(2,1)S(1)} %collective-permute-done.5.refs_0_.two_ref), channel_id=1, source_target_pairs={{0,8},{1,9},{2,10},{3,11},{4,12},{5,13},{6,14},{7,15},{8,0},{9,1},... | collective-permute-start | bytes 786440 | tf_op jit(solution)/shard_map/gated_three/ppermute | solution.py:414
  36.1 5.0 %collective-permute-start.8 = (bf16[2,128,512]{2,1,0:T(8,128)(2,1)S(1)}, bf16[2,128,512]{2,1,0:T(8,128)(2,1)S(1)}, u32[]{:S(2)}, u32[]{:S(2)}) collective-permute-start(bf16[2,128,512]{2,1,0:T(8,128)(2,1)S(1)} %slice_bitcast_fusion), channel_id=1, source_target_pairs={{0,1},{1,0},{2,3},{3,2},{4,5},{5,4},{6,7},{7,6},{8,9},{9,8},{10,11... | collective-permute-start | bytes 786440 | tf_op jit(solution)/shard_map/core_far/ppermute | solution.py:414
  41.1 6.9 %collective-permute-start.9 = (bf16[2,128,512]{2,1,0:T(8,128)(2,1)S(1)}, bf16[2,128,512]{2,1,0:T(8,128)(2,1)S(1)}, u32[]{:S(2)}, u32[]{:S(2)}) collective-permute-start(bf16[2,128,512]{2,1,0:T(8,128)(2,1)S(1)} %slice_bitcast_fusion.2), channel_id=1, source_target_pairs={{0,1},{1,0},{2,3},{3,2},{4,5},{5,4},{6,7},{7,6},{8,9},{9,8},{10,11... | collective-permute-start | bytes 786440 | tf_op jit(solution)/shard_map/core_near/ppermute | solution.py:414
  41.6 11.3 %collective-permute-start.12 = (bf16[2,128,512]{2,1,0:T(8,128)(2,1)S(1)}, bf16[2,128,512]{2,1,0:T(8,128)(2,1)S(1)}, u32[]{:S(2)}, u32[]{:S(2)}) collective-permute-start(bf16[2,128,512]{2,1,0:T(8,128)(2,1)S(1)} %fusion.1), channel_id=1, source_target_pairs={{0,16},{1,24},{4,20},{5,28},{8,17},{9,25},{12,21},{13,29},{18,2},{... | collective-permute-start | bytes 786440 | tf_op jit(solution)/shard_map/straight_2/ppermute | solution.py:414
  47.3 5.5 %collective-permute-start.13 = (bf16[2,128,512]{2,1,0:T(8,128)(2,1)S(1)}, bf16[2,128,512]{2,1,0:T(8,128)(2,1)S(1)}, u32[]{:S(2)}, u32[]{:S(2)}) collective-permute-start(bf16[2,128,512]{2,1,0:T(8,128)(2,1)S(1)} %fusion.1), channel_id=1, source_target_pairs={{2,16},{3,24},{6,20},{7,28},{10,17},{11,25},{14,21},{15,29},{16,2}... | collective-permute-start | bytes 786440 | tf_op jit(solution)/shard_map/across_2/ppermute | solution.py:414
  48.1 11.2 %collective-permute-start.10 = (bf16[2,128,512]{2,1,0:T(8,128)(2,1)S(1)}, bf16[2,128,512]{2,1,0:T(8,128)(2,1)S(1)}, u32[]{:S(2)}, u32[]{:S(2)}) collective-permute-start(bf16[2,128,512]{2,1,0:T(8,128)(2,1)S(1)} %fusion), channel_id=1, source_target_pairs={{0,0},{1,8},{4,4},{5,12},{8,1},{9,9},{12,5},{13,13},{18,18},{19,26... | collective-permute-start | bytes 786440 | tf_op jit(solution)/shard_map/straight_0/ppermute | solution.py:414
  50.0 10.4 %collective-permute-start.11 = (bf16[2,128,512]{2,1,0:T(8,128)(2,1)S(1)}, bf16[2,128,512]{2,1,0:T(8,128)(2,1)S(1)}, u32[]{:S(2)}, u32[]{:S(2)}) collective-permute-start(bf16[2,128,512]{2,1,0:T(8,128)(2,1)S(1)} %fusion), channel_id=1, source_target_pairs={{2,0},{3,8},{6,4},{7,12},{10,1},{11,9},{14,5},{15,13},{16,18},{17,... | collective-permute-start | bytes 786440 | tf_op jit(solution)/shard_map/across_0/ppermute | solution.py:414

commit v8 on v7

--- a/solution.py
+++ b/solution.py
@@ -362,19 +362,19 @@
 def other_kernel(
     place_ref, zero_ref, one_ref, two_ref, near_own_ref, two_own_ref, weight_ref, near_ref, out_ref
 ):
-    y, odd = place_ref[0], place_ref[1]
+    odd = place_ref[0]
     zero, one, two = project([zero_ref, one_ref, two_ref], weight_ref)
     for i, product in enumerate((zero, one)):
-        near_ref[odd ^ i, y] = near_own_ref[i]
-        near_ref[odd ^ i, 1 - y] = product
-    out_ref[y] = two_own_ref[0]
-    out_ref[1 - y] = two
+        near_ref[odd ^ i, 0] = near_own_ref[i]
+        near_ref[odd ^ i, 1] = product
+    out_ref[0] = two_own_ref[0]
+    out_ref[1] = two
 
 
 def far_project_kernel(place_ref, two_ref, three_ref, own_ref, other_ref, out_ref):
-    y, odd = place_ref[0], place_ref[1]
+    odd = place_ref[0]
     out_ref[odd] = two_ref[...]
-    for half, ref in ((y, own_ref), (1 - y, other_ref)):
+    for half, ref in enumerate((own_ref, other_ref)):
         out_ref[1 - odd, half] = project([three_ref], ref)[0]
 
 
@@ -391,16 +391,17 @@
     )(*operands)
 
 
-def finish_kernel(place_ref, *refs):
+def finish_kernel(kind_ref, y_ref, *refs):
     out_ref = refs[-1]
     width = refs[0].shape[2]
     for pair in range((len(refs) - 1) // 2):
-
-        @pl.when(place_ref[0] == pair)
-        def _(pair=pair):
-            for h in range(2):
-                total = refs[2 * pair][h].astype(F32) + refs[2 * pair + 1][h].astype(F32)
-                out_ref[:, h * width : (h + 1) * width] = total.astype(BF16)
+        for y in range(2):
+
+            @pl.when((kind_ref[0] == pair) & (y_ref[0] == y))
+            def _(pair=pair, y=y):
+                for h in range(2):
+                    total = refs[2 * pair][h ^ y].astype(F32) + refs[2 * pair + 1][h ^ y].astype(F32)
+                    out_ref[:, h * width : (h + 1) * width] = total.astype(BF16)
 
 
 def permute(name, x, move, keep=None):
@@ -460,7 +461,7 @@
     one = permute("gated_one", gated, over_z0)
     three = permute("gated_three", two, over_z0)
     odd = (z ^ tp) & 1
-    place = jnp.stack([y, odd]).astype(jnp.int32)
+    place = odd.reshape(1).astype(jnp.int32)
 
     def odd_of(z, y, x, c):
         return (z ^ c) % 2
@@ -506,12 +507,12 @@
     return pl.pallas_call(
         finish_kernel,
         out_shape=jax.ShapeDtypeStruct((tokens, 2 * out_weight.shape[0]), BF16),
-        in_specs=[SMEM] + [VMEM] * len(parts),
+        in_specs=[SMEM] * 2 + [VMEM] * len(parts),
         out_specs=VMEM,
         compiler_params=params(),
         cost_estimate=cost(4 * tokens * out_weight.shape[0], 2 << 20),
         name="finish",
-    )(kind.reshape(1).astype(jnp.int32), *parts)
+    )(kind.reshape(1).astype(jnp.int32), y.reshape(1).astype(jnp.int32), *parts)
 
 
 def per_device(features, short_taps, rates, residues, skip, out_weight):

time: 61.4 us -> 60.9 us (level)
  Pallas kernels: 8.01 us -> 6.95 us
    pallas_call x4, Pallas kernels: 3.46 us -> 2.37 us  [project_part(): pl.pallas_call(kernel, out_shape=out_shape, in_specs=[SMEM if x.dtype ==...]
    ppermute x14, waiting for transfers between devices: 23.4 us -> 24 us  [permute(): return lax.ppermute(x, AXES, pairs)]
where the time goes in v8:
time: 60.9 us; the launch traced here: 60.7 us
  starting transfers between devices  28.2 us (46%)
  waiting for transfers between devices  24 us (39%)
  Pallas kernels  6.95 us (11%)
  local copies, waits for them, and re-layouts  1.25 us (2%)
    ppermute x14, starting transfers between devices, permute(): return lax.ppermute(x, AXES, pairs)  28.2 us
    ppermute x14, waiting for transfers between devices, permute(): return lax.ppermute(x, AXES, pairs)  24 us
    pallas_call x4, Pallas kernels, project_part(): pl.pallas_call(kernel, out_shape=out_shape, in_specs=[SMEM if x.dtype ==...  2.37 us
    pallas_call x1, Pallas kernels, near_part(): pl.pallas_call(functools.partial(near_kernel, poles, taps), out_shape=(ja...  1.52 us
  transfers between devices with their start and end apart: 14, of which 9 were waited for; matrix products, arithmetic and copies ran while one was open for 0% of the time, Pallas kernels for 7%

profile of v8, /device:TPU:1, one launch (start us, length us, event | category | flops | bytes accessed | tf_op | source)
XLA Modules:
  0.0 60.7 jit_solution(13419839027420175156)
XLA Ops:
  0.0 0.0 copy-start.4
  0.0 1.2 %slice_bitcast_fusion.3 = (bf16[128,1024]{1,0:T(8,128)(2,1)S(1)}, bf16[128,1024]{1,0:T(8,128)(2,1)S(1)}, bf16[128,1024]{1,0:T(8,128)(2,1)S(1)}) fusion(bf16[128,3,1024]{2,0,1:T(8,128)(2,1)} %param.6), kind=kLoop, calls=%fused_computation.7 | loop fusion | bytes 1572864 | tf_op jit(solution)/shard_map/squeeze | solution.py:440
  1.2 0.0 copy-start
  1.2 0.0 copy-done.1
  1.2 0.0 copy-done.2
  1.2 0.0 copy-done.3
  1.3 0.0 copy-done.4
  1.3 1.1 %signal.1 = (f32[1032,128]{1,0:T(8,128)S(1)}, bf16[224,128]{1,0:T(8,128)(2,1)S(1)}, f32[336,128]{1,0:T(8,128)S(1)}) custom-call(f32[8,128]{1,0:T(8,128)S(1)} %bitcast.27, bf16[128,1024]{1,0:T(8,128)(2,1)S(1)} %get-tuple-element.26.q_ref, bf16[128,1024]{1,0:T(8,128)(2,1)S(1)} %get-tuple-element.27.k_ref, bf16[128,1024]{1,0:T(8,128)(2,1)S(1)} %get-tuple-element.25.v_ref, ...), custom_call_target="tpu_custom_call" | custom-call | flops 4194304 | bytes 2097152 | tf_op jit(solution)/shard_map/signal/pallas_call | solution.py:127
  2.4 3.1 %collective-permute-start = (bf16[224,128]{1,0:T(8,128)(2,1)S(1)}, bf16[224,128]{1,0:T(8,128)(2,1)S(1)}, u32[]{:S(2)}, u32[]{:S(2)}) collective-permute-start(bf16[224,128]{1,0:T(8,128)(2,1)S(1)} %get-tuple-element.19.refs_3_), channel_id=1, source_target_pairs={{0,12},{1,13},{2,14},{3,15},{4,8},{5,9},{6,10},{7,11},{8,4},{9,5},... | collective-permute-start | bytes 172040 | tf_op jit(solution)/shard_map/state_zy/ppermute | solution.py:415
  5.5 0.2 collective-permute-start.1
  5.7 0.2 collective-permute-start.2
  5.9 1.2 %collective-permute-done.refs_0_ = bf16[224,128]{1,0:T(8,128)(2,1)S(1)} collective-permute-done((bf16[224,128]{1,0:T(8,128)(2,1)S(1)}, bf16[224,128]{1,0:T(8,128)(2,1)S(1)}, u32[]{:S(2)}, u32[]{:S(2)}) %collective-permute-start) | collective-permute-done | bytes 57376 | tf_op jit(solution)/shard_map/state_zy/ppermute | solution.py:415
  7.1 1.9 %collective-permute-done.1.refs_1_ = bf16[224,128]{1,0:T(8,128)(2,1)S(1)} collective-permute-done((bf16[224,128]{1,0:T(8,128)(2,1)S(1)}, bf16[224,128]{1,0:T(8,128)(2,1)S(1)}, u32[]{:S(2)}, u32[]{:S(2)}) %collective-permute-start.1) | collective-permute-done | bytes 57376 | tf_op jit(solution)/shard_map/state_z/ppermute | solution.py:415
  9.0 0.0 collective-permute-done.2.refs_2_
  9.0 0.1 join_state.1
  9.2 0.1 state_weights.1.refs_5_
  9.2 0.0 copy-done
  9.2 0.4 collective-permute-start.6
  9.7 4.4 %collective-permute-start.3 = (bf16[224,128]{1,0:T(8,128)(2,1)S(1)}, bf16[224,128]{1,0:T(8,128)(2,1)S(1)}, u32[]{:S(2)}, u32[]{:S(2)}) collective-permute-start(bf16[224,128]{1,0:T(8,128)(2,1)S(1)} %join_state.1), channel_id=1, source_target_pairs={{0,16},{1,17},{2,18},{3,19},{4,20},{5,21},{6,22},{7,23},{8,24},{9,... | collective-permute-start | bytes 172040 | tf_op jit(solution)/shard_map/state_half/ppermute | solution.py:415
  14.0 1.5 %near_filter.1 = (bf16[128,1024]{1,0:T(8,128)(2,1)S(1)}, f32[128,1024]{1,0:T(8,128)S(1)}) custom-call(bf16[128,1024]{1,0:T(8,128)(2,1)S(1)} %get-tuple-element.26.q_ref, f32[1032,128]{1,0:T(8,128)S(1)} %get-tuple-element.15.signal_ref, f32[336,128]{1,0:T(8,128)S(1)} %get-tuple-element.20.table_ref.refs_4_), custom_call_target="tpu_custom_call" | custom-call | flops 8388608 | bytes 2097152 | tf_op jit(solution)/shard_map/near_filter/pallas_call | solution.py:145
  15.6 0.0 collective-permute-done.3.refs_4_
  15.6 1.0 %far_filter.1.refs_0_.zero_ref = bf16[128,1024]{1,0:T(8,128)(2,1)S(1)} custom-call(s32[1]{0:T(128)} %bitcast.3.place_ref, bf16[128,1024]{1,0:T(8,128)(2,1)S(1)} %get-tuple-element.17.near_ref, f32[128,1024]{1,0:T(8,128)S(1)} %get-tuple-element.18.gate_ref, f32[336,128]{1,0:T(8,128)S(1)} %get-tuple-element.20.table_ref.refs_4_, ...), custom_call_target="tpu_custom_call" | custom-call | flops 8388608 | bytes 3145728 | tf_op jit(solution)/shard_map/far_filter/pallas_call | solution.py:335
  16.5 2.5 %collective-permute-start.5 = (bf16[128,1024]{1,0:T(8,128)(2,1)S(1)}, bf16[128,1024]{1,0:T(8,128)(2,1)S(1)}, u32[]{:S(2)}, u32[]{:S(2)}) collective-permute-start(bf16[128,1024]{1,0:T(8,128)(2,1)S(1)} %far_filter.1.refs_0_.zero_ref), channel_id=1, source_target_pairs={{0,16},{1,17},{2,18},{3,19},{4,20},{5,21},{6,22},{7,23},{8,24},{9,... | collective-permute-start | bytes 786440 | tf_op jit(solution)/shard_map/gated_two/ppermute | solution.py:415
  19.0 1.7 %collective-permute-start.4 = (bf16[128,1024]{1,0:T(8,128)(2,1)S(1)}, bf16[128,1024]{1,0:T(8,128)(2,1)S(1)}, u32[]{:S(2)}, u32[]{:S(2)}) collective-permute-start(bf16[128,1024]{1,0:T(8,128)(2,1)S(1)} %far_filter.1.refs_0_.zero_ref), channel_id=1, source_target_pairs={{0,8},{1,9},{2,10},{3,11},{4,12},{5,13},{6,14},{7,15},{8,0},{9,1},... | collective-permute-start | bytes 786440 | tf_op jit(solution)/shard_map/gated_one/ppermute | solution.py:415
  20.8 8.2 %collective-permute-done.5.refs_0_.two_ref = bf16[128,1024]{1,0:T(8,128)(2,1)S(1)} collective-permute-done((bf16[128,1024]{1,0:T(8,128)(2,1)S(1)}, bf16[128,1024]{1,0:T(8,128)(2,1)S(1)}, u32[]{:S(2)}, u32[]{:S(2)}) %collective-permute-start.5) | collective-permute-done | bytes 262176 | tf_op jit(solution)/shard_map/gated_two/ppermute | solution.py:415
  29.0 1.7 %collective-permute-start.7 = (bf16[128,1024]{1,0:T(8,128)(2,1)S(1)}, bf16[128,1024]{1,0:T(8,128)(2,1)S(1)}, u32[]{:S(2)}, u32[]{:S(2)}) collective-permute-start(bf16[128,1024]{1,0:T(8,128)(2,1)S(1)} %collective-permute-done.5.refs_0_.two_ref), channel_id=1, source_target_pairs={{0,8},{1,9},{2,10},{3,11},{4,12},{5,13},{6,14},{7,15},{8,0},{9,1},... | collective-permute-start | bytes 786440 | tf_op jit(solution)/shard_map/gated_three/ppermute | solution.py:415
  30.7 0.5 project_two.1.two_own_ref
  31.2 0.0 collective-permute-done.4.refs_1_.one_ref
  31.2 0.5 project_near.1.near_own_ref
  31.7 0.2 collective-permute-done.6.weight_ref.other_ref
  31.9 0.6 project_other.1
  32.5 2.2 %collective-permute-done.7.three_ref = bf16[128,1024]{1,0:T(8,128)(2,1)S(1)} collective-permute-done((bf16[128,1024]{1,0:T(8,128)(2,1)S(1)}, bf16[128,1024]{1,0:T(8,128)(2,1)S(1)}, u32[]{:S(2)}, u32[]{:S(2)}) %collective-permute-start.7) | collective-permute-done | bytes 262176 | tf_op jit(solution)/shard_map/gated_three/ppermute | solution.py:415
  34.7 0.8 %project_far.1 = bf16[2,2,128,512]{3,2,1,0:T(8,128)(2,1)S(1)} custom-call(s32[1]{0:T(128)} %bitcast.2.place_ref, bf16[2,128,512]{2,1,0:T(8,128)(2,1)S(1)} %get-tuple-element.23.two_ref, bf16[128,1024]{1,0:T(8,128)(2,1)S(1)} %collective-permute-done.7.three_ref, bf16[512,1024]{1,0:T(8,128)(2,1)S(1)} %copy-done, ...), custom_call_target="tpu_custom_call" | custom-call | flops 268435456 | bytes 3145728 | tf_op jit(solution)/shard_map/project_far/pallas_call | solution.py:383
  35.5 3.8 %collective-permute-start.8 = (bf16[2,128,512]{2,1,0:T(8,128)(2,1)S(1)}, bf16[2,128,512]{2,1,0:T(8,128)(2,1)S(1)}, u32[]{:S(2)}, u32[]{:S(2)}) collective-permute-start(bf16[2,128,512]{2,1,0:T(8,128)(2,1)S(1)} %slice_bitcast_fusion), channel_id=1, source_target_pairs={{0,1},{1,0},{2,3},{3,2},{4,5},{5,4},{6,7},{7,6},{8,9},{9,8},{10,11... | collective-permute-start | bytes 786440 | tf_op jit(solution)/shard_map/core_far/ppermute | solution.py:415
  39.3 1.2 %collective-permute-done.8 = bf16[2,128,512]{2,1,0:T(8,128)(2,1)S(1)} collective-permute-done((bf16[2,128,512]{2,1,0:T(8,128)(2,1)S(1)}, bf16[2,128,512]{2,1,0:T(8,128)(2,1)S(1)}, u32[]{:S(2)}, u32[]{:S(2)}) %collective-permute-start.8) | collective-permute-done | bytes 262176 | tf_op jit(solution)/shard_map/core_far/ppermute | solution.py:415
  40.5 0.1 fusion.1
  40.6 0.4 collective-permute-start.9
  41.0 5.8 %collective-permute-start.12 = (bf16[2,128,512]{2,1,0:T(8,128)(2,1)S(1)}, bf16[2,128,512]{2,1,0:T(8,128)(2,1)S(1)}, u32[]{:S(2)}, u32[]{:S(2)}) collective-permute-start(bf16[2,128,512]{2,1,0:T(8,128)(2,1)S(1)} %fusion.1), channel_id=1, source_target_pairs={{0,16},{1,24},{4,20},{5,28},{8,17},{9,25},{12,21},{13,29},{18,2},{... | collective-permute-start | bytes 786440 | tf_op jit(solution)/shard_map/straight_2/ppermute | solution.py:415
  46.8 0.7 %collective-permute-start.13 = (bf16[2,128,512]{2,1,0:T(8,128)(2,1)S(1)}, bf16[2,128,512]{2,1,0:T(8,128)(2,1)S(1)}, u32[]{:S(2)}, u32[]{:S(2)}) collective-permute-start(bf16[2,128,512]{2,1,0:T(8,128)(2,1)S(1)} %fusion.1), channel_id=1, source_target_pairs={{2,16},{3,24},{6,20},{7,28},{10,17},{11,25},{14,21},{15,29},{16,2}... | collective-permute-start | bytes 786440 | tf_op jit(solution)/shard_map/across_2/ppermute | solution.py:415
  47.5 0.0 collective-permute-done.9
  47.5 0.1 fusion
  47.6 1.9 %collective-permute-start.10 = (bf16[2,128,512]{2,1,0:T(8,128)(2,1)S(1)}, bf16[2,128,512]{2,1,0:T(8,128)(2,1)S(1)}, u32[]{:S(2)}, u32[]{:S(2)}) collective-permute-start(bf16[2,128,512]{2,1,0:T(8,128)(2,1)S(1)} %fusion), channel_id=1, source_target_pairs={{0,0},{1,8},{4,4},{5,12},{8,1},{9,9},{12,5},{13,13},{18,18},{19,26... | collective-permute-start | bytes 786440 | tf_op jit(solution)/shard_map/straight_0/ppermute | solution.py:415
  49.5 1.3 %collective-permute-start.11 = (bf16[2,128,512]{2,1,0:T(8,128)(2,1)S(1)}, bf16[2,128,512]{2,1,0:T(8,128)(2,1)S(1)}, u32[]{:S(2)}, u32[]{:S(2)}) collective-permute-start(bf16[2,128,512]{2,1,0:T(8,128)(2,1)S(1)} %fusion), channel_id=1, source_target_pairs={{2,0},{3,8},{6,4},{7,12},{10,1},{11,9},{14,5},{15,13},{16,18},{17,... | collective-permute-start | bytes 786440 | tf_op jit(solution)/shard_map/across_0/ppermute | solution.py:415
  50.8 1.5 %collective-permute-done.12.refs_2_ = bf16[2,128,512]{2,1,0:T(8,128)(2,1)S(1)} collective-permute-done((bf16[2,128,512]{2,1,0:T(8,128)(2,1)S(1)}, bf16[2,128,512]{2,1,0:T(8,128)(2,1)S(1)}, u32[]{:S(2)}, u32[]{:S(2)}) %collective-permute-start.12) | collective-permute-done | bytes 262176 | tf_op jit(solution)/shard_map/straight_2/ppermute | solution.py:415
  52.4 0.0 collective-permute-done.13.refs_3_
  52.4 6.4 %collective-permute-done.10.refs_0_ = bf16[2,128,512]{2,1,0:T(8,128)(2,1)S(1)} collective-permute-done((bf16[2,128,512]{2,1,0:T(8,128)(2,1)S(1)}, bf16[2,128,512]{2,1,0:T(8,128)(2,1)S(1)}, u32[]{:S(2)}, u32[]{:S(2)}) %collective-permute-start.10) | collective-permute-done | bytes 262176 | tf_op jit(solution)/shard_map/straight_0/ppermute | solution.py:415
  58.8 1.2 %collective-permute-done.11.refs_1_ = bf16[2,128,512]{2,1,0:T(8,128)(2,1)S(1)} collective-permute-done((bf16[2,128,512]{2,1,0:T(8,128)(2,1)S(1)}, bf16[2,128,512]{2,1,0:T(8,128)(2,1)S(1)}, u32[]{:S(2)}, u32[]{:S(2)}) %collective-permute-start.11) | collective-permute-done | bytes 262176 | tf_op jit(solution)/shard_map/across_0/ppermute | solution.py:415
  59.9 0.8 %finish.1 = bf16[128,1024]{1,0:T(8,128)(2,1)} custom-call(s32[1]{0:T(128)} %bitcast.kind_ref, s32[1]{0:T(128)} %bitcast.1.y_ref, bf16[2,128,512]{2,1,0:T(8,128)(2,1)S(1)} %collective-permute-done.10.refs_0_, bf16[2,128,512]{2,1,0:T(8,128)(2,1)S(1)} %collective-permute-done.11.refs_1_, bf16[2,128,512]{2,1,0:T(8,128)(2,1)S(1)} %collective-permute-done.12.refs_2_, ...), custom_call_target="tpu_custom_call" | custom-call | flops 262144 | bytes 2097152 | tf_op jit(solution)/shard_map/finish/pallas_call | solution.py:507
  (5 shorter events, 0.0 us)
Async XLA Ops:
  0.0 1.2 %copy-start.1 = (f32[1024,16]{0,1:T(8,128)S(1)}, f32[1024,16]{0,1:T(8,128)}, u32[]{:S(2)}) copy-start(f32[1024,16]{0,1:T(8,128)} %param.8) | copy-start | bytes 196612
  0.0 1.2 %copy-start.2 = (f32[1024,16]{0,1:T(8,128)S(1)}, f32[1024,16]{0,1:T(8,128)}, u32[]{:S(2)}) copy-start(f32[1024,16]{0,1:T(8,128)} %param.9) | copy-start | bytes 196612
  0.0 1.2 %copy-start.3 = (bf16[3,3,1024]{2,1,0:T(4,128)(2,1)S(1)}, bf16[3,3,1024]{2,1,0:T(4,128)(2,1)}, u32[]{:S(2)}) copy-start(bf16[3,3,1024]{2,1,0:T(4,128)(2,1)} %taps_ref.1) | copy-start | bytes 55300
  0.0 1.3 %copy-start.4 = (f32[1024]{0:T(1024)S(1)}, f32[1024]{0:T(1024)}, u32[]{:S(2)}) copy-start(f32[1024]{0:T(1024)} %param.10) | copy-start | bytes 12292
  1.2 8.0 %copy-start = (bf16[512,1024]{1,0:T(8,128)(2,1)S(1)}, bf16[512,1024]{1,0:T(8,128)(2,1)}, u32[]{:S(2)}) copy-start(bf16[512,1024]{1,0:T(8,128)(2,1)} %own_ref.1) | copy-start | bytes 3145732
  2.4 4.7 %collective-permute-start = (bf16[224,128]{1,0:T(8,128)(2,1)S(1)}, bf16[224,128]{1,0:T(8,128)(2,1)S(1)}, u32[]{:S(2)}, u32[]{:S(2)}) collective-permute-start(bf16[224,128]{1,0:T(8,128)(2,1)S(1)} %get-tuple-element.19.refs_3_), channel_id=1, source_target_pairs={{0,12},{1,13},{2,14},{3,15},{4,8},{5,9},{6,10},{7,11},{8,4},{9,5},... | collective-permute-start | bytes 172040 | tf_op jit(solution)/shard_map/state_zy/ppermute | solution.py:415
  5.5 3.5 %collective-permute-start.1 = (bf16[224,128]{1,0:T(8,128)(2,1)S(1)}, bf16[224,128]{1,0:T(8,128)(2,1)S(1)}, u32[]{:S(2)}, u32[]{:S(2)}) collective-permute-start(bf16[224,128]{1,0:T(8,128)(2,1)S(1)} %get-tuple-element.19.refs_3_), channel_id=1, source_target_pairs={{0,8},{1,9},{2,10},{3,11},{4,12},{5,13},{6,14},{7,15},{8,0},{9,1},... | collective-permute-start | bytes 172040 | tf_op jit(solution)/shard_map/state_z/ppermute | solution.py:415
  5.7 3.3 %collective-permute-start.2 = (bf16[224,128]{1,0:T(8,128)(2,1)S(1)}, bf16[224,128]{1,0:T(8,128)(2,1)S(1)}, u32[]{:S(2)}, u32[]{:S(2)}) collective-permute-start(bf16[224,128]{1,0:T(8,128)(2,1)S(1)} %get-tuple-element.19.refs_3_), channel_id=1, source_target_pairs={{0,4},{1,5},{2,6},{3,7},{4,0},{5,1},{6,2},{7,3},{8,12},{9,13},{10,... | collective-permute-start | bytes 172040 | tf_op jit(solution)/shard_map/state_y/ppermute | solution.py:415
  9.2 22.6 %collective-permute-start.6 = (bf16[512,1024]{1,0:T(8,128)(2,1)S(1)}, bf16[512,1024]{1,0:T(8,128)(2,1)S(1)}, u32[]{:S(2)}, u32[]{:S(2)}) collective-permute-start(bf16[512,1024]{1,0:T(8,128)(2,1)S(1)} %copy-done), channel_id=1, source_target_pairs={{0,4},{1,5},{2,6},{3,7},{4,0},{5,1},{6,2},{7,3},{8,12},{9,13},{10,... | collective-permute-start | bytes 3145736 | tf_op jit(solution)/shard_map/weights/ppermute | solution.py:415
  9.7 5.9 %collective-permute-start.3 = (bf16[224,128]{1,0:T(8,128)(2,1)S(1)}, bf16[224,128]{1,0:T(8,128)(2,1)S(1)}, u32[]{:S(2)}, u32[]{:S(2)}) collective-permute-start(bf16[224,128]{1,0:T(8,128)(2,1)S(1)} %join_state.1), channel_id=1, source_target_pairs={{0,16},{1,17},{2,18},{3,19},{4,20},{5,21},{6,22},{7,23},{8,24},{9,... | collective-permute-start | bytes 172040 | tf_op jit(solution)/shard_map/state_half/ppermute | solution.py:415
  16.5 12.5 %collective-permute-start.5 = (bf16[128,1024]{1,0:T(8,128)(2,1)S(1)}, bf16[128,1024]{1,0:T(8,128)(2,1)S(1)}, u32[]{:S(2)}, u32[]{:S(2)}) collective-permute-start(bf16[128,1024]{1,0:T(8,128)(2,1)S(1)} %far_filter.1.refs_0_.zero_ref), channel_id=1, source_target_pairs={{0,16},{1,17},{2,18},{3,19},{4,20},{5,21},{6,22},{7,23},{8,24},{9,... | collective-permute-start | bytes 786440 | tf_op jit(solution)/shard_map/gated_two/ppermute | solution.py:415
  19.0 12.2 %collective-permute-start.4 = (bf16[128,1024]{1,0:T(8,128)(2,1)S(1)}, bf16[128,1024]{1,0:T(8,128)(2,1)S(1)}, u32[]{:S(2)}, u32[]{:S(2)}) collective-permute-start(bf16[128,1024]{1,0:T(8,128)(2,1)S(1)} %far_filter.1.refs_0_.zero_ref), channel_id=1, source_target_pairs={{0,8},{1,9},{2,10},{3,11},{4,12},{5,13},{6,14},{7,15},{8,0},{9,1},... | collective-permute-start | bytes 786440 | tf_op jit(solution)/shard_map/gated_one/ppermute | solution.py:415
  29.0 5.7 %collective-permute-start.7 = (bf16[128,1024]{1,0:T(8,128)(2,1)S(1)}, bf16[128,1024]{1,0:T(8,128)(2,1)S(1)}, u32[]{:S(2)}, u32[]{:S(2)}) collective-permute-start(bf16[128,1024]{1,0:T(8,128)(2,1)S(1)} %collective-permute-done.5.refs_0_.two_ref), channel_id=1, source_target_pairs={{0,8},{1,9},{2,10},{3,11},{4,12},{5,13},{6,14},{7,15},{8,0},{9,1},... | collective-permute-start | bytes 786440 | tf_op jit(solution)/shard_map/gated_three/ppermute | solution.py:415
  35.5 4.9 %collective-permute-start.8 = (bf16[2,128,512]{2,1,0:T(8,128)(2,1)S(1)}, bf16[2,128,512]{2,1,0:T(8,128)(2,1)S(1)}, u32[]{:S(2)}, u32[]{:S(2)}) collective-permute-start(bf16[2,128,512]{2,1,0:T(8,128)(2,1)S(1)} %slice_bitcast_fusion), channel_id=1, source_target_pairs={{0,1},{1,0},{2,3},{3,2},{4,5},{5,4},{6,7},{7,6},{8,9},{9,8},{10,11... | collective-permute-start | bytes 786440 | tf_op jit(solution)/shard_map/core_far/ppermute | solution.py:415
  40.6 6.9 %collective-permute-start.9 = (bf16[2,128,512]{2,1,0:T(8,128)(2,1)S(1)}, bf16[2,128,512]{2,1,0:T(8,128)(2,1)S(1)}, u32[]{:S(2)}, u32[]{:S(2)}) collective-permute-start(bf16[2,128,512]{2,1,0:T(8,128)(2,1)S(1)} %slice_bitcast_fusion.2), channel_id=1, source_target_pairs={{0,1},{1,0},{2,3},{3,2},{4,5},{5,4},{6,7},{7,6},{8,9},{9,8},{10,11... | collective-permute-start | bytes 786440 | tf_op jit(solution)/shard_map/core_near/ppermute | solution.py:415
  41.0 11.3 %collective-permute-start.12 = (bf16[2,128,512]{2,1,0:T(8,128)(2,1)S(1)}, bf16[2,128,512]{2,1,0:T(8,128)(2,1)S(1)}, u32[]{:S(2)}, u32[]{:S(2)}) collective-permute-start(bf16[2,128,512]{2,1,0:T(8,128)(2,1)S(1)} %fusion.1), channel_id=1, source_target_pairs={{0,16},{1,24},{4,20},{5,28},{8,17},{9,25},{12,21},{13,29},{18,2},{... | collective-permute-start | bytes 786440 | tf_op jit(solution)/shard_map/straight_2/ppermute | solution.py:415
  46.8 5.5 %collective-permute-start.13 = (bf16[2,128,512]{2,1,0:T(8,128)(2,1)S(1)}, bf16[2,128,512]{2,1,0:T(8,128)(2,1)S(1)}, u32[]{:S(2)}, u32[]{:S(2)}) collective-permute-start(bf16[2,128,512]{2,1,0:T(8,128)(2,1)S(1)} %fusion.1), channel_id=1, source_target_pairs={{2,16},{3,24},{6,20},{7,28},{10,17},{11,25},{14,21},{15,29},{16,2}... | collective-permute-start | bytes 786440 | tf_op jit(solution)/shard_map/across_2/ppermute | solution.py:415
  47.6 11.2 %collective-permute-start.10 = (bf16[2,128,512]{2,1,0:T(8,128)(2,1)S(1)}, bf16[2,128,512]{2,1,0:T(8,128)(2,1)S(1)}, u32[]{:S(2)}, u32[]{:S(2)}) collective-permute-start(bf16[2,128,512]{2,1,0:T(8,128)(2,1)S(1)} %fusion), channel_id=1, source_target_pairs={{0,0},{1,8},{4,4},{5,12},{8,1},{9,9},{12,5},{13,13},{18,18},{19,26... | collective-permute-start | bytes 786440 | tf_op jit(solution)/shard_map/straight_0/ppermute | solution.py:415
  49.5 10.4 %collective-permute-start.11 = (bf16[2,128,512]{2,1,0:T(8,128)(2,1)S(1)}, bf16[2,128,512]{2,1,0:T(8,128)(2,1)S(1)}, u32[]{:S(2)}, u32[]{:S(2)}) collective-permute-start(bf16[2,128,512]{2,1,0:T(8,128)(2,1)S(1)} %fusion), channel_id=1, source_target_pairs={{2,0},{3,8},{6,4},{7,12},{10,1},{11,9},{14,5},{15,13},{16,18},{17,... | collective-permute-start | bytes 786440 | tf_op jit(solution)/shard_map/across_0/ppermute | solution.py:415

commit v9 on v8

--- a/solution.py
+++ b/solution.py
@@ -67,7 +67,7 @@
         value = signal_ref[pl.ds(pl.multiple_of(t * fold, fold), fold), :]
         return tuple(d * m + value for d, m in zip(decay, modes))
 
-    modes = lax.fori_loop(0, tokens, step, (jnp.zeros((fold, LANES), F32),) * poles, unroll=8)
+    modes = lax.fori_loop(0, tokens, step, (jnp.zeros((fold, LANES), F32),) * poles, unroll=32)
     for r in range(poles):
         residue = table_ref[(poles + r) * fold : (poles + r + 1) * fold, :]
         message_s[r * fold : (r + 1) * fold, :] = residue * modes[r]
@@ -316,7 +316,7 @@
         conv_s[pl.ds(pl.multiple_of(t * fold, fold), fold), :] = tree_sum(modes)
         return modes
 
-    lax.fori_loop(edge, tokens, step, modes, unroll=6)
+    lax.fori_loop(edge, tokens, step, modes, unroll=18)
     row_id = lax.broadcasted_iota(jnp.int32, (tokens, LANES), 0)
     first = table.mixed(before, current, 0)
     for j in range(fold):

time: 60.9 us -> 60.8 us (level)
  no operation moved by 1% of the time
where the time goes in v9:
time: 60.8 us; the launch traced here: 60.6 us
  starting transfers between devices  28.2 us (46%)
  waiting for transfers between devices  24 us (39%)
  Pallas kernels  6.87 us (11%)
  local copies, waits for them, and re-layouts  1.25 us (2%)
    ppermute x14, starting transfers between devices, permute(): return lax.ppermute(x, AXES, pairs)  28.2 us
    ppermute x14, waiting for transfers between devices, permute(): return lax.ppermute(x, AXES, pairs)  24 us
    pallas_call x4, Pallas kernels, project_part(): pl.pallas_call(kernel, out_shape=out_shape, in_specs=[SMEM if x.dtype ==...  2.37 us
    pallas_call x1, Pallas kernels, near_part(): pl.pallas_call(functools.partial(near_kernel, poles, taps), out_shape=(ja...  1.52 us
  transfers between devices with their start and end apart: 14, of which 9 were waited for; matrix products, arithmetic and copies ran while one was open for 0% of the time, Pallas kernels for 7%

profile of v9, /device:TPU:1, one launch (start us, length us, event | category | flops | bytes accessed | tf_op | source)
XLA Modules:
  0.0 60.6 jit_solution(8833050385537654622)
XLA Ops:
  0.0 0.0 copy-start.4
  0.0 1.2 %slice_bitcast_fusion.3 = (bf16[128,1024]{1,0:T(8,128)(2,1)S(1)}, bf16[128,1024]{1,0:T(8,128)(2,1)S(1)}, bf16[128,1024]{1,0:T(8,128)(2,1)S(1)}) fusion(bf16[128,3,1024]{2,0,1:T(8,128)(2,1)} %param.6), kind=kLoop, calls=%fused_computation.7 | loop fusion | bytes 1572864 | tf_op jit(solution)/shard_map/squeeze | solution.py:440
  1.2 0.0 copy-start
  1.2 0.0 copy-done.1
  1.2 0.0 copy-done.2
  1.2 0.0 copy-done.3
  1.3 0.0 copy-done.4
  1.3 1.1 %signal.1 = (f32[1032,128]{1,0:T(8,128)S(1)}, bf16[224,128]{1,0:T(8,128)(2,1)S(1)}, f32[336,128]{1,0:T(8,128)S(1)}) custom-call(f32[8,128]{1,0:T(8,128)S(1)} %bitcast.27, bf16[128,1024]{1,0:T(8,128)(2,1)S(1)} %get-tuple-element.26.q_ref, bf16[128,1024]{1,0:T(8,128)(2,1)S(1)} %get-tuple-element.27.k_ref, bf16[128,1024]{1,0:T(8,128)(2,1)S(1)} %get-tuple-element.25.v_ref, ...), custom_call_target="tpu_custom_call" | custom-call | flops 4194304 | bytes 2097152 | tf_op jit(solution)/shard_map/signal/pallas_call | solution.py:127
  2.4 3.1 %collective-permute-start = (bf16[224,128]{1,0:T(8,128)(2,1)S(1)}, bf16[224,128]{1,0:T(8,128)(2,1)S(1)}, u32[]{:S(2)}, u32[]{:S(2)}) collective-permute-start(bf16[224,128]{1,0:T(8,128)(2,1)S(1)} %get-tuple-element.19.refs_3_), channel_id=1, source_target_pairs={{0,12},{1,13},{2,14},{3,15},{4,8},{5,9},{6,10},{7,11},{8,4},{9,5},... | collective-permute-start | bytes 172040 | tf_op jit(solution)/shard_map/state_zy/ppermute | solution.py:415
  5.5 0.2 collective-permute-start.1
  5.7 0.2 collective-permute-start.2
  5.9 1.2 %collective-permute-done.refs_0_ = bf16[224,128]{1,0:T(8,128)(2,1)S(1)} collective-permute-done((bf16[224,128]{1,0:T(8,128)(2,1)S(1)}, bf16[224,128]{1,0:T(8,128)(2,1)S(1)}, u32[]{:S(2)}, u32[]{:S(2)}) %collective-permute-start) | collective-permute-done | bytes 57376 | tf_op jit(solution)/shard_map/state_zy/ppermute | solution.py:415
  7.1 1.9 %collective-permute-done.1.refs_1_ = bf16[224,128]{1,0:T(8,128)(2,1)S(1)} collective-permute-done((bf16[224,128]{1,0:T(8,128)(2,1)S(1)}, bf16[224,128]{1,0:T(8,128)(2,1)S(1)}, u32[]{:S(2)}, u32[]{:S(2)}) %collective-permute-start.1) | collective-permute-done | bytes 57376 | tf_op jit(solution)/shard_map/state_z/ppermute | solution.py:415
  9.0 0.0 collective-permute-done.2.refs_2_
  9.0 0.1 join_state.1
  9.1 0.1 state_weights.1.refs_5_
  9.2 0.0 copy-done
  9.2 0.4 collective-permute-start.6
  9.6 4.4 %collective-permute-start.3 = (bf16[224,128]{1,0:T(8,128)(2,1)S(1)}, bf16[224,128]{1,0:T(8,128)(2,1)S(1)}, u32[]{:S(2)}, u32[]{:S(2)}) collective-permute-start(bf16[224,128]{1,0:T(8,128)(2,1)S(1)} %join_state.1), channel_id=1, source_target_pairs={{0,16},{1,17},{2,18},{3,19},{4,20},{5,21},{6,22},{7,23},{8,24},{9,... | collective-permute-start | bytes 172040 | tf_op jit(solution)/shard_map/state_half/ppermute | solution.py:415
  14.0 1.5 %near_filter.1 = (bf16[128,1024]{1,0:T(8,128)(2,1)S(1)}, f32[128,1024]{1,0:T(8,128)S(1)}) custom-call(bf16[128,1024]{1,0:T(8,128)(2,1)S(1)} %get-tuple-element.26.q_ref, f32[1032,128]{1,0:T(8,128)S(1)} %get-tuple-element.15.signal_ref, f32[336,128]{1,0:T(8,128)S(1)} %get-tuple-element.20.table_ref.refs_4_), custom_call_target="tpu_custom_call" | custom-call | flops 8388608 | bytes 2097152 | tf_op jit(solution)/shard_map/near_filter/pallas_call | solution.py:145
  15.5 0.0 collective-permute-done.3.refs_4_
  15.5 0.9 %far_filter.1.refs_0_.zero_ref = bf16[128,1024]{1,0:T(8,128)(2,1)S(1)} custom-call(s32[1]{0:T(128)} %bitcast.3.place_ref, bf16[128,1024]{1,0:T(8,128)(2,1)S(1)} %get-tuple-element.17.near_ref, f32[128,1024]{1,0:T(8,128)S(1)} %get-tuple-element.18.gate_ref, f32[336,128]{1,0:T(8,128)S(1)} %get-tuple-element.20.table_ref.refs_4_, ...), custom_call_target="tpu_custom_call" | custom-call | flops 8388608 | bytes 3145728 | tf_op jit(solution)/shard_map/far_filter/pallas_call | solution.py:335
  16.5 2.5 %collective-permute-start.5 = (bf16[128,1024]{1,0:T(8,128)(2,1)S(1)}, bf16[128,1024]{1,0:T(8,128)(2,1)S(1)}, u32[]{:S(2)}, u32[]{:S(2)}) collective-permute-start(bf16[128,1024]{1,0:T(8,128)(2,1)S(1)} %far_filter.1.refs_0_.zero_ref), channel_id=1, source_target_pairs={{0,16},{1,17},{2,18},{3,19},{4,20},{5,21},{6,22},{7,23},{8,24},{9,... | collective-permute-start | bytes 786440 | tf_op jit(solution)/shard_map/gated_two/ppermute | solution.py:415
  19.0 1.7 %collective-permute-start.4 = (bf16[128,1024]{1,0:T(8,128)(2,1)S(1)}, bf16[128,1024]{1,0:T(8,128)(2,1)S(1)}, u32[]{:S(2)}, u32[]{:S(2)}) collective-permute-start(bf16[128,1024]{1,0:T(8,128)(2,1)S(1)} %far_filter.1.refs_0_.zero_ref), channel_id=1, source_target_pairs={{0,8},{1,9},{2,10},{3,11},{4,12},{5,13},{6,14},{7,15},{8,0},{9,1},... | collective-permute-start | bytes 786440 | tf_op jit(solution)/shard_map/gated_one/ppermute | solution.py:415
  20.7 8.2 %collective-permute-done.5.refs_0_.two_ref = bf16[128,1024]{1,0:T(8,128)(2,1)S(1)} collective-permute-done((bf16[128,1024]{1,0:T(8,128)(2,1)S(1)}, bf16[128,1024]{1,0:T(8,128)(2,1)S(1)}, u32[]{:S(2)}, u32[]{:S(2)}) %collective-permute-start.5) | collective-permute-done | bytes 262176 | tf_op jit(solution)/shard_map/gated_two/ppermute | solution.py:415
  28.9 1.7 %collective-permute-start.7 = (bf16[128,1024]{1,0:T(8,128)(2,1)S(1)}, bf16[128,1024]{1,0:T(8,128)(2,1)S(1)}, u32[]{:S(2)}, u32[]{:S(2)}) collective-permute-start(bf16[128,1024]{1,0:T(8,128)(2,1)S(1)} %collective-permute-done.5.refs_0_.two_ref), channel_id=1, source_target_pairs={{0,8},{1,9},{2,10},{3,11},{4,12},{5,13},{6,14},{7,15},{8,0},{9,1},... | collective-permute-start | bytes 786440 | tf_op jit(solution)/shard_map/gated_three/ppermute | solution.py:415
  30.6 0.5 project_two.1.two_own_ref
  31.1 0.0 collective-permute-done.4.refs_1_.one_ref
  31.1 0.5 project_near.1.near_own_ref
  31.6 0.2 collective-permute-done.6.weight_ref.other_ref
  31.8 0.6 project_other.1
  32.4 2.1 %collective-permute-done.7.three_ref = bf16[128,1024]{1,0:T(8,128)(2,1)S(1)} collective-permute-done((bf16[128,1024]{1,0:T(8,128)(2,1)S(1)}, bf16[128,1024]{1,0:T(8,128)(2,1)S(1)}, u32[]{:S(2)}, u32[]{:S(2)}) %collective-permute-start.7) | collective-permute-done | bytes 262176 | tf_op jit(solution)/shard_map/gated_three/ppermute | solution.py:415
  34.6 0.8 %project_far.1 = bf16[2,2,128,512]{3,2,1,0:T(8,128)(2,1)S(1)} custom-call(s32[1]{0:T(128)} %bitcast.2.place_ref, bf16[2,128,512]{2,1,0:T(8,128)(2,1)S(1)} %get-tuple-element.23.two_ref, bf16[128,1024]{1,0:T(8,128)(2,1)S(1)} %collective-permute-done.7.three_ref, bf16[512,1024]{1,0:T(8,128)(2,1)S(1)} %copy-done, ...), custom_call_target="tpu_custom_call" | custom-call | flops 268435456 | bytes 3145728 | tf_op jit(solution)/shard_map/project_far/pallas_call | solution.py:383
  35.4 3.8 %collective-permute-start.8 = (bf16[2,128,512]{2,1,0:T(8,128)(2,1)S(1)}, bf16[2,128,512]{2,1,0:T(8,128)(2,1)S(1)}, u32[]{:S(2)}, u32[]{:S(2)}) collective-permute-start(bf16[2,128,512]{2,1,0:T(8,128)(2,1)S(1)} %slice_bitcast_fusion), channel_id=1, source_target_pairs={{0,1},{1,0},{2,3},{3,2},{4,5},{5,4},{6,7},{7,6},{8,9},{9,8},{10,11... | collective-permute-start | bytes 786440 | tf_op jit(solution)/shard_map/core_far/ppermute | solution.py:415
  39.2 1.2 %collective-permute-done.8 = bf16[2,128,512]{2,1,0:T(8,128)(2,1)S(1)} collective-permute-done((bf16[2,128,512]{2,1,0:T(8,128)(2,1)S(1)}, bf16[2,128,512]{2,1,0:T(8,128)(2,1)S(1)}, u32[]{:S(2)}, u32[]{:S(2)}) %collective-permute-start.8) | collective-permute-done | bytes 262176 | tf_op jit(solution)/shard_map/core_far/ppermute | solution.py:415
  40.4 0.1 fusion.1
  40.5 0.4 collective-permute-start.9
  40.9 5.8 %collective-permute-start.12 = (bf16[2,128,512]{2,1,0:T(8,128)(2,1)S(1)}, bf16[2,128,512]{2,1,0:T(8,128)(2,1)S(1)}, u32[]{:S(2)}, u32[]{:S(2)}) collective-permute-start(bf16[2,128,512]{2,1,0:T(8,128)(2,1)S(1)} %fusion.1), channel_id=1, source_target_pairs={{0,16},{1,24},{4,20},{5,28},{8,17},{9,25},{12,21},{13,29},{18,2},{... | collective-permute-start | bytes 786440 | tf_op jit(solution)/shard_map/straight_2/ppermute | solution.py:415
  46.7 0.7 %collective-permute-start.13 = (bf16[2,128,512]{2,1,0:T(8,128)(2,1)S(1)}, bf16[2,128,512]{2,1,0:T(8,128)(2,1)S(1)}, u32[]{:S(2)}, u32[]{:S(2)}) collective-permute-start(bf16[2,128,512]{2,1,0:T(8,128)(2,1)S(1)} %fusion.1), channel_id=1, source_target_pairs={{2,16},{3,24},{6,20},{7,28},{10,17},{11,25},{14,21},{15,29},{16,2}... | collective-permute-start | bytes 786440 | tf_op jit(solution)/shard_map/across_2/ppermute | solution.py:415
  47.4 0.0 collective-permute-done.9
  47.4 0.1 fusion
  47.5 1.9 %collective-permute-start.10 = (bf16[2,128,512]{2,1,0:T(8,128)(2,1)S(1)}, bf16[2,128,512]{2,1,0:T(8,128)(2,1)S(1)}, u32[]{:S(2)}, u32[]{:S(2)}) collective-permute-start(bf16[2,128,512]{2,1,0:T(8,128)(2,1)S(1)} %fusion), channel_id=1, source_target_pairs={{0,0},{1,8},{4,4},{5,12},{8,1},{9,9},{12,5},{13,13},{18,18},{19,26... | collective-permute-start | bytes 786440 | tf_op jit(solution)/shard_map/straight_0/ppermute | solution.py:415
  49.4 1.3 %collective-permute-start.11 = (bf16[2,128,512]{2,1,0:T(8,128)(2,1)S(1)}, bf16[2,128,512]{2,1,0:T(8,128)(2,1)S(1)}, u32[]{:S(2)}, u32[]{:S(2)}) collective-permute-start(bf16[2,128,512]{2,1,0:T(8,128)(2,1)S(1)} %fusion), channel_id=1, source_target_pairs={{2,0},{3,8},{6,4},{7,12},{10,1},{11,9},{14,5},{15,13},{16,18},{17,... | collective-permute-start | bytes 786440 | tf_op jit(solution)/shard_map/across_0/ppermute | solution.py:415
  50.7 1.5 %collective-permute-done.12.refs_2_ = bf16[2,128,512]{2,1,0:T(8,128)(2,1)S(1)} collective-permute-done((bf16[2,128,512]{2,1,0:T(8,128)(2,1)S(1)}, bf16[2,128,512]{2,1,0:T(8,128)(2,1)S(1)}, u32[]{:S(2)}, u32[]{:S(2)}) %collective-permute-start.12) | collective-permute-done | bytes 262176 | tf_op jit(solution)/shard_map/straight_2/ppermute | solution.py:415
  52.3 0.0 collective-permute-done.13.refs_3_
  52.3 6.4 %collective-permute-done.10.refs_0_ = bf16[2,128,512]{2,1,0:T(8,128)(2,1)S(1)} collective-permute-done((bf16[2,128,512]{2,1,0:T(8,128)(2,1)S(1)}, bf16[2,128,512]{2,1,0:T(8,128)(2,1)S(1)}, u32[]{:S(2)}, u32[]{:S(2)}) %collective-permute-start.10) | collective-permute-done | bytes 262176 | tf_op jit(solution)/shard_map/straight_0/ppermute | solution.py:415
  58.7 1.2 %collective-permute-done.11.refs_1_ = bf16[2,128,512]{2,1,0:T(8,128)(2,1)S(1)} collective-permute-done((bf16[2,128,512]{2,1,0:T(8,128)(2,1)S(1)}, bf16[2,128,512]{2,1,0:T(8,128)(2,1)S(1)}, u32[]{:S(2)}, u32[]{:S(2)}) %collective-permute-start.11) | collective-permute-done | bytes 262176 | tf_op jit(solution)/shard_map/across_0/ppermute | solution.py:415
  59.8 0.8 %finish.1 = bf16[128,1024]{1,0:T(8,128)(2,1)} custom-call(s32[1]{0:T(128)} %bitcast.kind_ref, s32[1]{0:T(128)} %bitcast.1.y_ref, bf16[2,128,512]{2,1,0:T(8,128)(2,1)S(1)} %collective-permute-done.10.refs_0_, bf16[2,128,512]{2,1,0:T(8,128)(2,1)S(1)} %collective-permute-done.11.refs_1_, bf16[2,128,512]{2,1,0:T(8,128)(2,1)S(1)} %collective-permute-done.12.refs_2_, ...), custom_call_target="tpu_custom_call" | custom-call | flops 262144 | bytes 2097152 | tf_op jit(solution)/shard_map/finish/pallas_call | solution.py:507
  (5 shorter events, 0.0 us)
Async XLA Ops:
  0.0 1.2 %copy-start.1 = (f32[1024,16]{0,1:T(8,128)S(1)}, f32[1024,16]{0,1:T(8,128)}, u32[]{:S(2)}) copy-start(f32[1024,16]{0,1:T(8,128)} %param.8) | copy-start | bytes 196612
  0.0 1.2 %copy-start.2 = (f32[1024,16]{0,1:T(8,128)S(1)}, f32[1024,16]{0,1:T(8,128)}, u32[]{:S(2)}) copy-start(f32[1024,16]{0,1:T(8,128)} %param.9) | copy-start | bytes 196612
  0.0 1.2 %copy-start.3 = (bf16[3,3,1024]{2,1,0:T(4,128)(2,1)S(1)}, bf16[3,3,1024]{2,1,0:T(4,128)(2,1)}, u32[]{:S(2)}) copy-start(bf16[3,3,1024]{2,1,0:T(4,128)(2,1)} %taps_ref.1) | copy-start | bytes 55300
  0.0 1.3 %copy-start.4 = (f32[1024]{0:T(1024)S(1)}, f32[1024]{0:T(1024)}, u32[]{:S(2)}) copy-start(f32[1024]{0:T(1024)} %param.10) | copy-start | bytes 12292
  1.2 8.0 %copy-start = (bf16[512,1024]{1,0:T(8,128)(2,1)S(1)}, bf16[512,1024]{1,0:T(8,128)(2,1)}, u32[]{:S(2)}) copy-start(bf16[512,1024]{1,0:T(8,128)(2,1)} %own_ref.1) | copy-start | bytes 3145732
  2.4 4.7 %collective-permute-start = (bf16[224,128]{1,0:T(8,128)(2,1)S(1)}, bf16[224,128]{1,0:T(8,128)(2,1)S(1)}, u32[]{:S(2)}, u32[]{:S(2)}) collective-permute-start(bf16[224,128]{1,0:T(8,128)(2,1)S(1)} %get-tuple-element.19.refs_3_), channel_id=1, source_target_pairs={{0,12},{1,13},{2,14},{3,15},{4,8},{5,9},{6,10},{7,11},{8,4},{9,5},... | collective-permute-start | bytes 172040 | tf_op jit(solution)/shard_map/state_zy/ppermute | solution.py:415
  5.5 3.5 %collective-permute-start.1 = (bf16[224,128]{1,0:T(8,128)(2,1)S(1)}, bf16[224,128]{1,0:T(8,128)(2,1)S(1)}, u32[]{:S(2)}, u32[]{:S(2)}) collective-permute-start(bf16[224,128]{1,0:T(8,128)(2,1)S(1)} %get-tuple-element.19.refs_3_), channel_id=1, source_target_pairs={{0,8},{1,9},{2,10},{3,11},{4,12},{5,13},{6,14},{7,15},{8,0},{9,1},... | collective-permute-start | bytes 172040 | tf_op jit(solution)/shard_map/state_z/ppermute | solution.py:415
  5.7 3.3 %collective-permute-start.2 = (bf16[224,128]{1,0:T(8,128)(2,1)S(1)}, bf16[224,128]{1,0:T(8,128)(2,1)S(1)}, u32[]{:S(2)}, u32[]{:S(2)}) collective-permute-start(bf16[224,128]{1,0:T(8,128)(2,1)S(1)} %get-tuple-element.19.refs_3_), channel_id=1, source_target_pairs={{0,4},{1,5},{2,6},{3,7},{4,0},{5,1},{6,2},{7,3},{8,12},{9,13},{10,... | collective-permute-start | bytes 172040 | tf_op jit(solution)/shard_map/state_y/ppermute | solution.py:415
  9.2 22.6 %collective-permute-start.6 = (bf16[512,1024]{1,0:T(8,128)(2,1)S(1)}, bf16[512,1024]{1,0:T(8,128)(2,1)S(1)}, u32[]{:S(2)}, u32[]{:S(2)}) collective-permute-start(bf16[512,1024]{1,0:T(8,128)(2,1)S(1)} %copy-done), channel_id=1, source_target_pairs={{0,4},{1,5},{2,6},{3,7},{4,0},{5,1},{6,2},{7,3},{8,12},{9,13},{10,... | collective-permute-start | bytes 3145736 | tf_op jit(solution)/shard_map/weights/ppermute | solution.py:415
  9.6 5.9 %collective-permute-start.3 = (bf16[224,128]{1,0:T(8,128)(2,1)S(1)}, bf16[224,128]{1,0:T(8,128)(2,1)S(1)}, u32[]{:S(2)}, u32[]{:S(2)}) collective-permute-start(bf16[224,128]{1,0:T(8,128)(2,1)S(1)} %join_state.1), channel_id=1, source_target_pairs={{0,16},{1,17},{2,18},{3,19},{4,20},{5,21},{6,22},{7,23},{8,24},{9,... | collective-permute-start | bytes 172040 | tf_op jit(solution)/shard_map/state_half/ppermute | solution.py:415
  16.5 12.4 %collective-permute-start.5 = (bf16[128,1024]{1,0:T(8,128)(2,1)S(1)}, bf16[128,1024]{1,0:T(8,128)(2,1)S(1)}, u32[]{:S(2)}, u32[]{:S(2)}) collective-permute-start(bf16[128,1024]{1,0:T(8,128)(2,1)S(1)} %far_filter.1.refs_0_.zero_ref), channel_id=1, source_target_pairs={{0,16},{1,17},{2,18},{3,19},{4,20},{5,21},{6,22},{7,23},{8,24},{9,... | collective-permute-start | bytes 786440 | tf_op jit(solution)/shard_map/gated_two/ppermute | solution.py:415
  19.0 12.2 %collective-permute-start.4 = (bf16[128,1024]{1,0:T(8,128)(2,1)S(1)}, bf16[128,1024]{1,0:T(8,128)(2,1)S(1)}, u32[]{:S(2)}, u32[]{:S(2)}) collective-permute-start(bf16[128,1024]{1,0:T(8,128)(2,1)S(1)} %far_filter.1.refs_0_.zero_ref), channel_id=1, source_target_pairs={{0,8},{1,9},{2,10},{3,11},{4,12},{5,13},{6,14},{7,15},{8,0},{9,1},... | collective-permute-start | bytes 786440 | tf_op jit(solution)/shard_map/gated_one/ppermute | solution.py:415
  28.9 5.7 %collective-permute-start.7 = (bf16[128,1024]{1,0:T(8,128)(2,1)S(1)}, bf16[128,1024]{1,0:T(8,128)(2,1)S(1)}, u32[]{:S(2)}, u32[]{:S(2)}) collective-permute-start(bf16[128,1024]{1,0:T(8,128)(2,1)S(1)} %collective-permute-done.5.refs_0_.two_ref), channel_id=1, source_target_pairs={{0,8},{1,9},{2,10},{3,11},{4,12},{5,13},{6,14},{7,15},{8,0},{9,1},... | collective-permute-start | bytes 786440 | tf_op jit(solution)/shard_map/gated_three/ppermute | solution.py:415
  35.4 5.0 %collective-permute-start.8 = (bf16[2,128,512]{2,1,0:T(8,128)(2,1)S(1)}, bf16[2,128,512]{2,1,0:T(8,128)(2,1)S(1)}, u32[]{:S(2)}, u32[]{:S(2)}) collective-permute-start(bf16[2,128,512]{2,1,0:T(8,128)(2,1)S(1)} %slice_bitcast_fusion), channel_id=1, source_target_pairs={{0,1},{1,0},{2,3},{3,2},{4,5},{5,4},{6,7},{7,6},{8,9},{9,8},{10,11... | collective-permute-start | bytes 786440 | tf_op jit(solution)/shard_map/core_far/ppermute | solution.py:415
  40.5 6.9 %collective-permute-start.9 = (bf16[2,128,512]{2,1,0:T(8,128)(2,1)S(1)}, bf16[2,128,512]{2,1,0:T(8,128)(2,1)S(1)}, u32[]{:S(2)}, u32[]{:S(2)}) collective-permute-start(bf16[2,128,512]{2,1,0:T(8,128)(2,1)S(1)} %slice_bitcast_fusion.2), channel_id=1, source_target_pairs={{0,1},{1,0},{2,3},{3,2},{4,5},{5,4},{6,7},{7,6},{8,9},{9,8},{10,11... | collective-permute-start | bytes 786440 | tf_op jit(solution)/shard_map/core_near/ppermute | solution.py:415
  40.9 11.3 %collective-permute-start.12 = (bf16[2,128,512]{2,1,0:T(8,128)(2,1)S(1)}, bf16[2,128,512]{2,1,0:T(8,128)(2,1)S(1)}, u32[]{:S(2)}, u32[]{:S(2)}) collective-permute-start(bf16[2,128,512]{2,1,0:T(8,128)(2,1)S(1)} %fusion.1), channel_id=1, source_target_pairs={{0,16},{1,24},{4,20},{5,28},{8,17},{9,25},{12,21},{13,29},{18,2},{... | collective-permute-start | bytes 786440 | tf_op jit(solution)/shard_map/straight_2/ppermute | solution.py:415
  46.7 5.5 %collective-permute-start.13 = (bf16[2,128,512]{2,1,0:T(8,128)(2,1)S(1)}, bf16[2,128,512]{2,1,0:T(8,128)(2,1)S(1)}, u32[]{:S(2)}, u32[]{:S(2)}) collective-permute-start(bf16[2,128,512]{2,1,0:T(8,128)(2,1)S(1)} %fusion.1), channel_id=1, source_target_pairs={{2,16},{3,24},{6,20},{7,28},{10,17},{11,25},{14,21},{15,29},{16,2}... | collective-permute-start | bytes 786440 | tf_op jit(solution)/shard_map/across_2/ppermute | solution.py:415
  47.5 11.2 %collective-permute-start.10 = (bf16[2,128,512]{2,1,0:T(8,128)(2,1)S(1)}, bf16[2,128,512]{2,1,0:T(8,128)(2,1)S(1)}, u32[]{:S(2)}, u32[]{:S(2)}) collective-permute-start(bf16[2,128,512]{2,1,0:T(8,128)(2,1)S(1)} %fusion), channel_id=1, source_target_pairs={{0,0},{1,8},{4,4},{5,12},{8,1},{9,9},{12,5},{13,13},{18,18},{19,26... | collective-permute-start | bytes 786440 | tf_op jit(solution)/shard_map/straight_0/ppermute | solution.py:415
  49.4 10.4 %collective-permute-start.11 = (bf16[2,128,512]{2,1,0:T(8,128)(2,1)S(1)}, bf16[2,128,512]{2,1,0:T(8,128)(2,1)S(1)}, u32[]{:S(2)}, u32[]{:S(2)}) collective-permute-start(bf16[2,128,512]{2,1,0:T(8,128)(2,1)S(1)} %fusion), channel_id=1, source_target_pairs={{2,0},{3,8},{6,4},{7,12},{10,1},{11,9},{14,5},{15,13},{16,18},{17,... | collective-permute-start | bytes 786440 | tf_op jit(solution)/shard_map/across_0/ppermute | solution.py:415

commit v10 on v9

--- a/solution.py
+++ b/solution.py
@@ -90,7 +90,7 @@
         conv_s[rows, :] = tree_sum(modes + (skip * value,))
         return modes
 
-    lax.fori_loop(0, tokens, step, (jnp.zeros((fold, LANES), F32),) * poles, unroll=4)
+    lax.fori_loop(0, tokens, step, (jnp.zeros((fold, LANES), F32),) * poles, unroll=8)
     for j in range(fold):
         lanes = slice(j * LANES, (j + 1) * LANES)
         value = q_ref[:, lanes].astype(F32)

time: 60.8 us -> 60.8 us (level)
  transfers between devices with their start and end apart: 14 -> 14, of which waited for: 9 -> 9; matrix products, arithmetic and copies ran while one was open for 0% -> 0% of each run, Pallas kernels for 7% -> 6%
where the time goes in v10:
time: 60.8 us; the launch traced here: 60.6 us
  starting transfers between devices  28.3 us (47%)
  waiting for transfers between devices  24 us (39%)
  Pallas kernels  6.79 us (11%)
  local copies, waits for them, and re-layouts  1.25 us (2%)
    ppermute x14, starting transfers between devices, permute(): return lax.ppermute(x, AXES, pairs)  28.3 us
    ppermute x14, waiting for transfers between devices, permute(): return lax.ppermute(x, AXES, pairs)  24 us
    pallas_call x4, Pallas kernels, project_part(): pl.pallas_call(kernel, out_shape=out_shape, in_specs=[SMEM if x.dtype ==...  2.37 us
    pallas_call x1, Pallas kernels, near_part(): pl.pallas_call(functools.partial(near_kernel, poles, taps), out_shape=(ja...  1.43 us
  transfers between devices with their start and end apart: 14, of which 9 were waited for; matrix products, arithmetic and copies ran while one was open for 0% of the time, Pallas kernels for 6%

profile of v10, /device:TPU:1, one launch (start us, length us, event | category | flops | bytes accessed | tf_op | source)
XLA Modules:
  0.0 60.6 jit_solution(31488013135719509)
XLA Ops:
  0.0 0.0 copy-start.4
  0.0 1.2 %slice_bitcast_fusion.3 = (bf16[128,1024]{1,0:T(8,128)(2,1)S(1)}, bf16[128,1024]{1,0:T(8,128)(2,1)S(1)}, bf16[128,1024]{1,0:T(8,128)(2,1)S(1)}) fusion(bf16[128,3,1024]{2,0,1:T(8,128)(2,1)} %param.6), kind=kLoop, calls=%fused_computation.7 | loop fusion | bytes 1572864 | tf_op jit(solution)/shard_map/squeeze | solution.py:440
  1.2 0.0 copy-start
  1.2 0.0 copy-done.1
  1.2 0.0 copy-done.2
  1.2 0.0 copy-done.3
  1.3 0.0 copy-done.4
  1.3 1.1 %signal.1 = (f32[1032,128]{1,0:T(8,128)S(1)}, bf16[224,128]{1,0:T(8,128)(2,1)S(1)}, f32[336,128]{1,0:T(8,128)S(1)}) custom-call(f32[8,128]{1,0:T(8,128)S(1)} %bitcast.27, bf16[128,1024]{1,0:T(8,128)(2,1)S(1)} %get-tuple-element.26.q_ref, bf16[128,1024]{1,0:T(8,128)(2,1)S(1)} %get-tuple-element.27.k_ref, bf16[128,1024]{1,0:T(8,128)(2,1)S(1)} %get-tuple-element.25.v_ref, ...), custom_call_target="tpu_custom_call" | custom-call | flops 4194304 | bytes 2097152 | tf_op jit(solution)/shard_map/signal/pallas_call | solution.py:127
  2.4 3.1 %collective-permute-start = (bf16[224,128]{1,0:T(8,128)(2,1)S(1)}, bf16[224,128]{1,0:T(8,128)(2,1)S(1)}, u32[]{:S(2)}, u32[]{:S(2)}) collective-permute-start(bf16[224,128]{1,0:T(8,128)(2,1)S(1)} %get-tuple-element.19.refs_3_), channel_id=1, source_target_pairs={{0,12},{1,13},{2,14},{3,15},{4,8},{5,9},{6,10},{7,11},{8,4},{9,5},... | collective-permute-start | bytes 172040 | tf_op jit(solution)/shard_map/state_zy/ppermute | solution.py:415
  5.5 0.2 collective-permute-start.1
  5.7 0.2 collective-permute-start.2
  5.9 1.2 %collective-permute-done.refs_0_ = bf16[224,128]{1,0:T(8,128)(2,1)S(1)} collective-permute-done((bf16[224,128]{1,0:T(8,128)(2,1)S(1)}, bf16[224,128]{1,0:T(8,128)(2,1)S(1)}, u32[]{:S(2)}, u32[]{:S(2)}) %collective-permute-start) | collective-permute-done | bytes 57376 | tf_op jit(solution)/shard_map/state_zy/ppermute | solution.py:415
  7.1 1.9 %collective-permute-done.1.refs_1_ = bf16[224,128]{1,0:T(8,128)(2,1)S(1)} collective-permute-done((bf16[224,128]{1,0:T(8,128)(2,1)S(1)}, bf16[224,128]{1,0:T(8,128)(2,1)S(1)}, u32[]{:S(2)}, u32[]{:S(2)}) %collective-permute-start.1) | collective-permute-done | bytes 57376 | tf_op jit(solution)/shard_map/state_z/ppermute | solution.py:415
  9.0 0.0 collective-permute-done.2.refs_2_
  9.0 0.1 join_state.1
  9.1 0.1 state_weights.1.refs_5_
  9.2 0.0 copy-done
  9.2 0.4 collective-permute-start.6
  9.6 4.4 %collective-permute-start.3 = (bf16[224,128]{1,0:T(8,128)(2,1)S(1)}, bf16[224,128]{1,0:T(8,128)(2,1)S(1)}, u32[]{:S(2)}, u32[]{:S(2)}) collective-permute-start(bf16[224,128]{1,0:T(8,128)(2,1)S(1)} %join_state.1), channel_id=1, source_target_pairs={{0,16},{1,17},{2,18},{3,19},{4,20},{5,21},{6,22},{7,23},{8,24},{9,... | collective-permute-start | bytes 172040 | tf_op jit(solution)/shard_map/state_half/ppermute | solution.py:415
  14.0 1.4 %near_filter.1 = (bf16[128,1024]{1,0:T(8,128)(2,1)S(1)}, f32[128,1024]{1,0:T(8,128)S(1)}) custom-call(bf16[128,1024]{1,0:T(8,128)(2,1)S(1)} %get-tuple-element.26.q_ref, f32[1032,128]{1,0:T(8,128)S(1)} %get-tuple-element.15.signal_ref, f32[336,128]{1,0:T(8,128)S(1)} %get-tuple-element.20.table_ref.refs_4_), custom_call_target="tpu_custom_call" | custom-call | flops 8388608 | bytes 2097152 | tf_op jit(solution)/shard_map/near_filter/pallas_call | solution.py:145
  15.4 0.0 collective-permute-done.3.refs_4_
  15.5 0.9 %far_filter.1.refs_0_.zero_ref = bf16[128,1024]{1,0:T(8,128)(2,1)S(1)} custom-call(s32[1]{0:T(128)} %bitcast.3.place_ref, bf16[128,1024]{1,0:T(8,128)(2,1)S(1)} %get-tuple-element.17.near_ref, f32[128,1024]{1,0:T(8,128)S(1)} %get-tuple-element.18.gate_ref, f32[336,128]{1,0:T(8,128)S(1)} %get-tuple-element.20.table_ref.refs_4_, ...), custom_call_target="tpu_custom_call" | custom-call | flops 8388608 | bytes 3145728 | tf_op jit(solution)/shard_map/far_filter/pallas_call | solution.py:335
  16.4 2.6 %collective-permute-start.5 = (bf16[128,1024]{1,0:T(8,128)(2,1)S(1)}, bf16[128,1024]{1,0:T(8,128)(2,1)S(1)}, u32[]{:S(2)}, u32[]{:S(2)}) collective-permute-start(bf16[128,1024]{1,0:T(8,128)(2,1)S(1)} %far_filter.1.refs_0_.zero_ref), channel_id=1, source_target_pairs={{0,16},{1,17},{2,18},{3,19},{4,20},{5,21},{6,22},{7,23},{8,24},{9,... | collective-permute-start | bytes 786440 | tf_op jit(solution)/shard_map/gated_two/ppermute | solution.py:415
  19.0 1.7 %collective-permute-start.4 = (bf16[128,1024]{1,0:T(8,128)(2,1)S(1)}, bf16[128,1024]{1,0:T(8,128)(2,1)S(1)}, u32[]{:S(2)}, u32[]{:S(2)}) collective-permute-start(bf16[128,1024]{1,0:T(8,128)(2,1)S(1)} %far_filter.1.refs_0_.zero_ref), channel_id=1, source_target_pairs={{0,8},{1,9},{2,10},{3,11},{4,12},{5,13},{6,14},{7,15},{8,0},{9,1},... | collective-permute-start | bytes 786440 | tf_op jit(solution)/shard_map/gated_one/ppermute | solution.py:415
  20.7 8.2 %collective-permute-done.5.refs_0_.two_ref = bf16[128,1024]{1,0:T(8,128)(2,1)S(1)} collective-permute-done((bf16[128,1024]{1,0:T(8,128)(2,1)S(1)}, bf16[128,1024]{1,0:T(8,128)(2,1)S(1)}, u32[]{:S(2)}, u32[]{:S(2)}) %collective-permute-start.5) | collective-permute-done | bytes 262176 | tf_op jit(solution)/shard_map/gated_two/ppermute | solution.py:415
  28.9 1.7 %collective-permute-start.7 = (bf16[128,1024]{1,0:T(8,128)(2,1)S(1)}, bf16[128,1024]{1,0:T(8,128)(2,1)S(1)}, u32[]{:S(2)}, u32[]{:S(2)}) collective-permute-start(bf16[128,1024]{1,0:T(8,128)(2,1)S(1)} %collective-permute-done.5.refs_0_.two_ref), channel_id=1, source_target_pairs={{0,8},{1,9},{2,10},{3,11},{4,12},{5,13},{6,14},{7,15},{8,0},{9,1},... | collective-permute-start | bytes 786440 | tf_op jit(solution)/shard_map/gated_three/ppermute | solution.py:415
  30.6 0.5 project_two.1.two_own_ref
  31.1 0.0 collective-permute-done.4.refs_1_.one_ref
  31.1 0.5 project_near.1.near_own_ref
  31.6 0.2 collective-permute-done.6.weight_ref.other_ref
  31.8 0.6 project_other.1
  32.4 2.1 %collective-permute-done.7.three_ref = bf16[128,1024]{1,0:T(8,128)(2,1)S(1)} collective-permute-done((bf16[128,1024]{1,0:T(8,128)(2,1)S(1)}, bf16[128,1024]{1,0:T(8,128)(2,1)S(1)}, u32[]{:S(2)}, u32[]{:S(2)}) %collective-permute-start.7) | collective-permute-done | bytes 262176 | tf_op jit(solution)/shard_map/gated_three/ppermute | solution.py:415
  34.6 0.8 %project_far.1 = bf16[2,2,128,512]{3,2,1,0:T(8,128)(2,1)S(1)} custom-call(s32[1]{0:T(128)} %bitcast.2.place_ref, bf16[2,128,512]{2,1,0:T(8,128)(2,1)S(1)} %get-tuple-element.23.two_ref, bf16[128,1024]{1,0:T(8,128)(2,1)S(1)} %collective-permute-done.7.three_ref, bf16[512,1024]{1,0:T(8,128)(2,1)S(1)} %copy-done, ...), custom_call_target="tpu_custom_call" | custom-call | flops 268435456 | bytes 3145728 | tf_op jit(solution)/shard_map/project_far/pallas_call | solution.py:383
  35.4 3.8 %collective-permute-start.8 = (bf16[2,128,512]{2,1,0:T(8,128)(2,1)S(1)}, bf16[2,128,512]{2,1,0:T(8,128)(2,1)S(1)}, u32[]{:S(2)}, u32[]{:S(2)}) collective-permute-start(bf16[2,128,512]{2,1,0:T(8,128)(2,1)S(1)} %slice_bitcast_fusion), channel_id=1, source_target_pairs={{0,1},{1,0},{2,3},{3,2},{4,5},{5,4},{6,7},{7,6},{8,9},{9,8},{10,11... | collective-permute-start | bytes 786440 | tf_op jit(solution)/shard_map/core_far/ppermute | solution.py:415
  39.2 1.2 %collective-permute-done.8 = bf16[2,128,512]{2,1,0:T(8,128)(2,1)S(1)} collective-permute-done((bf16[2,128,512]{2,1,0:T(8,128)(2,1)S(1)}, bf16[2,128,512]{2,1,0:T(8,128)(2,1)S(1)}, u32[]{:S(2)}, u32[]{:S(2)}) %collective-permute-start.8) | collective-permute-done | bytes 262176 | tf_op jit(solution)/shard_map/core_far/ppermute | solution.py:415
  40.4 0.1 fusion.1
  40.5 0.4 collective-permute-start.9
  40.9 5.8 %collective-permute-start.12 = (bf16[2,128,512]{2,1,0:T(8,128)(2,1)S(1)}, bf16[2,128,512]{2,1,0:T(8,128)(2,1)S(1)}, u32[]{:S(2)}, u32[]{:S(2)}) collective-permute-start(bf16[2,128,512]{2,1,0:T(8,128)(2,1)S(1)} %fusion.1), channel_id=1, source_target_pairs={{0,16},{1,24},{4,20},{5,28},{8,17},{9,25},{12,21},{13,29},{18,2},{... | collective-permute-start | bytes 786440 | tf_op jit(solution)/shard_map/straight_2/ppermute | solution.py:415
  46.7 0.7 %collective-permute-start.13 = (bf16[2,128,512]{2,1,0:T(8,128)(2,1)S(1)}, bf16[2,128,512]{2,1,0:T(8,128)(2,1)S(1)}, u32[]{:S(2)}, u32[]{:S(2)}) collective-permute-start(bf16[2,128,512]{2,1,0:T(8,128)(2,1)S(1)} %fusion.1), channel_id=1, source_target_pairs={{2,16},{3,24},{6,20},{7,28},{10,17},{11,25},{14,21},{15,29},{16,2}... | collective-permute-start | bytes 786440 | tf_op jit(solution)/shard_map/across_2/ppermute | solution.py:415
  47.4 0.0 collective-permute-done.9
  47.4 0.1 fusion
  47.5 1.9 %collective-permute-start.10 = (bf16[2,128,512]{2,1,0:T(8,128)(2,1)S(1)}, bf16[2,128,512]{2,1,0:T(8,128)(2,1)S(1)}, u32[]{:S(2)}, u32[]{:S(2)}) collective-permute-start(bf16[2,128,512]{2,1,0:T(8,128)(2,1)S(1)} %fusion), channel_id=1, source_target_pairs={{0,0},{1,8},{4,4},{5,12},{8,1},{9,9},{12,5},{13,13},{18,18},{19,26... | collective-permute-start | bytes 786440 | tf_op jit(solution)/shard_map/straight_0/ppermute | solution.py:415
  49.4 1.3 %collective-permute-start.11 = (bf16[2,128,512]{2,1,0:T(8,128)(2,1)S(1)}, bf16[2,128,512]{2,1,0:T(8,128)(2,1)S(1)}, u32[]{:S(2)}, u32[]{:S(2)}) collective-permute-start(bf16[2,128,512]{2,1,0:T(8,128)(2,1)S(1)} %fusion), channel_id=1, source_target_pairs={{2,0},{3,8},{6,4},{7,12},{10,1},{11,9},{14,5},{15,13},{16,18},{17,... | collective-permute-start | bytes 786440 | tf_op jit(solution)/shard_map/across_0/ppermute | solution.py:415
  50.7 1.5 %collective-permute-done.12.refs_2_ = bf16[2,128,512]{2,1,0:T(8,128)(2,1)S(1)} collective-permute-done((bf16[2,128,512]{2,1,0:T(8,128)(2,1)S(1)}, bf16[2,128,512]{2,1,0:T(8,128)(2,1)S(1)}, u32[]{:S(2)}, u32[]{:S(2)}) %collective-permute-start.12) | collective-permute-done | bytes 262176 | tf_op jit(solution)/shard_map/straight_2/ppermute | solution.py:415
  52.3 0.0 collective-permute-done.13.refs_3_
  52.3 6.4 %collective-permute-done.10.refs_0_ = bf16[2,128,512]{2,1,0:T(8,128)(2,1)S(1)} collective-permute-done((bf16[2,128,512]{2,1,0:T(8,128)(2,1)S(1)}, bf16[2,128,512]{2,1,0:T(8,128)(2,1)S(1)}, u32[]{:S(2)}, u32[]{:S(2)}) %collective-permute-start.10) | collective-permute-done | bytes 262176 | tf_op jit(solution)/shard_map/straight_0/ppermute | solution.py:415
  58.7 1.2 %collective-permute-done.11.refs_1_ = bf16[2,128,512]{2,1,0:T(8,128)(2,1)S(1)} collective-permute-done((bf16[2,128,512]{2,1,0:T(8,128)(2,1)S(1)}, bf16[2,128,512]{2,1,0:T(8,128)(2,1)S(1)}, u32[]{:S(2)}, u32[]{:S(2)}) %collective-permute-start.11) | collective-permute-done | bytes 262176 | tf_op jit(solution)/shard_map/across_0/ppermute | solution.py:415
  59.8 0.8 %finish.1 = bf16[128,1024]{1,0:T(8,128)(2,1)} custom-call(s32[1]{0:T(128)} %bitcast.kind_ref, s32[1]{0:T(128)} %bitcast.1.y_ref, bf16[2,128,512]{2,1,0:T(8,128)(2,1)S(1)} %collective-permute-done.10.refs_0_, bf16[2,128,512]{2,1,0:T(8,128)(2,1)S(1)} %collective-permute-done.11.refs_1_, bf16[2,128,512]{2,1,0:T(8,128)(2,1)S(1)} %collective-permute-done.12.refs_2_, ...), custom_call_target="tpu_custom_call" | custom-call | flops 262144 | bytes 2097152 | tf_op jit(solution)/shard_map/finish/pallas_call | solution.py:507
  (5 shorter events, 0.0 us)
Async XLA Ops:
  0.0 1.2 %copy-start.1 = (f32[1024,16]{0,1:T(8,128)S(1)}, f32[1024,16]{0,1:T(8,128)}, u32[]{:S(2)}) copy-start(f32[1024,16]{0,1:T(8,128)} %param.8) | copy-start | bytes 196612
  0.0 1.2 %copy-start.2 = (f32[1024,16]{0,1:T(8,128)S(1)}, f32[1024,16]{0,1:T(8,128)}, u32[]{:S(2)}) copy-start(f32[1024,16]{0,1:T(8,128)} %param.9) | copy-start | bytes 196612
  0.0 1.2 %copy-start.3 = (bf16[3,3,1024]{2,1,0:T(4,128)(2,1)S(1)}, bf16[3,3,1024]{2,1,0:T(4,128)(2,1)}, u32[]{:S(2)}) copy-start(bf16[3,3,1024]{2,1,0:T(4,128)(2,1)} %taps_ref.1) | copy-start | bytes 55300
  0.0 1.3 %copy-start.4 = (f32[1024]{0:T(1024)S(1)}, f32[1024]{0:T(1024)}, u32[]{:S(2)}) copy-start(f32[1024]{0:T(1024)} %param.10) | copy-start | bytes 12292
  1.2 8.0 %copy-start = (bf16[512,1024]{1,0:T(8,128)(2,1)S(1)}, bf16[512,1024]{1,0:T(8,128)(2,1)}, u32[]{:S(2)}) copy-start(bf16[512,1024]{1,0:T(8,128)(2,1)} %own_ref.1) | copy-start | bytes 3145732
  2.4 4.7 %collective-permute-start = (bf16[224,128]{1,0:T(8,128)(2,1)S(1)}, bf16[224,128]{1,0:T(8,128)(2,1)S(1)}, u32[]{:S(2)}, u32[]{:S(2)}) collective-permute-start(bf16[224,128]{1,0:T(8,128)(2,1)S(1)} %get-tuple-element.19.refs_3_), channel_id=1, source_target_pairs={{0,12},{1,13},{2,14},{3,15},{4,8},{5,9},{6,10},{7,11},{8,4},{9,5},... | collective-permute-start | bytes 172040 | tf_op jit(solution)/shard_map/state_zy/ppermute | solution.py:415
  5.5 3.5 %collective-permute-start.1 = (bf16[224,128]{1,0:T(8,128)(2,1)S(1)}, bf16[224,128]{1,0:T(8,128)(2,1)S(1)}, u32[]{:S(2)}, u32[]{:S(2)}) collective-permute-start(bf16[224,128]{1,0:T(8,128)(2,1)S(1)} %get-tuple-element.19.refs_3_), channel_id=1, source_target_pairs={{0,8},{1,9},{2,10},{3,11},{4,12},{5,13},{6,14},{7,15},{8,0},{9,1},... | collective-permute-start | bytes 172040 | tf_op jit(solution)/shard_map/state_z/ppermute | solution.py:415
  5.7 3.3 %collective-permute-start.2 = (bf16[224,128]{1,0:T(8,128)(2,1)S(1)}, bf16[224,128]{1,0:T(8,128)(2,1)S(1)}, u32[]{:S(2)}, u32[]{:S(2)}) collective-permute-start(bf16[224,128]{1,0:T(8,128)(2,1)S(1)} %get-tuple-element.19.refs_3_), channel_id=1, source_target_pairs={{0,4},{1,5},{2,6},{3,7},{4,0},{5,1},{6,2},{7,3},{8,12},{9,13},{10,... | collective-permute-start | bytes 172040 | tf_op jit(solution)/shard_map/state_y/ppermute | solution.py:415
  9.2 22.6 %collective-permute-start.6 = (bf16[512,1024]{1,0:T(8,128)(2,1)S(1)}, bf16[512,1024]{1,0:T(8,128)(2,1)S(1)}, u32[]{:S(2)}, u32[]{:S(2)}) collective-permute-start(bf16[512,1024]{1,0:T(8,128)(2,1)S(1)} %copy-done), channel_id=1, source_target_pairs={{0,4},{1,5},{2,6},{3,7},{4,0},{5,1},{6,2},{7,3},{8,12},{9,13},{10,... | collective-permute-start | bytes 3145736 | tf_op jit(solution)/shard_map/weights/ppermute | solution.py:415
  9.6 5.8 %collective-permute-start.3 = (bf16[224,128]{1,0:T(8,128)(2,1)S(1)}, bf16[224,128]{1,0:T(8,128)(2,1)S(1)}, u32[]{:S(2)}, u32[]{:S(2)}) collective-permute-start(bf16[224,128]{1,0:T(8,128)(2,1)S(1)} %join_state.1), channel_id=1, source_target_pairs={{0,16},{1,17},{2,18},{3,19},{4,20},{5,21},{6,22},{7,23},{8,24},{9,... | collective-permute-start | bytes 172040 | tf_op jit(solution)/shard_map/state_half/ppermute | solution.py:415
  16.4 12.5 %collective-permute-start.5 = (bf16[128,1024]{1,0:T(8,128)(2,1)S(1)}, bf16[128,1024]{1,0:T(8,128)(2,1)S(1)}, u32[]{:S(2)}, u32[]{:S(2)}) collective-permute-start(bf16[128,1024]{1,0:T(8,128)(2,1)S(1)} %far_filter.1.refs_0_.zero_ref), channel_id=1, source_target_pairs={{0,16},{1,17},{2,18},{3,19},{4,20},{5,21},{6,22},{7,23},{8,24},{9,... | collective-permute-start | bytes 786440 | tf_op jit(solution)/shard_map/gated_two/ppermute | solution.py:415
  19.0 12.2 %collective-permute-start.4 = (bf16[128,1024]{1,0:T(8,128)(2,1)S(1)}, bf16[128,1024]{1,0:T(8,128)(2,1)S(1)}, u32[]{:S(2)}, u32[]{:S(2)}) collective-permute-start(bf16[128,1024]{1,0:T(8,128)(2,1)S(1)} %far_filter.1.refs_0_.zero_ref), channel_id=1, source_target_pairs={{0,8},{1,9},{2,10},{3,11},{4,12},{5,13},{6,14},{7,15},{8,0},{9,1},... | collective-permute-start | bytes 786440 | tf_op jit(solution)/shard_map/gated_one/ppermute | solution.py:415
  28.9 5.7 %collective-permute-start.7 = (bf16[128,1024]{1,0:T(8,128)(2,1)S(1)}, bf16[128,1024]{1,0:T(8,128)(2,1)S(1)}, u32[]{:S(2)}, u32[]{:S(2)}) collective-permute-start(bf16[128,1024]{1,0:T(8,128)(2,1)S(1)} %collective-permute-done.5.refs_0_.two_ref), channel_id=1, source_target_pairs={{0,8},{1,9},{2,10},{3,11},{4,12},{5,13},{6,14},{7,15},{8,0},{9,1},... | collective-permute-start | bytes 786440 | tf_op jit(solution)/shard_map/gated_three/ppermute | solution.py:415
  35.4 5.0 %collective-permute-start.8 = (bf16[2,128,512]{2,1,0:T(8,128)(2,1)S(1)}, bf16[2,128,512]{2,1,0:T(8,128)(2,1)S(1)}, u32[]{:S(2)}, u32[]{:S(2)}) collective-permute-start(bf16[2,128,512]{2,1,0:T(8,128)(2,1)S(1)} %slice_bitcast_fusion), channel_id=1, source_target_pairs={{0,1},{1,0},{2,3},{3,2},{4,5},{5,4},{6,7},{7,6},{8,9},{9,8},{10,11... | collective-permute-start | bytes 786440 | tf_op jit(solution)/shard_map/core_far/ppermute | solution.py:415
  40.5 6.9 %collective-permute-start.9 = (bf16[2,128,512]{2,1,0:T(8,128)(2,1)S(1)}, bf16[2,128,512]{2,1,0:T(8,128)(2,1)S(1)}, u32[]{:S(2)}, u32[]{:S(2)}) collective-permute-start(bf16[2,128,512]{2,1,0:T(8,128)(2,1)S(1)} %slice_bitcast_fusion.2), channel_id=1, source_target_pairs={{0,1},{1,0},{2,3},{3,2},{4,5},{5,4},{6,7},{7,6},{8,9},{9,8},{10,11... | collective-permute-start | bytes 786440 | tf_op jit(solution)/shard_map/core_near/ppermute | solution.py:415
  40.9 11.3 %collective-permute-start.12 = (bf16[2,128,512]{2,1,0:T(8,128)(2,1)S(1)}, bf16[2,128,512]{2,1,0:T(8,128)(2,1)S(1)}, u32[]{:S(2)}, u32[]{:S(2)}) collective-permute-start(bf16[2,128,512]{2,1,0:T(8,128)(2,1)S(1)} %fusion.1), channel_id=1, source_target_pairs={{0,16},{1,24},{4,20},{5,28},{8,17},{9,25},{12,21},{13,29},{18,2},{... | collective-permute-start | bytes 786440 | tf_op jit(solution)/shard_map/straight_2/ppermute | solution.py:415
  46.7 5.5 %collective-permute-start.13 = (bf16[2,128,512]{2,1,0:T(8,128)(2,1)S(1)}, bf16[2,128,512]{2,1,0:T(8,128)(2,1)S(1)}, u32[]{:S(2)}, u32[]{:S(2)}) collective-permute-start(bf16[2,128,512]{2,1,0:T(8,128)(2,1)S(1)} %fusion.1), channel_id=1, source_target_pairs={{2,16},{3,24},{6,20},{7,28},{10,17},{11,25},{14,21},{15,29},{16,2}... | collective-permute-start | bytes 786440 | tf_op jit(solution)/shard_map/across_2/ppermute | solution.py:415
  47.5 11.2 %collective-permute-start.10 = (bf16[2,128,512]{2,1,0:T(8,128)(2,1)S(1)}, bf16[2,128,512]{2,1,0:T(8,128)(2,1)S(1)}, u32[]{:S(2)}, u32[]{:S(2)}) collective-permute-start(bf16[2,128,512]{2,1,0:T(8,128)(2,1)S(1)} %fusion), channel_id=1, source_target_pairs={{0,0},{1,8},{4,4},{5,12},{8,1},{9,9},{12,5},{13,13},{18,18},{19,26... | collective-permute-start | bytes 786440 | tf_op jit(solution)/shard_map/straight_0/ppermute | solution.py:415
  49.4 10.4 %collective-permute-start.11 = (bf16[2,128,512]{2,1,0:T(8,128)(2,1)S(1)}, bf16[2,128,512]{2,1,0:T(8,128)(2,1)S(1)}, u32[]{:S(2)}, u32[]{:S(2)}) collective-permute-start(bf16[2,128,512]{2,1,0:T(8,128)(2,1)S(1)} %fusion), channel_id=1, source_target_pairs={{2,0},{3,8},{6,4},{7,12},{10,1},{11,9},{14,5},{15,13},{16,18},{17,... | collective-permute-start | bytes 786440 | tf_op jit(solution)/shard_map/across_0/ppermute | solution.py:415
